TPU v7x, 32 devices: a whole 2x2x4 slice. The times are simulated.
32 devices in a mesh: tm: 4 (over z), row: 4 (over y, core), col: 2 (over x).
Axes of the slice: x: 2, y: 2, z: 4, core: 2. Of those that a mesh axis runs over, the one named last changes fastest.
Arguments:
- c_occ: float32 [1536, 1536], P(None, 'tm'), may hold values from -1 to 1
- c_vir: float32 [1536, 1536], P(None, 'tm'), may hold values from -1 to 1
- eps_occ: float32 [1536], P('tm'), may hold values from -1.6 to -0.05, as said below
- eps_vir: float32 [1536], P('tm'), may hold values from 0.05 to 1.6, as said below
- tau: float32 [4], replicated, may hold values from 0.03 to 10
- tweight: float32 [4], replicated, may hold values from 0.02 to 0.15
- omega: float32 [16], replicated, may hold values from 0.05 to 5
- coulomb: float32 [1536, 1536], replicated, may hold values from -2 to 2
Outputs:
- screened: float32 [16, 1536, 1536], P('tm', 'row', 'col')
Inputs may be any that keep to these rules, and one draw needn't show every extreme that they name: `eps_occ`: ascending along the orbital index. `eps_vir`: ascending along the orbital index.
All inputs are finite; a program needn't handle non-finite values.
Results may differ from a plain program's by a relative error of at most 0.00005.
Values sent between devices are 32-bit elements; how exact they have to be, the bound alone decides.
No kernel may reach another device: no remote copies, remote signals or barrier semaphores. Data moves between devices by JAX's collectives and lax.ppermute only.
A program may use at most 128 MiB of HBM per device.

v0:
```python
import jax
import jax.numpy as jnp
from jax import lax
from jax.sharding import PartitionSpec as P

HIGH = lax.Precision.HIGHEST


def green_block(rows_c, cols_c, energies, taus, sign):
    factor = jnp.exp(sign * taus[:, None] * energies[None, :])
    width = rows_c.shape[1]
    scaled = rows_c[:, None, :] * factor[None, :, :]
    lead = (rows_c.shape[0], taus.shape[0])
    flat = scaled.reshape(lead[0] * lead[1], width)
    product = lax.dot_general(
        flat, cols_c, (((1,), (1,)), ((), ())), precision=HIGH, preferred_element_type=jnp.float32
    )
    return product.reshape(lead[0], lead[1], cols_c.shape[0])


def on_device(c_occ, c_vir, eps_occ, eps_vir, tau, tweight, omega, coulomb):
    grid = coulomb.shape[0]
    tile_rows = grid // lax.axis_size("row")
    tile_cols = grid // lax.axis_size("col")
    row_start = lax.axis_index("row") * tile_rows
    col_start = lax.axis_index("col") * tile_cols
    occ_rows = lax.dynamic_slice_in_dim(c_occ, row_start, tile_rows, 0)
    occ_cols = lax.dynamic_slice_in_dim(c_occ, col_start, tile_cols, 0)
    vir_rows = lax.dynamic_slice_in_dim(c_vir, row_start, tile_rows, 0)
    vir_cols = lax.dynamic_slice_in_dim(c_vir, col_start, tile_cols, 0)
    gamma = tweight[None, :] * jnp.cos(omega[:, None] * tau[None, :])
    green_occ = green_block(occ_rows, occ_cols, eps_occ, tau, 1.0)
    green_vir = green_block(vir_rows, vir_cols, eps_vir, tau, -1.0)
    greens = lax.psum_scatter(
        jnp.stack([green_occ, green_vir], axis=1), "tm", scatter_dimension=0, tiled=True
    )
    polar_time = -2.0 * greens[:, 0] * greens[:, 1]
    polar_all = jnp.einsum("kj,ijc->kic", gamma, polar_time, precision=HIGH)
    polar = lax.all_to_all(polar_all, "tm", split_axis=0, concat_axis=1, tiled=True)
    coulomb_rows = lax.dynamic_slice_in_dim(coulomb, row_start, tile_rows, 0)
    coulomb_cols = lax.dynamic_slice_in_dim(coulomb, col_start, tile_cols, 1)
    coulomb_tile = lax.dynamic_slice_in_dim(coulomb_rows, col_start, tile_cols, 1)
    left = coulomb_rows
    coupled = jnp.einsum(
        "ik,fkj->fij", left, lax.all_gather(polar, "row", axis=1, tiled=True), precision=HIGH
    )
    coupled_rows = lax.all_gather(coupled, "col", axis=2, tiled=True)
    first = coulomb_tile[None] + jnp.einsum(
        "fik,kj->fij", coupled_rows, coulomb_cols, precision=HIGH
    )
    left = coupled_rows
    return jnp.einsum(
        "fik,fkj->fij", left, lax.all_gather(first, "row", axis=1, tiled=True), precision=HIGH
    )


def solution(mesh):
    in_specs = (P(None, "tm"), P(None, "tm"), P("tm"), P("tm"), P(), P(), P(), P())
    out_specs = P("tm", "row", "col")
    return jax.shard_map(
        on_device, mesh=mesh, in_specs=in_specs, out_specs=out_specs, check_vma=False
    )
```

profile of v0, /device:TPU:0, one launch (start us, length us, event | category | flops | bytes accessed | tf_op | source)
XLA Modules:
  0.0 778.7 jit_solution(17444164138658813179)
XLA Ops:
  6.5 0.0 copy-start
  6.5 0.0 reduce-scatter.2.cloned.1.call-start
  6.5 0.8 broadcast_multiply_fusion
  7.3 0.8 multiply_exponential_fusion.1
  8.1 0.8 multiply_exponential_fusion
  8.9 1.3 constant_dynamic-slice_fusion
  10.2 9.7 %fusion.16 = f32[384,1,4,768]{3,0,2,1:T(8,128)S(1)} fusion(f32[1536,384]{1,0:T(8,128)} %param.9, s32[]{:T(128)S(6)} %select_n.16, f32[4,384]{1,0:T(4,128)S(1)} %multiply_exponential_fusion, f32[384,384]{1,0:T(8,128)S(1)} %get-tuple-element.5), kind=kOutput, calls=%fused_computation.14 | convolution fusion | flops 5436407808 | bytes 6494212 | tf_op jit(solution)/shard_map/dot_general | solution.py:15
  19.9 0.0 copy-done
  19.9 8.7 %fusion.13 = f32[384,1,4,768]{3,0,2,1:T(8,128)S(1)} fusion(f32[1536,384]{1,0:T(8,128)S(1)} %copy-done, s32[]{:T(128)S(6)} %select_n.16, f32[4,384]{1,0:T(4,128)S(1)} %multiply_exponential_fusion.1, f32[384,384]{1,0:T(8,128)S(1)} %get-tuple-element.6), kind=kOutput, calls=%fused_computation.13 | convolution fusion | flops 5436407808 | bytes 6494212 | tf_op jit(solution)/shard_map/dot_general | solution.py:15
  28.6 4.7 pad_maximum_fusion
  33.3 0.0 copy-start.1
  33.3 0.0 copy-start.2
  33.3 0.0 copy-start.3
  33.3 0.0 reduce-scatter.2.cloned.1.call-update
  33.3 0.0 all-gather.4.cloned.1.call-start
  33.3 164.1 %reduce-scatter.2.cloned.1.call-done = f32[96,2,4,768]{3,0,2,1:T(8,128)} async-done(((f32[384,2,4,768]{3,0,2,1:T(8,128)}), f32[96,2,4,768]{3,0,2,1:T(8,128)}) %reduce-scatter.2.cloned.1.call-update) | async-done | bytes 2359312 | tf_op jit(solution)/shard_map/reduce_scatter | solution.py:34
  197.4 1.8 fusion.21
  199.2 0.0 copy-done.1
  199.2 0.0 copy-done.2
  199.2 0.0 copy-done.3
  199.2 4.7 fusion.24
  203.9 2.7 copy.22
  206.6 108.8 %all_to_all.18 = f32[16,96,768]{2,1,0:T(8,128)S(1)} all-to-all(f32[16,96,768]{2,1,0:T(8,128)S(1)} %copy.22), channel_id=1, replica_groups=mesh['tm'=4,'row'=4,'col'=2] {'tm'}, dimensions={0} | all-to-all | bytes 9437184 | tf_op jit(solution)/shard_map/all_to_all | solution.py:39
  315.4 2.6 copy.23
  318.0 6.0 copy.24
  324.1 0.0 all-gather.4.cloned.1.call-update
  324.1 9.3 %all-gather.6.cloned.1.call-start = ((), (), s32[]{:S(2)}) async-start(), calls=%async_computation.4 | async-start | bytes 14155776 | tf_op jit(solution)/shard_map/all_gather | solution.py:47
  333.4 110.2 %all-gather.4.cloned.1.call-done = f32[4,1536,768]{1,2,0:T(8,128)} async-done(((f32[4,384,768]{1,2,0:T(8,128)}), f32[4,1536,768]{1,2,0:T(8,128)}) %all-gather.4.cloned.1.call-update) | async-done | bytes 18874384 | tf_op jit(solution)/shard_map/all_gather | solution.py:45
  443.6 34.8 %fusion.10 = f32[4,384,768]{1,2,0:T(8,128)} fusion(f32[4,1536,768]{1,2,0:T(8,128)} %all-gather.4.cloned.1.call-done, f32[1536,1536]{1,0:T(8,128)} %param.15, s32[]{:T(128)S(6)} %select_n.15), kind=kOutput, calls=%fused_computation.12 | convolution fusion | flops 21743271936 | bytes 25952260 | tf_op jit(solution)/shard_map/ik,fkj->fij/dot_general | solution.py:44
  478.4 0.0 all-gather.6.cloned.1.call-update
  478.4 0.0 all-gather.8.cloned.1.call-start
  478.5 1.7 dynamic_slice.26
  480.2 115.6 %all-gather.6.cloned.1.call-done = f32[4,384,1536]{1,2,0:T(8,128)} async-done(((f32[4,384,768]{1,2,0:T(8,128)}), f32[4,384,1536]{1,2,0:T(8,128)}) %all-gather.6.cloned.1.call-update) | async-done | bytes 9437200 | tf_op jit(solution)/shard_map/all_gather | solution.py:47
  595.8 28.5 %broadcast_add_fusion = f32[4,384,768]{2,1,0:T(8,128)} fusion(f32[384,768]{1,0:T(8,128)S(1)} %dynamic_slice.26, f32[4,384,1536]{1,2,0:T(8,128)} %all-gather.6.cloned.1.call-done, f32[1536,1536]{1,0:T(8,128)} %param.15, s32[]{:T(128)S(6)} %select_n.16), kind=kOutput, calls=%fused_computation.6 | convolution fusion | flops 21744451584 | bytes 20054020 | tf_op jit(solution)/shard_map/fik,kj->fij/dot_general | solution.py:48
  624.3 0.0 all-gather.8.cloned.1.call-update
  624.4 119.4 %all-gather.8.cloned.1.call-done = f32[4,1536,768]{2,1,0:T(8,128)} async-done(((f32[4,384,768]{2,1,0:T(8,128)}), f32[4,1536,768]{2,1,0:T(8,128)}) %all-gather.8.cloned.1.call-update) | async-done | bytes 18874384 | tf_op jit(solution)/shard_map/all_gather | solution.py:53
  743.8 28.2 %fusion.43 = f32[4,384,768]{2,1,0:T(8,128)} fusion(f32[4,384,1536]{1,2,0:T(8,128)} %all-gather.6.cloned.1.call-done, f32[4,1536,768]{2,1,0:T(8,128)} %all-gather.8.cloned.1.call-done), kind=kOutput, calls=%fused_computation.44 | convolution fusion | flops 21743271936 | bytes 33030144 | tf_op jit(solution)/shard_map/fik,fkj->fij/dot_general | solution.py:52
Async XLA Ops:
  6.5 13.3 %copy-start = (f32[1536,384]{1,0:T(8,128)S(1)}, f32[1536,384]{1,0:T(8,128)}, u32[]{:S(2)}) copy-start(f32[1536,384]{1,0:T(8,128)} %param.8) | copy-start | bytes 7077892
  6.5 190.9 %reduce-scatter.2.cloned.1.call-start = ((), (), s32[]{:S(2)}) async-start(), calls=%async_computation.2 | async-start | bytes 11796480 | tf_op jit(solution)/shard_map/reduce_scatter | solution.py:34
  33.3 165.9 %copy-start.1 = (f32[4]{0:T(128)S(1)}, f32[4]{0:T(128)}, u32[]{:S(2)}) copy-start(f32[4]{0:T(128)} %param.12) | copy-start | bytes 52
  33.3 165.9 %copy-start.2 = (f32[16]{0:T(128)S(1)}, f32[16]{0:T(128)}, u32[]{:S(2)}) copy-start(f32[16]{0:T(128)} %param.14) | copy-start | bytes 196
  33.3 165.9 %copy-start.3 = (f32[4]{0:T(128)S(1)}, f32[4]{0:T(128)}, u32[]{:S(2)}) copy-start(f32[4]{0:T(128)} %param.13) | copy-start | bytes 52
  33.3 410.3 %all-gather.4.cloned.1.call-start = ((), (), s32[]{:S(2)}) async-start(), calls=%async_computation.3 | async-start | bytes 23592960 | tf_op jit(solution)/shard_map/all_gather | solution.py:45
  324.1 271.7 %all-gather.6.cloned.1.call-start = ((), (), s32[]{:S(2)}) async-start(), calls=%async_computation.4 | async-start | bytes 14155776 | tf_op jit(solution)/shard_map/all_gather | solution.py:47
  478.4 265.4 %all-gather.8.cloned.1.call-start = ((), (), s32[]{:S(2)}) async-start(), calls=%async_computation.5 | async-start | bytes 23592960 | tf_op jit(solution)/shard_map/all_gather | solution.py:53
Sparse Core Ops, SparseCore 0:
  33.4 163.9 reduce-scatter.1
  324.2 119.3 all-gather.3
  478.5 117.2 all-gather.5
  624.5 119.2 all-gather.7
where the time goes:
time: 788 us; the launch traced here: 779 us
  waiting for transfers between devices  509 us (65%)
  matrix products  114 us (14%)
  blocking collectives  109 us (14%)
  local copies, waits for them, and re-layouts  14.5 us (2%)
  between operations  13.4 us (2%)
  starting transfers between devices  9.43 us (1%)
  other arithmetic  8.79 us (1%)
    reduce_scatter x1, waiting for transfers between devices, on_device(): lax.psum_scatter(jnp.stack([green_occ, green_vir], axis=1), 'tm', scatter...  164 us
    all_gather x1, waiting for transfers between devices, on_device(): lax.all_gather(first, 'row', axis=1, tiled=True)  119 us
    all_gather x1, waiting for transfers between devices, on_device(): coupled_rows = lax.all_gather(coupled, 'col', axis=2, tiled=True)  116 us
    all_gather x1, waiting for transfers between devices, on_device(): lax.all_gather(polar, 'row', axis=1, tiled=True)  110 us
    all_to_all x1, blocking collectives, on_device(): lax.all_to_all(polar_all, 'tm', split_axis=0, concat_axis=1, tiled=True)  109 us
    dot_general x1, matrix products, on_device(): jnp.einsum('ik,fkj->fij', left, lax.all_gather(polar, 'row', axis=1, tile...  34.8 us
    dot_general x1, matrix products, on_device(): jnp.einsum('fik,kj->fij', coupled_rows, coulomb_cols, precision=HIGH)  28.5 us
    dot_general x1, matrix products, on_device(): jnp.einsum('fik,fkj->fij', left, lax.all_gather(first, 'row', axis=1, til...  28.2 us
  transfers between devices with their start and end apart: 4, of which 4 were waited for; matrix products, arithmetic and copies ran while one was open for 0% of the time, Pallas kernels for 0%

commit v1 on v0

--- a/solution.py
+++ b/solution.py
@@ -1,9 +1,376 @@
+import functools
+
 import jax
 import jax.numpy as jnp
 from jax import lax
+from jax.experimental import pallas as pl
+from jax.experimental.pallas import tpu as pltpu
 from jax.sharding import PartitionSpec as P
 
 HIGH = lax.Precision.HIGHEST
+F32, BF16 = jnp.float32, jnp.bfloat16
+VMEM_LIMIT = 60 << 20
+TILE = 256
+
+
+def halves(x):
+    high = x.astype(BF16)
+    return high, (x - high.astype(F32)).astype(BF16)
+
+
+def dot(a, b):
+    return lax.dot_general(a, b, (((1,), (0,)), ((), ())), preferred_element_type=F32)
+
+
+def dot_t(a, b):
+    return lax.dot_general(a, b, (((1,), (1,)), ((), ())), preferred_element_type=F32)
+
+
+def dot3(a_high, a_low, b_high, b_low):
+    return dot(a_high, b_high) + dot(a_low, b_high) + dot(a_high, b_low)
+
+
+def split_kernel(v_ref, high_ref, low_ref):
+    high_ref[...], low_ref[...] = halves(v_ref[...])
+
+
+def split(v):
+    rows, cols = v.shape
+    spec = pl.BlockSpec((rows // 4, cols), lambda i: (i, 0))
+    return pl.pallas_call(
+        split_kernel,
+        grid=(4,),
+        in_specs=[spec],
+        out_specs=[spec] * 2,
+        out_shape=[jax.ShapeDtypeStruct((rows, cols), BF16)] * 2,
+        compiler_params=pltpu.CompilerParams(vmem_limit_bytes=VMEM_LIMIT),
+        name="split_coulomb",
+    )(v)
+
+
+def tile_tables(blocks):
+    lists = ([], [])
+    for i in range(blocks):
+        mine = min(lists, key=len)
+        mine.extend((i, j) for j in range(i, blocks))
+    count = max(map(len, lists))
+    return [tiles + [tiles[-1]] * (count - len(tiles)) for tiles in lists]
+
+
+def green_kernel(species, pieces, first, last, tab_i, tab_j, fresh, offset, coef, *refs):
+    refs = list(refs)
+    sources = [refs.pop(0) for _ in range(pieces)]
+    factor = refs.pop(0)
+    acc_in = None if first else refs.pop(0)
+    occ_in = refs.pop(0) if last else None
+    outs = [refs.pop(0) for _ in range(2 if last else 1)]
+    c_buf, left, right, sem = refs
+    step = pl.program_id(0)
+    width = c_buf.shape[1]
+    times = factor.shape[0]
+
+    @pl.when(step == 0)
+    def _():
+        copies = []
+        if pieces == 1:
+            copies.append(pltpu.make_async_copy(sources[0], c_buf, sem))
+        else:
+            per = sources[0].shape[0]
+            rows = sources[0].shape[2]
+            for s, source in enumerate(sources):
+                for p in range(per):
+                    start = pl.multiple_of(offset[s * per + p], 16)
+                    copies.append(
+                        pltpu.make_async_copy(
+                            source.at[p, species], c_buf.at[pl.ds(start, rows), :], sem
+                        )
+                    )
+        for copy in copies:
+            copy.start()
+        for copy in copies:
+            copy.wait()
+        high, low = halves(c_buf[...])
+        right[:, :width] = high
+        right[:, width : 2 * width] = high
+        right[:, 2 * width :] = low
+
+    @pl.when(fresh[step] == 1)
+    def _():
+        row = pl.multiple_of(tab_i[step] * TILE, TILE)
+        c = c_buf[pl.ds(row, TILE), :]
+        for t in range(times):
+            high, low = halves(c * factor[t : t + 1, :])
+            s = slice(t * TILE, (t + 1) * TILE)
+            left[s, :width] = high
+            left[s, width : 2 * width] = low
+            left[s, 2 * width :] = high
+
+    col = pl.multiple_of(tab_j[step] * TILE, TILE)
+    green = dot_t(left[...], right[pl.ds(col, TILE), :])
+    green = green.reshape(1, times, TILE, TILE)
+    if not first:
+        green = green + acc_in[...]
+    if not last:
+        outs[0][...] = green
+    else:
+        for n, out in enumerate(outs):
+            total = jnp.zeros((TILE, TILE), F32)
+            for t in range(times):
+                total = total + coef[n, t] * (occ_in[0, t] * green[0, t])
+            out[0] = total
+
+
+def green_call(species, sources, factor, tables, offset, coef, grid, acc=None, occ=None):
+    times, width = factor.shape
+    count = tables[0].shape[0]
+    first, last = acc is None, occ is not None
+    acc_spec = pl.BlockSpec((1, times, TILE, TILE), lambda n, *_: (n, 0, 0, 0))
+    tile_spec = pl.BlockSpec((1, TILE, TILE), lambda n, *_: (n, 0, 0))
+    args = list(sources) + [factor]
+    specs = [pl.BlockSpec(memory_space=pl.ANY)] * len(sources)
+    specs += [pl.BlockSpec((times, width), lambda n, *_: (0, 0))]
+    aliases = {}
+    if not first:
+        if not last:
+            aliases = {5 + len(args): 0}
+        args.append(acc)
+        specs.append(acc_spec)
+    if last:
+        args.append(occ)
+        specs.append(acc_spec)
+        out_shape = [jax.ShapeDtypeStruct((count, TILE, TILE), F32)] * 2
+        out_specs = [tile_spec] * 2
+    else:
+        out_shape = jax.ShapeDtypeStruct((count, times, TILE, TILE), F32)
+        out_specs = acc_spec
+    flops = 2 * 3 * count * times * TILE * TILE * width
+    return pl.pallas_call(
+        functools.partial(green_kernel, species, len(sources), first, last),
+        grid_spec=pltpu.PrefetchScalarGridSpec(
+            num_scalar_prefetch=5,
+            grid=(count,),
+            in_specs=specs,
+            out_specs=out_specs,
+            scratch_shapes=[
+                pltpu.VMEM((grid, width), F32),
+                pltpu.VMEM((times * TILE, 3 * width), BF16),
+                pltpu.VMEM((grid, 3 * width), BF16),
+                pltpu.SemaphoreType.DMA,
+            ],
+        ),
+        out_shape=out_shape,
+        input_output_aliases=aliases,
+        compiler_params=pltpu.CompilerParams(vmem_limit_bytes=VMEM_LIMIT),
+        cost_estimate=pl.CostEstimate(flops=flops, bytes_accessed=24 << 20, transcendentals=0),
+        name="green_" + ("occ", "vir")[species],
+    )(*tables, offset, coef, *args)
+
+
+def assemble_kernel(tab_i, tab_j, tile_ref, high_ref, low_ref):
+    n = pl.program_id(0)
+    i = pl.multiple_of(tab_i[n] * TILE, TILE)
+    j = pl.multiple_of(tab_j[n] * TILE, TILE)
+    tile = tile_ref[0]
+    high_ref[pl.ds(i, TILE), pl.ds(j, TILE)], low_ref[pl.ds(i, TILE), pl.ds(j, TILE)] = halves(tile)
+
+    @pl.when(tab_i[n] != tab_j[n])
+    def _():
+        high, low = halves(tile.T)
+        high_ref[pl.ds(j, TILE), pl.ds(i, TILE)] = high
+        low_ref[pl.ds(j, TILE), pl.ds(i, TILE)] = low
+
+
+def assemble(tiles, tab_i, tab_j, grid):
+    whole = pl.BlockSpec((grid, grid), lambda n, *_: (0, 0))
+    return pl.pallas_call(
+        assemble_kernel,
+        grid_spec=pltpu.PrefetchScalarGridSpec(
+            num_scalar_prefetch=2,
+            grid=(tiles.shape[0],),
+            in_specs=[pl.BlockSpec((1, TILE, TILE), lambda n, *_: (n, 0, 0))],
+            out_specs=[whole] * 2,
+        ),
+        out_shape=[jax.ShapeDtypeStruct((grid, grid), BF16)] * 2,
+        compiler_params=pltpu.CompilerParams(vmem_limit_bytes=VMEM_LIMIT),
+        name="assemble_polar",
+    )(tab_i, tab_j, tiles)
+
+
+def chain_kernel(block, at, v_high, v_low, p_high, p_low, near_ref, far_ref, *scratch):
+    vh, vl, ph, plo, rh, rl, xf, xh, xl, sem_p, sem_v, sem_r = scratch
+    n = vh.shape[0]
+    m = rh.shape[0]
+    half = near_ref.shape[1]
+    count = n // block
+    row = pl.multiple_of(at[0], 16)
+    row_copies = [
+        pltpu.make_async_copy(v_high.at[pl.ds(row, m), :], rh, sem_r.at[0]),
+        pltpu.make_async_copy(v_low.at[pl.ds(row, m), :], rl, sem_r.at[1]),
+    ]
+
+    def column_copies(pairs, sems, b):
+        cols = pl.ds(b * block, block)
+        return [
+            pltpu.make_async_copy(src.at[:, cols], dst.at[:, cols], sems.at[k, b])
+            for k, (src, dst) in enumerate(pairs)
+        ]
+
+    p_copies = [column_copies(((p_high, ph), (p_low, plo)), sem_p, b) for b in range(count)]
+    v_copies = [column_copies(((v_high, vh), (v_low, vl)), sem_v, b) for b in range(count)]
+    for copy in row_copies:
+        copy.start()
+    for b in range(count):
+        for copy in p_copies[b]:
+            copy.start()
+    for copy in row_copies:
+        copy.wait()
+    high, low = rh[...], rl[...]
+    for b in range(count):
+        for copy in p_copies[b]:
+            copy.wait()
+        for copy in v_copies[b]:
+            copy.start()
+        s = slice(b * block, (b + 1) * block)
+        r = dot3(high, low, ph[:, s], plo[:, s])
+        xf[:, s] = r
+        xh[:, s], xl[:, s] = halves(r)
+    high, low = xh[...], xl[...]
+    for b in range(count):
+        for copy in v_copies[b]:
+            copy.wait()
+        s = slice(b * block, (b + 1) * block)
+        rh[:, s], rl[:, s] = halves(dot3(high, low, vh[:, s], vl[:, s]))
+    high, low = rh[...], rl[...]
+    for b in range(count):
+        s = slice(b * block, (b + 1) * block)
+        xh[:, s], xl[:, s] = halves(xf[:, s] + dot3(high, low, ph[:, s], plo[:, s]))
+    high, low = xh[...], xl[...]
+    near = pl.multiple_of(at[1] * half, 128)
+    far = pl.multiple_of((1 - at[1]) * half, 128)
+    for start, out in ((far, far_ref), (near, near_ref)):
+        out[...] = dot3(high, low, vh[:, pl.ds(start, half)], vl[:, pl.ds(start, half)])
+
+
+def chain(at, v_high, v_low, p_high, p_low, rows, cols):
+    n = v_high.shape[0]
+    block = n // 3 if n % 384 == 0 else n
+    count = n // block
+    big = pltpu.VMEM((n, n), BF16)
+    strip = pltpu.VMEM((rows, n), BF16)
+    return pl.pallas_call(
+        functools.partial(chain_kernel, block),
+        in_specs=[pl.BlockSpec(memory_space=pltpu.SMEM)] + [pl.BlockSpec(memory_space=pl.ANY)] * 4,
+        out_specs=[pl.BlockSpec(memory_space=pltpu.VMEM)] * 2,
+        out_shape=[jax.ShapeDtypeStruct((rows, cols), F32)] * 2,
+        scratch_shapes=[big] * 4
+        + [strip] * 2
+        + [pltpu.VMEM((rows, n), F32)]
+        + [strip] * 2
+        + [pltpu.SemaphoreType.DMA((2, count))] * 2
+        + [pltpu.SemaphoreType.DMA((2,))],
+        compiler_params=pltpu.CompilerParams(vmem_limit_bytes=VMEM_LIMIT),
+        cost_estimate=pl.CostEstimate(flops=24 * rows * n * n, bytes_accessed=20 << 20, transcendentals=0),
+        name="chain",
+    )(at, v_high, v_low, p_high, p_low)
+
+
+def swap(x, axis, bit):
+    size = lax.axis_size(axis)
+    return lax.ppermute(x, axis, [(i, i ^ bit) for i in range(size)])
+
+
+def ring(x, axis):
+    size = lax.axis_size(axis)
+    return lax.ppermute(x, axis, [(i, (i + 1) % size) for i in range(size)])
+
+
+def swap_far(x):
+    rows, cols = lax.axis_size("row"), lax.axis_size("col")
+    pairs = [(r * cols + c, (r ^ 1) * cols + (c ^ 1)) for r in range(rows) for c in range(cols)]
+    return lax.ppermute(x, ("row", "col"), pairs)
+
+
+def on_plane(c_occ, c_vir, eps_occ, eps_vir, tau, tweight, omega, coulomb):
+    grid = coulomb.shape[0]
+    planes = lax.axis_size("tm")
+    rows_n, cols_n = lax.axis_size("row"), lax.axis_size("col")
+    z, r, x = lax.axis_index("tm"), lax.axis_index("row"), lax.axis_index("col")
+    y, core = r // 2, r % 2
+    own = grid // (rows_n * cols_n)
+    tile_rows, tile_cols = grid // rows_n, grid // cols_n
+
+    def place(dy, dc, dx):
+        return ((((y ^ dy) * 2 + (core ^ dc)) * cols_n) + (x ^ dx)) * own
+
+    shifts = [(0, 0), (0, 1), (1, 0), (1, 1)]
+    offset = jnp.stack([place(dy, dc, dx) for dc in range(2) for dy, dx in shifts]).astype(jnp.int32)
+    start = place(0, 0, 0)
+    piece = jnp.stack(
+        [
+            lax.dynamic_slice_in_dim(c_occ, start, own, 0),
+            lax.dynamic_slice_in_dim(c_vir, start, own, 0),
+        ]
+    )
+    eps = lax.all_gather(jnp.stack([eps_occ, -eps_vir]), "tm", axis=0)
+    factors = jnp.exp(eps[:, :, None, :] * tau[None, None, :, None])
+    factors_here = jnp.exp(jnp.stack([eps_occ, -eps_vir])[:, None, :] * tau[None, :, None])
+
+    gamma = tweight[None, :] * jnp.cos(omega[:, None] * tau[None, :])
+    per_plane = omega.shape[0] // planes
+    mine = z * per_plane + x * 2 + core
+    other = z * per_plane + x * 2 + 1 - core
+    coef = -2.0 * jnp.stack([gamma[mine], gamma[other]])
+
+    lists = tile_tables(grid // TILE)
+    tab = jnp.array(lists, jnp.int32)
+    fresh = jnp.array(
+        [[int(n == 0 or t[n][0] != t[n - 1][0]) for n in range(len(t))] for t in lists], jnp.int32
+    )
+    tables = (tab[core, :, 0], tab[core, :, 1], fresh[core])
+    tab_both = jnp.concatenate([tab[core], tab[1 - core]])
+
+    v_high, v_low = split(coulomb)
+    acc = [
+        green_call(s, [c], factors_here[s], tables, offset, coef, grid)
+        for s, c in enumerate((c_occ, c_vir))
+    ]
+    for t in range(1, planes):
+        piece = ring(piece, "tm")
+        by_x = swap(piece, "col", 1)
+        by_y = swap(piece, "row", 2)
+        far_occ = swap(by_x[0], "row", 2)
+        far_vir = swap(by_y[1], "col", 1)
+        chip = jnp.stack([piece, by_x, by_y, jnp.stack([far_occ, far_vir])])
+        chips = [chip, swap(chip, "row", 1)]
+        factor = factors[(z - t) % planes]
+        if t < planes - 1:
+            acc = [
+                green_call(s, chips, factor[s], tables, offset, coef, grid, acc[s])
+                for s in range(2)
+            ]
+        else:
+            acc[0] = green_call(0, chips, factor[0], tables, offset, coef, grid, acc[0])
+            mine_tiles, other_tiles = green_call(
+                1, chips, factor[1], tables, offset, coef, grid, acc[1], acc[0]
+            )
+    tiles = jnp.concatenate([mine_tiles, swap(other_tiles, "row", 1)])
+    p_high, p_low = assemble(tiles, tab_both[:, 0], tab_both[:, 1], grid)
+
+    out = jnp.zeros((per_plane, tile_rows, tile_cols), F32)
+
+    def put(out, value, dx, dc):
+        return lax.dynamic_update_slice(out, value[None], ((x ^ dx) * 2 + (core ^ dc), 0, 0))
+
+    for dc in range(2):
+        at = jnp.stack([(y * 2 + (core ^ dc)) * tile_rows, x]).astype(jnp.int32)
+        near, far = chain(at, v_high, v_low, p_high, p_low, tile_rows, tile_cols)
+        if dc == 0:
+            out = put(out, near, 0, 0)
+            out = put(out, swap(far, "col", 1), 1, 0)
+        else:
+            out = put(out, swap(near, "row", 1), 0, 1)
+            out = put(out, swap_far(far), 1, 1)
+    return out
 
 
 def green_block(rows_c, cols_c, energies, taus, sign):
@@ -13,7 +380,7 @@
     lead = (rows_c.shape[0], taus.shape[0])
     flat = scaled.reshape(lead[0] * lead[1], width)
     product = lax.dot_general(
-        flat, cols_c, (((1,), (1,)), ((), ())), precision=HIGH, preferred_element_type=jnp.float32
+        flat, cols_c, (((1,), (1,)), ((), ())), precision=HIGH, preferred_element_type=F32
     )
     return product.reshape(lead[0], lead[1], cols_c.shape[0])
 
@@ -40,23 +407,29 @@
     coulomb_rows = lax.dynamic_slice_in_dim(coulomb, row_start, tile_rows, 0)
     coulomb_cols = lax.dynamic_slice_in_dim(coulomb, col_start, tile_cols, 1)
     coulomb_tile = lax.dynamic_slice_in_dim(coulomb_rows, col_start, tile_cols, 1)
-    left = coulomb_rows
     coupled = jnp.einsum(
-        "ik,fkj->fij", left, lax.all_gather(polar, "row", axis=1, tiled=True), precision=HIGH
+        "ik,fkj->fij", coulomb_rows, lax.all_gather(polar, "row", axis=1, tiled=True), precision=HIGH
     )
     coupled_rows = lax.all_gather(coupled, "col", axis=2, tiled=True)
     first = coulomb_tile[None] + jnp.einsum(
         "fik,kj->fij", coupled_rows, coulomb_cols, precision=HIGH
     )
-    left = coupled_rows
     return jnp.einsum(
-        "fik,fkj->fij", left, lax.all_gather(first, "row", axis=1, tiled=True), precision=HIGH
+        "fik,fkj->fij", coupled_rows, lax.all_gather(first, "row", axis=1, tiled=True), precision=HIGH
     )
 
 
 def solution(mesh):
     in_specs = (P(None, "tm"), P(None, "tm"), P("tm"), P("tm"), P(), P(), P(), P())
     out_specs = P("tm", "row", "col")
+    square = mesh.shape["row"] == 4 and mesh.shape["col"] == 2
+
+    def body(*args):
+        omega, coulomb = args[6], args[7]
+        fits = omega.shape[0] == 2 * mesh.shape["tm"] * mesh.shape["col"]
+        fits = fits and coulomb.shape[0] % (2 * TILE) == 0 and args[0].shape[1] % 128 == 0
+        return (on_plane if square and fits else on_device)(*args)
+
     return jax.shard_map(
-        on_device, mesh=mesh, in_specs=in_specs, out_specs=out_specs, check_vma=False
-    )
+        body, mesh=mesh, in_specs=in_specs, out_specs=out_specs, check_vma=False
+    )

time: 788 us -> 377 us (0.48)
  waiting for transfers between devices: 509 us -> 67.7 us
  Pallas kernels: 0 us -> 206 us
  matrix products: 114 us -> 0 us
  blocking collectives: 109 us -> 13.2 us
  other arithmetic: 8.79 us -> 49 us
  between operations: 13.4 us -> 0.65 us
  starting transfers between devices: 9.43 us -> 19.2 us
    all_gather x3 -> x0, waiting for transfers between devices: 345 us -> none  [the longest x1 119 us: on_device(): lax.all_gather(first, 'row', axis=1, tiled=True)]
    pallas_call x0 -> x11, Pallas kernels: none -> 206 us  [the longest x8 148 us: green_call(): pl.pallas_call(functools.partial(green_kernel, species, len(sources), fir...]
    reduce_scatter x1 -> x0, waiting for transfers between devices: 164 us -> none  [on_device(): lax.psum_scatter(jnp.stack([green_occ, green_vir], axis=1), 'tm', scatter...]
    dot_general x6 -> x0, matrix products: 114 us -> none  [the longest x1 34.8 us: on_device(): jnp.einsum('ik,fkj->fij', left, lax.all_gather(polar, 'row', axis=1, tile...]
    all_to_all x1 -> x0, blocking collectives: 109 us -> none  [on_device(): lax.all_to_all(polar_all, 'tm', split_axis=0, concat_axis=1, tiled=True)]
    ppermute x0 -> x22, waiting for transfers between devices: none -> 67.7 us  [the longest x3 26 us: ring(): return lax.ppermute(x, axis, [(i, (i + 1) % size) for i in range(size)])]
    pallas_call x0 -> x1, other arithmetic: none -> 32.9 us  [chain(): pl.pallas_call(functools.partial(chain_kernel, block), in_specs=[pl.Block...]
    ppermute x0 -> x22, starting transfers between devices: none -> 19.2 us  [the longest x18 15.2 us: swap(): return lax.ppermute(x, axis, [(i, i ^ bit) for i in range(size)])]
  transfers between devices with their start and end apart: 4 -> 22, of which waited for: 4 -> 9; matrix products, arithmetic and copies ran while one was open for 0% -> 6% of each run, Pallas kernels for 0% -> 40%
where the time goes in v1:
time: 377 us; the launch traced here: 370 us
  Pallas kernels  206 us (55%)
  waiting for transfers between devices  67.7 us (18%)
  other arithmetic  49 us (13%)
  starting transfers between devices  19.2 us (5%)
  local copies, waits for them, and re-layouts  14.2 us (4%)
  blocking collectives  13.2 us (4%)
    pallas_call x8, Pallas kernels, green_call(): pl.pallas_call(functools.partial(green_kernel, species, len(sources), fir...  148 us
    pallas_call x1, other arithmetic, chain(): pl.pallas_call(functools.partial(chain_kernel, block), in_specs=[pl.Block...  32.9 us
    pallas_call x1, Pallas kernels, chain(): pl.pallas_call(functools.partial(chain_kernel, block), in_specs=[pl.Block...  32.8 us
    ppermute x3, waiting for transfers between devices, ring(): return lax.ppermute(x, axis, [(i, (i + 1) % size) for i in range(size)])  26 us
    ppermute x1, waiting for transfers between devices, swap_far(): return lax.ppermute(x, ('row', 'col'), pairs)  24.3 us
    ppermute x18, waiting for transfers between devices, swap(): return lax.ppermute(x, axis, [(i, i ^ bit) for i in range(size)])  17.4 us
    pallas_call x1, Pallas kernels, assemble(): pl.pallas_call(assemble_kernel, grid_spec=pltpu.PrefetchScalarGridSpec(nu...  17 us
    ppermute x18, starting transfers between devices, swap(): return lax.ppermute(x, axis, [(i, i ^ bit) for i in range(size)])  15.2 us
  transfers between devices with their start and end apart: 22, of which 9 were waited for; matrix products, arithmetic and copies ran while one was open for 6% of the time, Pallas kernels for 40%

profile of v1, /device:TPU:0, one launch (start us, length us, event | category | flops | bytes accessed | tf_op | source)
XLA Modules:
  0.0 370.0 jit_solution(3929752472466202551)
XLA Ops:
  0.1 1.1 dynamic-slice_bitcast_fusion
  1.3 3.1 collective-permute-start
  4.4 0.1 cosine_multiply_fusion
  4.5 0.1 multiply_exponential_fusion.1
  4.6 15.1 %collective-permute-done = f32[2,192,384]{2,1,0:T(8,128)S(1)} collective-permute-done((f32[2,192,384]{2,1,0:T(8,128)S(1)}, f32[2,192,384]{2,1,0:T(8,128)S(1)}, u32[]{:S(2)}, u32[]{:S(2)}) %collective-permute-start) | collective-permute-done | bytes 589856 | tf_op jit(solution)/shard_map/ppermute | solution.py:284
  19.7 1.5 collective-permute-start.13
  21.2 0.6 maximum_multiply_fusion.coef
  21.8 1.5 collective-permute-start.14
  23.3 0.6 fusion.3
  23.9 0.6 stack.150.offset
  24.5 0.6 slice_bitcast_fusion.6
  25.1 0.5 fusion.4.fresh
  25.6 8.6 %collective-permute-done.13 = f32[2,192,384]{2,1,0:T(8,128)S(1)} collective-permute-done((f32[2,192,384]{2,1,0:T(8,128)S(1)}, f32[2,192,384]{2,1,0:T(8,128)S(1)}, u32[]{:S(2)}, u32[]{:S(2)}) %collective-permute-start.13) | collective-permute-done | bytes 589856 | tf_op jit(solution)/shard_map/ppermute | solution.py:279
  34.2 1.3 collective-permute-start.15
  35.6 0.5 collective-permute-done.14
  36.1 1.0 collective-permute-start.16
  37.1 3.6 collective-permute-done.1
  40.7 0.5 collective-permute-start.8
  41.2 0.8 collective-permute-start.9
  42.0 15.8 %green_occ.4.refs_3_ = f32[11,4,256,256]{3,2,1,0:T(8,128)} custom-call(s32[11]{0:T(128)} %get-tuple-element.42.tab_i, s32[11]{0:T(128)} %get-tuple-element.41.tab_j, s32[11]{0:T(128)} %fusion.4.fresh, s32[8]{0:T(128)} %stack.150.offset, f32[2,4]{1,0:T(2,128)} %maximum_multiply_fusion.coef, f32[1536,384]{1,0:T(8,128)} %refs_0_.3, ...), custom_call_target="tpu_custom_call" | custom-call | flops 6643777536 | bytes 25165824 | tf_op jit(solution)/shard_map/green_occ/pallas_call | solution.py:147
  57.9 1.0 maximum_bitcast_fusion.2
  58.9 1.6 pad_maximum_fusion.3.refs_0_
  60.6 0.9 slice_bitcast_fusion.3
  61.5 1.3 collective-permute-start.10
  62.8 0.7 slice_bitcast_fusion.2
  63.5 1.5 collective-permute-start.11
  65.0 7.4 %collective-permute-done.2 = f32[2,192,384]{2,1,0:T(8,128)} collective-permute-done((f32[2,192,384]{2,1,0:T(8,128)}, f32[2,192,384]{2,1,0:T(8,128)}, u32[]{:S(2)}, u32[]{:S(2)}) %collective-permute-start.2) | collective-permute-done | bytes 589856 | tf_op jit(solution)/shard_map/ppermute | solution.py:284
  72.4 1.0 collective-permute-start.3
  73.4 1.5 collective-permute-start.4
  75.0 15.8 %green_vir.4.refs_3_ = f32[11,4,256,256]{3,2,1,0:T(8,128)} custom-call(s32[11]{0:T(128)} %get-tuple-element.42.tab_i, s32[11]{0:T(128)} %get-tuple-element.41.tab_j, s32[11]{0:T(128)} %fusion.4.fresh, s32[8]{0:T(128)} %stack.150.offset, f32[2,4]{1,0:T(2,128)} %maximum_multiply_fusion.coef, f32[1536,384]{1,0:T(8,128)} %refs_0_.2, ...), custom_call_target="tpu_custom_call" | custom-call | flops 6643777536 | bytes 25165824 | tf_op jit(solution)/shard_map/green_vir/pallas_call | solution.py:147
  90.8 13.2 %all-gather.1 = f32[4,2,384]{2,1,0:T(2,128)S(1)} all-gather(f32[1,2,384]{2,1,0:T(2,128)S(1)} %get-tuple-element.40), channel_id=2, replica_groups=mesh['tm'=4,'row'=4,'col'=2] {'tm'}, dimensions={0}, use_global_device_ids=true | all-gather | bytes 15360 | tf_op jit(solution)/shard_map/all_gather | solution.py:314
  104.0 1.1 maximum_bitcast_fusion.1
  105.1 2.7 pad_maximum_fusion.2.refs_0_
  107.8 1.0 slice_bitcast_fusion.5
  108.8 0.6 collective-permute-start.5
  109.4 1.0 slice_bitcast_fusion.4
  110.4 1.1 collective-permute-start.6
  111.5 0.1 multiply_exponential_fusion
  111.6 0.6 dynamic-slice_bitcast_fusion.2
  112.2 6.1 %collective-permute-done.5 = f32[192,384]{1,0:T(8,128)S(1)} collective-permute-done((f32[192,384]{1,0:T(8,128)S(1)}, f32[192,384]{1,0:T(8,128)S(1)}, u32[]{:S(2)}, u32[]{:S(2)}) %collective-permute-start.5) | collective-permute-done | bytes 294944 | tf_op jit(solution)/shard_map/ppermute | solution.py:279
  118.3 1.3 collective-permute-done.6
  119.6 3.1 pad_maximum_fusion.1.refs_0_
  122.7 19.2 %green_occ.5.refs_3_ = f32[11,4,256,256]{3,2,1,0:T(8,128)} custom-call(s32[11]{0:T(128)} %get-tuple-element.42.tab_i, s32[11]{0:T(128)} %get-tuple-element.41.tab_j, s32[11]{0:T(128)} %fusion.4.fresh, s32[8]{0:T(128)} %stack.150.offset, f32[2,4]{1,0:T(2,128)} %maximum_multiply_fusion.coef, ...), custom_call_target="tpu_custom_call", output_to_operand_aliasing={{}: (8, {})} | custom-call | flops 6643777536 | bytes 25165824 | tf_op jit(solution)/shard_map/green_occ/pallas_call | solution.py:147
  141.9 19.2 %green_vir.5.refs_3_ = f32[11,4,256,256]{3,2,1,0:T(8,128)} custom-call(s32[11]{0:T(128)} %get-tuple-element.42.tab_i, s32[11]{0:T(128)} %get-tuple-element.41.tab_j, s32[11]{0:T(128)} %fusion.4.fresh, s32[8]{0:T(128)} %stack.150.offset, f32[2,4]{1,0:T(2,128)} %maximum_multiply_fusion.coef, ...), custom_call_target="tpu_custom_call", output_to_operand_aliasing={{}: (8, {})} | custom-call | flops 6643777536 | bytes 25165824 | tf_op jit(solution)/shard_map/green_vir/pallas_call | solution.py:147
  161.2 19.2 %green_occ.6.refs_3_ = f32[11,4,256,256]{3,2,1,0:T(8,128)} custom-call(s32[11]{0:T(128)} %get-tuple-element.42.tab_i, s32[11]{0:T(128)} %get-tuple-element.41.tab_j, s32[11]{0:T(128)} %fusion.4.fresh, s32[8]{0:T(128)} %stack.150.offset, f32[2,4]{1,0:T(2,128)} %maximum_multiply_fusion.coef, ...), custom_call_target="tpu_custom_call", output_to_operand_aliasing={{}: (8, {})} | custom-call | flops 6643777536 | bytes 25165824 | tf_op jit(solution)/shard_map/green_occ/pallas_call | solution.py:147
  180.4 19.2 %green_vir.6.refs_3_ = f32[11,4,256,256]{3,2,1,0:T(8,128)} custom-call(s32[11]{0:T(128)} %get-tuple-element.42.tab_i, s32[11]{0:T(128)} %get-tuple-element.41.tab_j, s32[11]{0:T(128)} %fusion.4.fresh, s32[8]{0:T(128)} %stack.150.offset, f32[2,4]{1,0:T(2,128)} %maximum_multiply_fusion.coef, ...), custom_call_target="tpu_custom_call", output_to_operand_aliasing={{}: (8, {})} | custom-call | flops 6643777536 | bytes 25165824 | tf_op jit(solution)/shard_map/green_vir/pallas_call | solution.py:147
  199.7 19.2 %green_occ.7.refs_4_ = f32[11,4,256,256]{3,2,1,0:T(8,128)} custom-call(s32[11]{0:T(128)} %get-tuple-element.42.tab_i, s32[11]{0:T(128)} %get-tuple-element.41.tab_j, s32[11]{0:T(128)} %fusion.4.fresh, s32[8]{0:T(128)} %stack.150.offset, f32[2,4]{1,0:T(2,128)} %maximum_multiply_fusion.coef, ...), custom_call_target="tpu_custom_call", output_to_operand_aliasing={{}: (8, {})} | custom-call | flops 6643777536 | bytes 25165824 | tf_op jit(solution)/shard_map/green_occ/pallas_call | solution.py:147
  218.9 20.2 %green_vir.7 = (f32[11,256,256]{2,1,0:T(8,128)}, f32[11,256,256]{2,1,0:T(8,128)}) custom-call(s32[11]{0:T(128)} %get-tuple-element.42.tab_i, s32[11]{0:T(128)} %get-tuple-element.41.tab_j, s32[11]{0:T(128)} %fusion.4.fresh, s32[8]{0:T(128)} %stack.150.offset, f32[2,4]{1,0:T(2,128)} %maximum_multiply_fusion.coef, ...), custom_call_target="tpu_custom_call" | custom-call | flops 6643777536 | bytes 25165824 | tf_op jit(solution)/shard_map/green_vir/pallas_call | solution.py:147
  239.2 8.3 %split_coulomb.1 = (bf16[1536,1536]{1,0:T(8,128)(2,1)}, bf16[1536,1536]{1,0:T(8,128)(2,1)}) custom-call(f32[1536,1536]{1,0:T(8,128)} %v_ref.1), custom_call_target="tpu_custom_call" | custom-call | tf_op jit(solution)/shard_map/split_coulomb/pallas_call | solution.py:40
  247.6 0.6 pad_add_fusion.1
  248.2 0.6 slice_bitcast_fusion.8
  248.8 5.0 %pad_maximum_fusion.tile_ref = f32[22,256,256]{2,1,0:T(8,128)} fusion(f32[11,256,256]{2,1,0:T(8,128)} %collective-permute-done.18, f32[11,256,256]{2,1,0:T(8,128)S(1)} %copy-done.1), kind=kLoop, calls=%fused_computation | loop fusion | flops 1441792 | bytes 11534336 | tf_op jit(solution)/shard_map/concatenate | solution.py:356
  253.8 17.0 %assemble_polar.1 = (bf16[1536,1536]{1,0:T(8,128)(2,1)}, bf16[1536,1536]{1,0:T(8,128)(2,1)}) custom-call(s32[22]{0:T(128)} %get-tuple-element.46.tab_i, s32[22]{0:T(128)} %get-tuple-element.45.tab_j, f32[22,256,256]{2,1,0:T(8,128)} %pad_maximum_fusion.tile_ref), custom_call_target="tpu_custom_call" | custom-call | tf_op jit(solution)/shard_map/assemble_polar/pallas_call | solution.py:185
  270.8 2.6 broadcast_in_dim.10
  273.4 32.9 %chain.3 = (f32[4,384,768]{2,1,0:T(8,128)}, f32[384,768]{1,0:T(8,128)}) fusion(f32[4,384,768]{2,1,0:T(8,128)} %broadcast_in_dim.10, s32[]{:T(128)S(6)} %select_n.76, s32[2]{0:T(128)S(1)} %get-tuple-element.47, bf16[1536,1536]{1,0:T(8,128)(2,1)} %get-tuple-element.15.v_high, bf16[1536,1536]{1,0:T(8,128)(2,1)} %get-tuple-element.16.v_low, ...), kind=kCustom, calls=%fused_computation.7 | custom fusion | flops 21743271936 | bytes 21233676 | tf_op jit(solution)/shard_map/chain/pallas_call | solution.py:260
  306.3 1.0 collective-permute-start.19
  307.4 32.8 %chain.2 = (f32[384,768]{1,0:T(8,128)}, f32[384,768]{1,0:T(8,128)}) custom-call(s32[2]{0:T(128)} %get-tuple-element.48.at, bf16[1536,1536]{1,0:T(8,128)(2,1)} %get-tuple-element.15.v_high, bf16[1536,1536]{1,0:T(8,128)(2,1)} %get-tuple-element.16.v_low, bf16[1536,1536]{1,0:T(8,128)(2,1)} %get-tuple-element.19.p_high, bf16[1536,1536]{1,0:T(8,128)(2,1)} %get-tuple-element.20.p_low), custom_call_target="tpu_custom_call" | custom-call | flops 21743271936 | bytes 20971520 | tf_op jit(solution)/shard_map/chain/pallas_call | solution.py:260
  340.2 0.3 collective-permute-start.20
  340.5 0.8 collective-permute-start.21
  341.4 1.1 bitcast_dynamic-update-slice_fusion.2
  342.5 0.8 collective-permute-done.20
  343.3 1.1 bitcast_dynamic-update-slice_fusion.1
  344.4 24.3 %collective-permute-done.21 = f32[384,768]{1,0:T(8,128)S(1)} collective-permute-done((f32[384,768]{1,0:T(8,128)}, f32[384,768]{1,0:T(8,128)S(1)}, u32[]{:S(2)}, u32[]{:S(2)}) %collective-permute-start.21) | collective-permute-done | bytes 1179680 | tf_op jit(solution)/shard_map/ppermute | solution.py:290
  368.7 1.1 bitcast_dynamic-update-slice_fusion
  (54 shorter events, 0.5 us)
Async XLA Ops:
  0.0 23.3 %copy-start.6 = (s32[2,11,2]{1,2,0:T(2,128)S(1)}, s32[2,11,2]{1,2,0:T(2,128)}, u32[]{:S(2)}) copy-start(s32[2,11,2]{1,2,0:T(2,128)} %constant.78.clone) | copy-start | bytes 532
  0.0 25.1 %copy-start.11 = (s32[2,11]{1,0:T(2,128)S(1)}, s32[2,11]{1,0:T(2,128)}, u32[]{:S(2)}) copy-start(s32[2,11]{1,0:T(2,128)} %constant.79.clone) | copy-start | bytes 268
  0.0 4.3 %copy-start.8 = (f32[384]{0:T(512)S(1)}, f32[384]{0:T(512)}, u32[]{:S(2)}) copy-start(f32[384]{0:T(512)} %param.13) | copy-start | bytes 4612
  0.0 4.3 %copy-start.7 = (f32[384]{0:T(512)S(1)}, f32[384]{0:T(512)}, u32[]{:S(2)}) copy-start(f32[384]{0:T(512)} %param.12) | copy-start | bytes 4612
  0.0 4.4 %copy-start.5 = (f32[4]{0:T(128)S(1)}, f32[4]{0:T(128)}, u32[]{:S(2)}) copy-start(f32[4]{0:T(128)} %param.14) | copy-start | bytes 52
  0.0 4.4 %copy-start.10 = (f32[4]{0:T(128)S(1)}, f32[4]{0:T(128)}, u32[]{:S(2)}) copy-start(f32[4]{0:T(128)} %param.15) | copy-start | bytes 52
  0.0 4.4 %copy-start.9 = (f32[16]{0:T(128)S(1)}, f32[16]{0:T(128)}, u32[]{:S(2)}) copy-start(f32[16]{0:T(128)} %param.16) | copy-start | bytes 196
  1.3 18.4 %collective-permute-start = (f32[2,192,384]{2,1,0:T(8,128)S(1)}, f32[2,192,384]{2,1,0:T(8,128)S(1)}, u32[]{:S(2)}, u32[]{:S(2)}) collective-permute-start(f32[2,192,384]{2,1,0:T(8,128)S(1)} %pad_maximum_fusion.4), channel_id=1, source_target_pairs={{0,8},{8,16},{16,24},{24,0},{1,9},{9,17},{17,25},{25,1},{2,10},{10... | collective-permute-start | bytes 1769480 | tf_op jit(solution)/shard_map/ppermute | solution.py:284
  19.7 38.1 %copy-start.4 = (f32[2,192,384]{2,1,0:T(8,128)}, f32[2,192,384]{2,1,0:T(8,128)S(1)}, u32[]{:S(2)}) copy-start(f32[2,192,384]{2,1,0:T(8,128)S(1)} %collective-permute-done) | copy-start | bytes 1769476
  19.7 14.5 %collective-permute-start.13 = (f32[2,192,384]{2,1,0:T(8,128)S(1)}, f32[2,192,384]{2,1,0:T(8,128)S(1)}, u32[]{:S(2)}, u32[]{:S(2)}) collective-permute-start(f32[2,192,384]{2,1,0:T(8,128)S(1)} %collective-permute-done), channel_id=1, source_target_pairs={{0,1},{1,0},{2,3},{3,2},{4,5},{5,4},{6,7},{7,6},{8,9},{9,8},{10,11... | collective-permute-start | bytes 1769480 | tf_op jit(solution)/shard_map/ppermute | solution.py:279
  21.8 14.3 %collective-permute-start.14 = (f32[2,192,384]{2,1,0:T(8,128)S(1)}, f32[2,192,384]{2,1,0:T(8,128)S(1)}, u32[]{:S(2)}, u32[]{:S(2)}) collective-permute-start(f32[2,192,384]{2,1,0:T(8,128)S(1)} %collective-permute-done), channel_id=1, source_target_pairs={{0,4},{2,6},{4,0},{6,2},{1,5},{3,7},{5,1},{7,3},{8,12},{10,14},{12... | collective-permute-start | bytes 1769480 | tf_op jit(solution)/shard_map/ppermute | solution.py:279
  25.1 15.6 %collective-permute-start.1 = (f32[2,192,384]{2,1,0:T(8,128)S(1)}, f32[2,192,384]{2,1,0:T(8,128)}, u32[]{:S(2)}, u32[]{:S(2)}) collective-permute-start(f32[2,192,384]{2,1,0:T(8,128)S(1)} %collective-permute-done), channel_id=1, source_target_pairs={{0,8},{8,16},{16,24},{24,0},{1,9},{9,17},{17,25},{25,1},{2,10},{10... | collective-permute-start | bytes 1769480 | tf_op jit(solution)/shard_map/ppermute | solution.py:284
  34.2 23.6 %copy-start.2 = (f32[2,192,384]{2,1,0:T(8,128)}, f32[2,192,384]{2,1,0:T(8,128)S(1)}, u32[]{:S(2)}) copy-start(f32[2,192,384]{2,1,0:T(8,128)S(1)} %collective-permute-done.13) | copy-start | bytes 1769476
  34.2 23.6 %collective-permute-start.15 = (f32[192,384]{1,0:T(8,128)S(1)}, f32[192,384]{1,0:T(8,128)S(1)}, u32[]{:S(2)}, u32[]{:S(2)}) collective-permute-start(f32[192,384]{1,0:T(8,128)S(1)} %slice_bitcast_fusion.1), channel_id=1, source_target_pairs={{0,4},{2,6},{4,0},{6,2},{1,5},{3,7},{5,1},{7,3},{8,12},{10,14},{12... | collective-permute-start | bytes 884744 | tf_op jit(solution)/shard_map/ppermute | solution.py:279
  36.1 21.7 %copy-start.3 = (f32[2,192,384]{2,1,0:T(8,128)}, f32[2,192,384]{2,1,0:T(8,128)S(1)}, u32[]{:S(2)}) copy-start(f32[2,192,384]{2,1,0:T(8,128)S(1)} %collective-permute-done.14) | copy-start | bytes 1769476
  36.1 21.7 %collective-permute-start.16 = (f32[192,384]{1,0:T(8,128)S(1)}, f32[192,384]{1,0:T(8,128)}, u32[]{:S(2)}, u32[]{:S(2)}) collective-permute-start(f32[192,384]{1,0:T(8,128)S(1)} %slice_bitcast_fusion), channel_id=1, source_target_pairs={{0,1},{1,0},{2,3},{3,2},{4,5},{5,4},{6,7},{7,6},{8,9},{9,8},{10,11... | collective-permute-start | bytes 884744 | tf_op jit(solution)/shard_map/ppermute | solution.py:279
  40.7 19.9 %collective-permute-start.8 = (f32[2,192,384]{2,1,0:T(8,128)}, f32[2,192,384]{2,1,0:T(8,128)S(1)}, u32[]{:S(2)}, u32[]{:S(2)}) collective-permute-start(f32[2,192,384]{2,1,0:T(8,128)} %collective-permute-done.1), channel_id=1, source_target_pairs={{0,1},{1,0},{2,3},{3,2},{4,5},{5,4},{6,7},{7,6},{8,9},{9,8},{10,11... | collective-permute-start | bytes 1769480 | tf_op jit(solution)/shard_map/ppermute | solution.py:279
  41.2 21.5 %collective-permute-start.9 = (f32[2,192,384]{2,1,0:T(8,128)}, f32[2,192,384]{2,1,0:T(8,128)S(1)}, u32[]{:S(2)}, u32[]{:S(2)}) collective-permute-start(f32[2,192,384]{2,1,0:T(8,128)} %collective-permute-done.1), channel_id=1, source_target_pairs={{0,4},{2,6},{4,0},{6,2},{1,5},{3,7},{5,1},{7,3},{8,12},{10,14},{12... | collective-permute-start | bytes 1769480 | tf_op jit(solution)/shard_map/ppermute | solution.py:279
  57.8 14.6 %collective-permute-start.2 = (f32[2,192,384]{2,1,0:T(8,128)}, f32[2,192,384]{2,1,0:T(8,128)}, u32[]{:S(2)}, u32[]{:S(2)}) collective-permute-start(f32[2,192,384]{2,1,0:T(8,128)} %collective-permute-done.1), channel_id=1, source_target_pairs={{0,8},{8,16},{16,24},{24,0},{1,9},{9,17},{17,25},{25,1},{2,10},{10... | collective-permute-start | bytes 1769480 | tf_op jit(solution)/shard_map/ppermute | solution.py:284
  60.5 30.2 %copy-start = (f32[4,2,192,384]{3,2,1,0:T(8,128)}, f32[4,2,192,384]{3,2,1,0:T(8,128)S(1)}, u32[]{:S(2)}) copy-start(f32[4,2,192,384]{3,2,1,0:T(8,128)S(1)} %pad_maximum_fusion.3.refs_0_) | copy-start | bytes 7077892
  60.5 62.2 %collective-permute-start.17 = (f32[4,2,192,384]{3,2,1,0:T(8,128)S(1)}, f32[4,2,192,384]{3,2,1,0:T(8,128)}, u32[]{:S(2)}, u32[]{:S(2)}) collective-permute-start(f32[4,2,192,384]{3,2,1,0:T(8,128)S(1)} %pad_maximum_fusion.3.refs_0_), channel_id=1, source_target_pairs={{0,2},{2,0},{4,6},{6,4},{1,3},{3,1},{5,7},{7,5},{8,10},{10,8},{12,... | collective-permute-start | bytes 7077896 | tf_op jit(solution)/shard_map/ppermute | solution.py:279
  61.5 42.5 %collective-permute-start.10 = (f32[192,384]{1,0:T(8,128)}, f32[192,384]{1,0:T(8,128)}, u32[]{:S(2)}, u32[]{:S(2)}) collective-permute-start(f32[192,384]{1,0:T(8,128)} %slice_bitcast_fusion.3), channel_id=1, source_target_pairs={{0,4},{2,6},{4,0},{6,2},{1,5},{3,7},{5,1},{7,3},{8,12},{10,14},{12... | collective-permute-start | bytes 884744 | tf_op jit(solution)/shard_map/ppermute | solution.py:279
  63.5 40.5 %collective-permute-start.11 = (f32[192,384]{1,0:T(8,128)}, f32[192,384]{1,0:T(8,128)}, u32[]{:S(2)}, u32[]{:S(2)}) collective-permute-start(f32[192,384]{1,0:T(8,128)} %slice_bitcast_fusion.2), channel_id=1, source_target_pairs={{0,1},{1,0},{2,3},{3,2},{4,5},{5,4},{6,7},{7,6},{8,9},{9,8},{10,11... | collective-permute-start | bytes 884744 | tf_op jit(solution)/shard_map/ppermute | solution.py:279
  72.4 35.4 %collective-permute-start.3 = (f32[2,192,384]{2,1,0:T(8,128)}, f32[2,192,384]{2,1,0:T(8,128)}, u32[]{:S(2)}, u32[]{:S(2)}) collective-permute-start(f32[2,192,384]{2,1,0:T(8,128)} %collective-permute-done.2), channel_id=1, source_target_pairs={{0,1},{1,0},{2,3},{3,2},{4,5},{5,4},{6,7},{7,6},{8,9},{9,8},{10,11... | collective-permute-start | bytes 1769480 | tf_op jit(solution)/shard_map/ppermute | solution.py:279
  73.4 35.9 %collective-permute-start.4 = (f32[2,192,384]{2,1,0:T(8,128)}, f32[2,192,384]{2,1,0:T(8,128)}, u32[]{:S(2)}, u32[]{:S(2)}) collective-permute-start(f32[2,192,384]{2,1,0:T(8,128)} %collective-permute-done.2), channel_id=1, source_target_pairs={{0,4},{2,6},{4,0},{6,2},{1,5},{3,7},{5,1},{7,3},{8,12},{10,14},{12... | collective-permute-start | bytes 1769480 | tf_op jit(solution)/shard_map/ppermute | solution.py:279
  107.8 53.4 %collective-permute-start.12 = (f32[4,2,192,384]{3,2,1,0:T(8,128)}, f32[4,2,192,384]{3,2,1,0:T(8,128)}, u32[]{:S(2)}, u32[]{:S(2)}) collective-permute-start(f32[4,2,192,384]{3,2,1,0:T(8,128)} %pad_maximum_fusion.2.refs_0_), channel_id=1, source_target_pairs={{0,2},{2,0},{4,6},{6,4},{1,3},{3,1},{5,7},{7,5},{8,10},{10,8},{12,... | collective-permute-start | bytes 7077896 | tf_op jit(solution)/shard_map/ppermute | solution.py:279
  108.8 9.5 %collective-permute-start.5 = (f32[192,384]{1,0:T(8,128)S(1)}, f32[192,384]{1,0:T(8,128)S(1)}, u32[]{:S(2)}, u32[]{:S(2)}) collective-permute-start(f32[192,384]{1,0:T(8,128)S(1)} %slice_bitcast_fusion.5), channel_id=1, source_target_pairs={{0,4},{2,6},{4,0},{6,2},{1,5},{3,7},{5,1},{7,3},{8,12},{10,14},{12... | collective-permute-start | bytes 884744 | tf_op jit(solution)/shard_map/ppermute | solution.py:279
  110.4 9.2 %collective-permute-start.6 = (f32[192,384]{1,0:T(8,128)S(1)}, f32[192,384]{1,0:T(8,128)S(1)}, u32[]{:S(2)}, u32[]{:S(2)}) collective-permute-start(f32[192,384]{1,0:T(8,128)S(1)} %slice_bitcast_fusion.4), channel_id=1, source_target_pairs={{0,1},{1,0},{2,3},{3,2},{4,5},{5,4},{6,7},{7,6},{8,9},{9,8},{10,11... | collective-permute-start | bytes 884744 | tf_op jit(solution)/shard_map/ppermute | solution.py:279
  122.7 77.0 %collective-permute-start.7 = (f32[4,2,192,384]{3,2,1,0:T(8,128)}, f32[4,2,192,384]{3,2,1,0:T(8,128)}, u32[]{:S(2)}, u32[]{:S(2)}) collective-permute-start(f32[4,2,192,384]{3,2,1,0:T(8,128)} %pad_maximum_fusion.1.refs_0_), channel_id=1, source_target_pairs={{0,2},{2,0},{4,6},{6,4},{1,3},{3,1},{5,7},{7,5},{8,10},{10,8},{12,... | collective-permute-start | bytes 7077896 | tf_op jit(solution)/shard_map/ppermute | solution.py:279
  239.1 9.7 %collective-permute-start.18 = (f32[11,256,256]{2,1,0:T(8,128)}, f32[11,256,256]{2,1,0:T(8,128)}, u32[]{:S(2)}, u32[]{:S(2)}) collective-permute-start(f32[11,256,256]{2,1,0:T(8,128)} %get-tuple-element.18), channel_id=1, source_target_pairs={{0,2},{2,0},{4,6},{6,4},{1,3},{3,1},{5,7},{7,5},{8,10},{10,8},{12,... | collective-permute-start | bytes 8650760 | tf_op jit(solution)/shard_map/ppermute | solution.py:279
  239.2 9.6 %copy-start.1 = (f32[11,256,256]{2,1,0:T(8,128)S(1)}, f32[11,256,256]{2,1,0:T(8,128)}, u32[]{:S(2)}) copy-start(f32[11,256,256]{2,1,0:T(8,128)} %get-tuple-element.17) | copy-start | bytes 8650756
  306.3 35.1 %collective-permute-start.19 = (f32[384,768]{1,0:T(8,128)}, f32[384,768]{1,0:T(8,128)S(1)}, u32[]{:S(2)}, u32[]{:S(2)}) collective-permute-start(f32[384,768]{1,0:T(8,128)} %get-tuple-element.28), channel_id=1, source_target_pairs={{0,1},{1,0},{2,3},{3,2},{4,5},{5,4},{6,7},{7,6},{8,9},{9,8},{10,11... | collective-permute-start | bytes 3538952 | tf_op jit(solution)/shard_map/ppermute | solution.py:279
  340.2 3.1 collective-permute-start.20
  340.5 28.1 %collective-permute-start.21 = (f32[384,768]{1,0:T(8,128)}, f32[384,768]{1,0:T(8,128)S(1)}, u32[]{:S(2)}, u32[]{:S(2)}) collective-permute-start(f32[384,768]{1,0:T(8,128)} %get-tuple-element.24), channel_id=1, source_target_pairs={{0,3},{1,2},{2,1},{3,0},{4,7},{5,6},{6,5},{7,4},{8,11},{9,10},{10,... | collective-permute-start | bytes 3538952 | tf_op jit(solution)/shard_map/ppermute | solution.py:290

commit v2 on v0

--- a/solution.py
+++ b/solution.py
@@ -1,9 +1,381 @@
+import functools
+
 import jax
 import jax.numpy as jnp
+import numpy as np
 from jax import lax
+from jax.experimental import pallas as pl
+from jax.experimental.pallas import tpu as pltpu
 from jax.sharding import PartitionSpec as P
 
 HIGH = lax.Precision.HIGHEST
+F32, BF16 = jnp.float32, jnp.bfloat16
+VMEM_LIMIT = 60 << 20
+TILE = 256
+
+
+def halves(x):
+    high = x.astype(BF16)
+    return high, (x - high.astype(F32)).astype(BF16)
+
+
+def dot(a, b):
+    return lax.dot_general(a, b, (((1,), (0,)), ((), ())), preferred_element_type=F32)
+
+
+def dot_t(a, b):
+    return lax.dot_general(a, b, (((1,), (1,)), ((), ())), preferred_element_type=F32)
+
+
+def dot3(a_high, a_low, b_high, b_low):
+    return dot(a_high, b_high) + dot(a_low, b_high) + dot(a_high, b_low)
+
+
+def split_kernel(v_ref, high_ref, low_ref):
+    high_ref[...], low_ref[...] = halves(v_ref[...])
+
+
+def split(v):
+    rows, cols = v.shape
+    spec = pl.BlockSpec((rows // 4, cols), lambda i: (i, 0))
+    return pl.pallas_call(
+        split_kernel,
+        grid=(4,),
+        in_specs=[spec],
+        out_specs=[spec] * 2,
+        out_shape=[jax.ShapeDtypeStruct((rows, cols), BF16)] * 2,
+        compiler_params=pltpu.CompilerParams(vmem_limit_bytes=VMEM_LIMIT),
+        name="split_coulomb",
+    )(v)
+
+
+def green_kernel(merged, first, last, meta, coef, *refs):
+    refs = list(refs)
+    sources = [refs.pop(0) for _ in range(merged or 1)]
+    factor = refs.pop(0)
+    acc_in = None if first else refs.pop(0)
+    occ_in = refs.pop(0) if last else None
+    outs = [refs.pop(0) for _ in range(coef.shape[0] if last else 1)]
+    c_buf, left, right, sem = refs
+    step = pl.program_id(0)
+    width = c_buf.shape[1]
+    times = factor.shape[0]
+    strip = left.shape[0] // times
+    size = c_buf.shape[0] // 3
+
+    @pl.when(step == 0)
+    def _():
+        copies = []
+        for k, source in enumerate(sources):
+            for s in range(3):
+                if merged:
+                    rows, part = source.shape[1:]
+                    start = pl.multiple_of(meta[k % 2], 16) + s * size
+                    here = c_buf.at[pl.ds(start, rows), pl.ds(k // 2 * part, part)]
+                    copies.append(pltpu.make_async_copy(source.at[s], here, sem))
+                else:
+                    start = pl.multiple_of(meta[2 + s], 16)
+                    here = c_buf.at[pl.ds(s * size, size), :]
+                    copies.append(pltpu.make_async_copy(source.at[pl.ds(start, size), :], here, sem))
+        for copy in copies:
+            copy.start()
+        for copy in copies:
+            copy.wait()
+        high, low = halves(c_buf[...])
+        right[:, :width] = high
+        right[:, width : 2 * width] = high
+        right[:, 2 * width :] = low
+
+    c = c_buf[pl.ds(pl.multiple_of(meta[5 + step], 16), strip), :]
+    for t in range(times):
+        high, low = halves(c * factor[t : t + 1, :])
+        s = slice(t * strip, (t + 1) * strip)
+        left[s, :width] = high
+        left[s, width : 2 * width] = low
+        left[s, 2 * width :] = high
+
+    row = pl.multiple_of(meta[10 + step], 128)
+    green = dot_t(left[...], right[pl.ds(row, size), :])
+    green = green.reshape(1, times, strip, size)
+    if not first:
+        green = green + acc_in[...]
+    if not last:
+        outs[0][...] = green
+    else:
+        pairs = [occ_in[0, t] * green[0, t] for t in range(times)]
+        for n, out in enumerate(outs):
+            total = coef[n, 0] * pairs[0]
+            for t in range(1, times):
+                total = total + coef[n, t] * pairs[t]
+            out[0] = total
+
+
+def green_call(name, sources, factor, meta, coef, size, acc=None, occ=None):
+    times, width = factor.shape
+    strip = size // 4
+    first, last = acc is None, occ is not None
+    merged = len(sources) if len(sources) > 1 else 0
+    acc_spec = pl.BlockSpec((1, times, strip, size), lambda n, *_: (n, 0, 0, 0))
+    part_spec = pl.BlockSpec((1, strip, size), lambda n, *_: (n, 0, 0))
+    args = list(sources) + [factor]
+    specs = [pl.BlockSpec(memory_space=pl.ANY)] * len(sources)
+    specs += [pl.BlockSpec((times, width), lambda n, *_: (0, 0))]
+    aliases = {}
+    if not first:
+        if not last:
+            aliases = {2 + len(args): 0}
+        args.append(acc)
+        specs.append(acc_spec)
+    if last:
+        args.append(occ)
+        specs.append(acc_spec)
+        out_shape = [jax.ShapeDtypeStruct((5, strip, size), F32)] * coef.shape[0]
+        out_specs = [part_spec] * coef.shape[0]
+    else:
+        out_shape = jax.ShapeDtypeStruct((5, times, strip, size), F32)
+        out_specs = acc_spec
+    return pl.pallas_call(
+        functools.partial(green_kernel, merged, first, last),
+        grid_spec=pltpu.PrefetchScalarGridSpec(
+            num_scalar_prefetch=2,
+            grid=(5,),
+            in_specs=specs,
+            out_specs=out_specs,
+            scratch_shapes=[
+                pltpu.VMEM((3 * size, width), F32),
+                pltpu.VMEM((times * strip, 3 * width), BF16),
+                pltpu.VMEM((3 * size, 3 * width), BF16),
+                pltpu.SemaphoreType.DMA,
+            ],
+        ),
+        out_shape=out_shape,
+        input_output_aliases=aliases,
+        compiler_params=pltpu.CompilerParams(vmem_limit_bytes=VMEM_LIMIT),
+        cost_estimate=pl.CostEstimate(
+            flops=6 * 5 * times * strip * size * width, bytes_accessed=12 << 20, transcendentals=0
+        ),
+        name=name,
+    )(meta, coef, *args)
+
+
+def chain_kernel(block, *refs):
+    at, spots = refs[:2]
+    parts, (v_high, v_low, near_ref, far_ref) = refs[2:10], refs[10:14]
+    vh, vl, pf, ph, plo, rh, rl, xf, xh, xl, sem_p, sem_v, sem_r = refs[14:]
+    n = vh.shape[0]
+    m = rh.shape[0]
+    half = far_ref.shape[1]
+    count, strip, size = parts[0].shape
+    row = pl.multiple_of(at[0], 16)
+    row_copies = [
+        pltpu.make_async_copy(v_high.at[pl.ds(row, m), :], rh, sem_r.at[0]),
+        pltpu.make_async_copy(v_low.at[pl.ds(row, m), :], rl, sem_r.at[1]),
+    ]
+    p_copies = []
+    for k, part in enumerate(parts):
+        for t in range(count):
+            i = pl.multiple_of(spots[2 * (k * count + t)], 16)
+            j = pl.multiple_of(spots[2 * (k * count + t) + 1], 128)
+            there = pf.at[pl.ds(i, strip), pl.ds(j, size)]
+            p_copies.append(pltpu.make_async_copy(part.at[t], there, sem_p))
+    v_copies = []
+    for b in range(n // block):
+        cols = pl.ds(b * block, block)
+        v_copies.append(
+            [
+                pltpu.make_async_copy(v_high.at[:, cols], vh.at[:, cols], sem_v.at[0, b]),
+                pltpu.make_async_copy(v_low.at[:, cols], vl.at[:, cols], sem_v.at[1, b]),
+            ]
+        )
+    for copy in p_copies + row_copies:
+        copy.start()
+    for copy in p_copies + row_copies:
+        copy.wait()
+    for pair in v_copies:
+        for copy in pair:
+            copy.start()
+    for b in range(n // block):
+        s = slice(b * block, (b + 1) * block)
+        for g in range(size, n, size):
+            if s.start < g < s.stop:
+                pf[g : s.stop, s.start : g] = pf[s.start : g, g : s.stop].T
+        ph[: s.stop, s], plo[: s.stop, s] = halves(pf[: s.stop, s])
+
+    def times_p(high, low, b):
+        s = slice(b * block, (b + 1) * block)
+        r = dot3(high[:, : s.stop], low[:, : s.stop], ph[: s.stop, s], plo[: s.stop, s])
+        if s.stop < n:
+            h, lo = high[:, s.stop :], low[:, s.stop :]
+            ph_t, pl_t = ph[s, s.stop :], plo[s, s.stop :]
+            r = r + dot_t(h, ph_t) + dot_t(lo, ph_t) + dot_t(h, pl_t)
+        return r
+
+    high, low = rh[...], rl[...]
+    for b in range(n // block):
+        s = slice(b * block, (b + 1) * block)
+        r = times_p(high, low, b)
+        xf[:, s] = r
+        xh[:, s], xl[:, s] = halves(r)
+    high, low = xh[...], xl[...]
+    for b in range(n // block):
+        for copy in v_copies[b]:
+            copy.wait()
+        s = slice(b * block, (b + 1) * block)
+        rh[:, s], rl[:, s] = halves(dot3(high, low, vh[:, s], vl[:, s]))
+    high, low = rh[...], rl[...]
+    for b in range(n // block):
+        s = slice(b * block, (b + 1) * block)
+        xh[:, s], xl[:, s] = halves(xf[:, s] + times_p(high, low, b))
+    high, low = xh[...], xl[...]
+    near = pl.multiple_of(at[1] * half, 128)
+    far = pl.multiple_of((1 - at[1]) * half, 128)
+    for start, out in ((far, far_ref), (near, near_ref)):
+        out[...] = dot3(high, low, vh[:, pl.ds(start, half)], vl[:, pl.ds(start, half)])
+
+
+def chain(at, spots, parts, v_high, v_low, rows, cols):
+    n = v_high.shape[0]
+    block = 2 * TILE
+    big = pltpu.VMEM((n, n), BF16)
+    strip = pltpu.VMEM((rows, n), BF16)
+    smem, hbm = pl.BlockSpec(memory_space=pltpu.SMEM), pl.BlockSpec(memory_space=pl.ANY)
+    scratch = [big, big, pltpu.VMEM((n, n), F32), big, big, strip, strip]
+    scratch += [pltpu.VMEM((rows, n), F32), strip, strip]
+    scratch += [pltpu.SemaphoreType.DMA, pltpu.SemaphoreType.DMA((2, n // block))]
+    scratch += [pltpu.SemaphoreType.DMA((2,))]
+    return pl.pallas_call(
+        functools.partial(chain_kernel, block),
+        in_specs=[smem] * 2 + [hbm] * (len(parts) + 2),
+        out_specs=[pl.BlockSpec(memory_space=pltpu.VMEM)] * 2,
+        out_shape=[jax.ShapeDtypeStruct((rows, cols), F32)] * 2,
+        scratch_shapes=scratch,
+        compiler_params=pltpu.CompilerParams(vmem_limit_bytes=VMEM_LIMIT),
+        cost_estimate=pl.CostEstimate(
+            flops=24 * rows * n * n, bytes_accessed=20 << 20, transcendentals=0
+        ),
+        name="chain",
+    )(at, spots, *parts, v_high, v_low)
+
+
+def move(v, where):
+    cols = lax.axis_size("col")
+    pairs = []
+    for r in range(lax.axis_size("row")):
+        for c in range(cols):
+            x, y, core = where(c, r // 2, r % 2)
+            pairs.append((r * cols + c, (2 * y + core) * cols + x))
+    return lax.ppermute(v, ("row", "col"), pairs)
+
+
+def over(v, dx, dy, dc):
+    return move(v, lambda x, y, c: (x ^ dx, y ^ dy, c ^ dc))
+
+
+def ring(v, steps=1):
+    size = lax.axis_size("tm")
+    return lax.ppermute(v, "tm", [(i, (i + steps) % size) for i in range(size)])
+
+
+def after(v, *others):
+    return lax.optimization_barrier((v,) + others)[0]
+
+
+def tables_of(size):
+    strip = size // 4
+    devices = [(x, y, c) for y in range(2) for c in range(2) for x in range(2)]
+
+    def strips(x, y, c):
+        return [2 * c, 2 * c + 1, 2 * x + c, 2 * y + c, 2 * x + c]
+
+    def spots(x, y, c):
+        cross = y ^ (1 - x)
+        left = [2 * x + y, 2 * x + y, y, 2 * x, cross]
+        right = [2 * x + y, 2 * x + y, 2 + y, 2 * x + 1, 3 - cross]
+        return [(a * size + t * strip, b * size) for a, b, t in zip(left, right, strips(x, y, c))]
+
+    meta, places = [], []
+    for x, y, c in devices:
+        sets = [2 * x + y, 2 * (1 - x) + y, 2 * x + 1 - y]
+        left, right = [0, 0, x, 2 * y, 2 - x], [0, 0, 1 - x, 2 - 2 * y, 1 + x]
+        meta.append(
+            [c * 2 * strip, (1 - c) * 2 * strip]
+            + [s * size for s in sets]
+            + [s * size + t * strip for s, t in zip(left, strips(x, y, c))]
+            + [s * size for s in right]
+        )
+        places.append(
+            [spots(x ^ dx, y ^ dy, c ^ dc) for dc in range(2) for dx in range(2) for dy in range(2)]
+        )
+    flat = np.array(places, np.int32).reshape(len(devices), -1)
+    return np.array(meta, np.int32), flat
+
+
+def on_plane(c_occ, c_vir, eps_occ, eps_vir, tau, tweight, omega, coulomb):
+    grid = coulomb.shape[0]
+    planes = lax.axis_size("tm")
+    rows_n, cols_n = lax.axis_size("row"), lax.axis_size("col")
+    z, r, x = lax.axis_index("tm"), lax.axis_index("row"), lax.axis_index("col")
+    y, core = r // 2, r % 2
+    tile_rows, tile_cols = grid // rows_n, grid // cols_n
+    size = grid // 4
+    strip = size // 4
+    ways = [(dx, dy) for dx in range(2) for dy in range(2)]
+    here = (2 * y + core) * cols_n + x
+    meta, spots = (jnp.array(t)[here] for t in tables_of(size))
+
+    energies = jnp.stack([eps_occ, -eps_vir])
+    arriving = jnp.concatenate([ring(energies, t) for t in range(1, planes)], axis=1)
+
+    def factor(e):
+        return jnp.exp(e[None, :] * tau[:, None])
+
+    gamma = tweight[None, :] * jnp.cos(omega[:, None] * tau[None, :])
+    per_plane = omega.shape[0] // planes
+    coef = -2.0 * jnp.stack(
+        [gamma[z * per_plane + 2 * (x ^ dx) + (y ^ dy)] for dx, dy in ways]
+    )
+
+    start = (2 * x + y) * size + core * 2 * strip
+    common = (meta, coef, size)
+    own = [None, None]
+    sources = [[], []]
+    piece = None
+    v_high = v_low = None
+    for s, c in enumerate((c_occ, c_vir)):
+        before = piece
+        piece = lax.dynamic_slice_in_dim(c, start, 2 * strip, 0)
+        if before is not None:
+            piece = after(piece, before, own[1])
+        for t in range(1, planes):
+            arrived = piece = ring(piece)
+            if s == 0 and t == 1:
+                v_high, v_low = split(coulomb)
+                piece = after(piece, v_high)
+            elif s == 0 and t < 4:
+                args = (("green_occ_own", c_occ), ("green_vir_own", c_vir))[t - 2]
+                own[t - 2] = green_call(
+                    args[0], [after(args[1], arrived)], factor(energies[t - 2]), *common
+                )
+                piece = after(piece, own[t - 2])
+            sets = jnp.stack([arrived, over(arrived, 1, 0, 0), over(arrived, 0, 1, 0)])
+            sources[s] += [sets, over(sets, 0, 0, 1)]
+    occ = green_call("green_occ", sources[0], factor(arriving[0]), *common, own[0])
+    parts = green_call("green_vir", sources[1], factor(arriving[1]), *common, own[1], occ)
+
+    parts = [over(p, dx, dy, 0) if dx + dy else p for p, (dx, dy) in zip(parts, ways)]
+    parts += [over(p, 0, 0, 1) for p in parts]
+
+    arrivals = []
+    for e in range(2):
+        at = jnp.stack([(2 * core + (y ^ e)) * tile_rows, x]).astype(jnp.int32)
+        near, far = chain(at, spots, parts, v_high, v_low, tile_rows, tile_cols)
+        for dx, value in ((1, far), (0, near)):
+            value = move(value, lambda x, y, c, dx=dx, e=e: (x ^ dx, c, y ^ e))
+            arrivals.append((2 * (x ^ dx) + (core ^ e), value))
+    out = jnp.zeros((per_plane, tile_rows, tile_cols), F32)
+    for k, value in arrivals:
+        out = lax.dynamic_update_slice(out, value[None], (k, 0, 0))
+    return out
 
 
 def green_block(rows_c, cols_c, energies, taus, sign):
@@ -13,7 +385,7 @@
     lead = (rows_c.shape[0], taus.shape[0])
     flat = scaled.reshape(lead[0] * lead[1], width)
     product = lax.dot_general(
-        flat, cols_c, (((1,), (1,)), ((), ())), precision=HIGH, preferred_element_type=jnp.float32
+        flat, cols_c, (((1,), (1,)), ((), ())), precision=HIGH, preferred_element_type=F32
     )
     return product.reshape(lead[0], lead[1], cols_c.shape[0])
 
@@ -40,23 +412,29 @@
     coulomb_rows = lax.dynamic_slice_in_dim(coulomb, row_start, tile_rows, 0)
     coulomb_cols = lax.dynamic_slice_in_dim(coulomb, col_start, tile_cols, 1)
     coulomb_tile = lax.dynamic_slice_in_dim(coulomb_rows, col_start, tile_cols, 1)
-    left = coulomb_rows
     coupled = jnp.einsum(
-        "ik,fkj->fij", left, lax.all_gather(polar, "row", axis=1, tiled=True), precision=HIGH
+        "ik,fkj->fij", coulomb_rows, lax.all_gather(polar, "row", axis=1, tiled=True), precision=HIGH
     )
     coupled_rows = lax.all_gather(coupled, "col", axis=2, tiled=True)
     first = coulomb_tile[None] + jnp.einsum(
         "fik,kj->fij", coupled_rows, coulomb_cols, precision=HIGH
     )
-    left = coupled_rows
     return jnp.einsum(
-        "fik,fkj->fij", left, lax.all_gather(first, "row", axis=1, tiled=True), precision=HIGH
+        "fik,fkj->fij", coupled_rows, lax.all_gather(first, "row", axis=1, tiled=True), precision=HIGH
     )
 
 
 def solution(mesh):
     in_specs = (P(None, "tm"), P(None, "tm"), P("tm"), P("tm"), P(), P(), P(), P())
     out_specs = P("tm", "row", "col")
+    square = mesh.shape["row"] == 4 and mesh.shape["col"] == 2
+
+    def body(*args):
+        omega, coulomb = args[6], args[7]
+        fits = omega.shape[0] == 2 * mesh.shape["tm"] * mesh.shape["col"]
+        fits = fits and coulomb.shape[0] % (6 * TILE) == 0 and args[0].shape[1] % 128 == 0
+        return (on_plane if square and fits else on_device)(*args)
+
     return jax.shard_map(
-        on_device, mesh=mesh, in_specs=in_specs, out_specs=out_specs, check_vma=False
-    )
+        body, mesh=mesh, in_specs=in_specs, out_specs=out_specs, check_vma=False
+    )

time: 788 us -> 283 us (0.36)
  waiting for transfers between devices: 509 us -> 107 us
  Pallas kernels: 0 us -> 127 us
  matrix products: 114 us -> 0 us
  blocking collectives: 109 us -> 0 us
  starting transfers between devices: 9.43 us -> 28 us
  between operations: 13.4 us -> 0.58 us
    all_gather x3 -> x0, waiting for transfers between devices: 345 us -> none  [the longest x1 119 us: on_device(): lax.all_gather(first, 'row', axis=1, tiled=True)]
    reduce_scatter x1 -> x0, waiting for transfers between devices: 164 us -> none  [on_device(): lax.psum_scatter(jnp.stack([green_occ, green_vir], axis=1), 'tm', scatter...]
    pallas_call x0 -> x7, Pallas kernels: none -> 127 us  [the longest x2 74.4 us: chain(): pl.pallas_call(functools.partial(chain_kernel, block), in_specs=[smem] *...]
    dot_general x6 -> x0, matrix products: 114 us -> none  [the longest x1 34.8 us: on_device(): jnp.einsum('ik,fkj->fij', left, lax.all_gather(polar, 'row', axis=1, tile...]
    all_to_all x1 -> x0, blocking collectives: 109 us -> none  [on_device(): lax.all_to_all(polar_all, 'tm', split_axis=0, concat_axis=1, tiled=True)]
    ppermute x0 -> x38, waiting for transfers between devices: none -> 107 us  [the longest x29 74.3 us: move(): return lax.ppermute(v, ('row', 'col'), pairs)]
    ppermute x0 -> x38, starting transfers between devices: none -> 28 us  [the longest x29 22.8 us: move(): return lax.ppermute(v, ('row', 'col'), pairs)]
    all_gather x3 -> x0, starting transfers between devices: 9.43 us -> none  [the longest x1 9.34 us: on_device(): coupled_rows = lax.all_gather(coupled, 'col', axis=2, tiled=True)]
  transfers between devices with their start and end apart: 4 -> 38, of which waited for: 4 -> 18; matrix products, arithmetic and copies ran while one was open for 0% -> 4% of each run, Pallas kernels for 0% -> 22%
where the time goes in v2:
time: 283 us; the launch traced here: 280 us
  Pallas kernels  127 us (45%)
  waiting for transfers between devices  107 us (38%)
  starting transfers between devices  28 us (10%)
  local copies, waits for them, and re-layouts  11.9 us (4%)
  other arithmetic  5.72 us (2%)
    pallas_call x2, Pallas kernels, chain(): pl.pallas_call(functools.partial(chain_kernel, block), in_specs=[smem] *...  74.4 us
    ppermute x29, waiting for transfers between devices, move(): return lax.ppermute(v, ('row', 'col'), pairs)  74.3 us
    pallas_call x4, Pallas kernels, green_call(): pl.pallas_call(functools.partial(green_kernel, merged, first, last), grid...  45.1 us
    ppermute x9, waiting for transfers between devices, ring(): return lax.ppermute(v, 'tm', [(i, (i + steps) % size) for i in range(size)])  32.3 us
    ppermute x29, starting transfers between devices, move(): return lax.ppermute(v, ('row', 'col'), pairs)  22.8 us
    pallas_call x1, Pallas kernels, split(): pl.pallas_call(split_kernel, grid=(4,), in_specs=[spec], out_specs=[spec]...  7.92 us
  transfers between devices with their start and end apart: 38, of which 18 were waited for; matrix products, arithmetic and copies ran while one was open for 4% of the time, Pallas kernels for 22%

profile of v2, /device:TPU:0, one launch (start us, length us, event | category | flops | bytes accessed | tf_op | source)
XLA Modules:
  0.0 280.3 jit_solution(4969211661185005562)
XLA Ops:
  0.0 1.0 constant_dynamic-slice_fusion
  1.0 3.1 %collective-permute-start = (f32[192,384]{1,0:T(8,128)S(1)}, f32[192,384]{1,0:T(8,128)S(1)}, u32[]{:S(2)}, u32[]{:S(2)}) collective-permute-start(f32[192,384]{1,0:T(8,128)S(1)} %constant_dynamic-slice_fusion), channel_id=1, source_target_pairs={{0,8},{8,16},{16,24},{24,0},{1,9},{9,17},{17,25},{25,1},{2,10},{10... | collective-permute-start | bytes 884744 | tf_op jit(solution)/shard_map/ppermute | solution.py:276
  4.1 0.8 cosine_multiply_fusion
  4.9 7.9 %split_coulomb.1 = (bf16[1536,1536]{1,0:T(8,128)(2,1)}, bf16[1536,1536]{1,0:T(8,128)(2,1)}) custom-call(f32[1536,1536]{1,0:T(8,128)} %v_ref.1), custom_call_target="tpu_custom_call" | custom-call | tf_op jit(solution)/shard_map/split_coulomb/pallas_call | solution.py:41
  12.9 0.6 maximum_multiply_fusion.coef
  13.5 1.6 collective-permute-start.1
  15.0 1.3 fusion.1.meta
  16.3 0.7 multiply_exponential_fusion.2
  17.0 6.7 %collective-permute-done.1 = f32[192,384]{1,0:T(8,128)S(1)} collective-permute-done((f32[192,384]{1,0:T(8,128)S(1)}, f32[192,384]{1,0:T(8,128)S(1)}, u32[]{:S(2)}, u32[]{:S(2)}) %collective-permute-start.1) | collective-permute-done | bytes 294944 | tf_op jit(solution)/shard_map/ppermute | solution.py:276
  23.7 7.7 %green_occ_own.1.refs_7_ = f32[5,4,96,384]{3,2,1,0:T(8,128)} custom-call(s32[15]{0:T(128)} %fusion.1.meta, f32[4,4]{1,0:T(4,128)} %maximum_multiply_fusion.coef, f32[1536,384]{1,0:T(8,128)} %refs_0_, f32[4,384]{1,0:T(4,128)} %get-tuple-element.44.refs_1_), custom_call_target="tpu_custom_call" | custom-call | flops 1698693120 | bytes 12582912 | tf_op jit(solution)/shard_map/green_occ_own/pallas_call | solution.py:137
  31.5 1.0 constant_dynamic-slice_fusion.1
  32.5 1.6 collective-permute-start.18
  34.0 1.5 collective-permute-start.19
  35.6 5.3 %collective-permute-done.2 = f32[192,384]{1,0:T(8,128)S(1)} collective-permute-done((f32[192,384]{1,0:T(8,128)S(1)}, f32[192,384]{1,0:T(8,128)S(1)}, u32[]{:S(2)}, u32[]{:S(2)}) %collective-permute-start.2) | collective-permute-done | bytes 294944 | tf_op jit(solution)/shard_map/ppermute | solution.py:276
  40.8 7.7 %green_vir_own.1.refs_7_ = f32[5,4,96,384]{3,2,1,0:T(8,128)} custom-call(s32[15]{0:T(128)} %fusion.1.meta, f32[4,4]{1,0:T(4,128)} %maximum_multiply_fusion.coef, f32[1536,384]{1,0:T(8,128)} %refs_0_.1, f32[4,384]{1,0:T(4,128)} %get-tuple-element.43.refs_1_), custom_call_target="tpu_custom_call" | custom-call | flops 1698693120 | bytes 12582912 | tf_op jit(solution)/shard_map/green_vir_own/pallas_call | solution.py:137
  48.6 1.5 collective-permute-start.21
  50.3 6.9 %collective-permute-done.15 = f32[2,384]{1,0:T(2,128)S(1)} collective-permute-done((f32[2,384]{1,0:T(2,128)S(1)}, f32[2,384]{1,0:T(2,128)S(1)}, u32[]{:S(2)}, u32[]{:S(2)}) %collective-permute-start.15) | collective-permute-done | bytes 3104 | tf_op jit(solution)/shard_map/ppermute | solution.py:276
  57.2 4.5 %collective-permute-done.16 = f32[2,384]{1,0:T(2,128)S(1)} collective-permute-done((f32[2,384]{1,0:T(2,128)S(1)}, f32[2,384]{1,0:T(2,128)S(1)}, u32[]{:S(2)}, u32[]{:S(2)}) %collective-permute-start.16) | collective-permute-done | bytes 3104 | tf_op jit(solution)/shard_map/ppermute | solution.py:276
  61.7 0.4 collective-permute-start.17
  62.1 3.2 %collective-permute-done.17 = f32[2,384]{1,0:T(2,128)S(1)} collective-permute-done((f32[2,384]{1,0:T(2,128)S(1)}, f32[2,384]{1,0:T(2,128)S(1)}, u32[]{:S(2)}, u32[]{:S(2)}) %collective-permute-start.17) | collective-permute-done | bytes 3104 | tf_op jit(solution)/shard_map/ppermute | solution.py:276
  65.3 1.5 collective-permute-start.22
  66.8 1.5 collective-permute-start.24
  68.3 0.5 collective-permute-start.25
  68.8 0.6 collective-permute-start.4
  69.5 2.5 collective-permute-done.22
  72.0 1.5 collective-permute-done.24
  73.5 0.5 collective-permute-start.5
  74.1 3.3 %collective-permute-done.7 = f32[192,384]{1,0:T(8,128)S(1)} collective-permute-done((f32[192,384]{1,0:T(8,128)S(1)}, f32[192,384]{1,0:T(8,128)S(1)}, u32[]{:S(2)}, u32[]{:S(2)}) %collective-permute-start.7) | collective-permute-done | bytes 294944 | tf_op jit(solution)/shard_map/ppermute | solution.py:276
  77.4 0.5 collective-permute-start.8
  77.9 1.5 collective-permute-start.9
  79.6 3.9 %collective-permute-done.5 = f32[192,384]{1,0:T(8,128)S(1)} collective-permute-done((f32[192,384]{1,0:T(8,128)S(1)}, f32[192,384]{1,0:T(8,128)S(1)}, u32[]{:S(2)}, u32[]{:S(2)}) %collective-permute-start.5) | collective-permute-done | bytes 294944 | tf_op jit(solution)/shard_map/ppermute | solution.py:267
  83.5 2.4 collective-permute-done.11
  85.9 0.5 collective-permute-start.12
  86.4 1.4 collective-permute-done.9
  87.8 1.5 collective-permute-start.13
  89.5 1.1 pad_maximum_fusion.1.refs_2_
  90.5 4.8 %collective-permute-done.12 = f32[192,384]{1,0:T(8,128)S(1)} collective-permute-done((f32[192,384]{1,0:T(8,128)S(1)}, f32[192,384]{1,0:T(8,128)S(1)}, u32[]{:S(2)}, u32[]{:S(2)}) %collective-permute-start.12) | collective-permute-done | bytes 294944 | tf_op jit(solution)/shard_map/ppermute | solution.py:267
  95.3 0.4 collective-permute-done.13
  95.8 1.0 pad_maximum_fusion.2.refs_4_
  96.8 0.5 collective-permute-start.14
  97.3 0.7 multiply_exponential_fusion
  98.0 0.9 copy-done.9
  98.9 0.9 copy-done.10
  99.8 14.2 %green_occ.1.refs_8_ = f32[5,4,96,384]{3,2,1,0:T(8,128)} custom-call(s32[15]{0:T(128)} %fusion.1.meta, f32[4,4]{1,0:T(4,128)} %maximum_multiply_fusion.coef, f32[3,192,384]{2,1,0:T(8,128)} %copy-done.1, f32[3,192,384]{2,1,0:T(8,128)} %copy-done.8, f32[3,192,384]{2,1,0:T(8,128)} %copy-done.2, ...), custom_call_target="tpu_custom_call", output_to_operand_aliasing={{}: (9, {})} | custom-call | flops 5096079360 | bytes 12582912 | tf_op jit(solution)/shard_map/green_occ/pallas_call | solution.py:137
  114.1 15.4 %green_vir.1 = (f32[5,96,384]{2,1,0:T(8,128)}, f32[5,96,384]{2,1,0:T(8,128)}, f32[5,96,384]{2,1,0:T(8,128)}, f32[5,96,384]{2,1,0:T(8,128)}) custom-call(s32[15]{0:T(128)} %fusion.1.meta, f32[4,4]{1,0:T(4,128)} %maximum_multiply_fusion.coef, f32[3,192,384]{2,1,0:T(8,128)} %copy-done.4, f32[3,192,384]{2,1,0:T(8,128)} %collective-permute-done.6.refs_1_, ...), custom_call_target="tpu_custom_call" | custom-call | flops 5096079360 | bytes 12582912 | tf_op jit(solution)/shard_map/green_vir/pallas_call | solution.py:137
  129.6 1.8 collective-permute-start.27
  131.4 1.5 collective-permute-start.28
  133.1 15.3 %collective-permute-done.27.refs_3_ = f32[5,96,384]{2,1,0:T(8,128)S(1)} collective-permute-done((f32[5,96,384]{2,1,0:T(8,128)}, f32[5,96,384]{2,1,0:T(8,128)S(1)}, u32[]{:S(2)}, u32[]{:S(2)}) %collective-permute-start.27) | collective-permute-done | bytes 737312 | tf_op jit(solution)/shard_map/ppermute | solution.py:267
  148.4 2.5 collective-permute-done.28.refs_4_
  150.9 14.5 %collective-permute-done.29.refs_5_ = f32[5,96,384]{2,1,0:T(8,128)S(1)} collective-permute-done((f32[5,96,384]{2,1,0:T(8,128)}, f32[5,96,384]{2,1,0:T(8,128)S(1)}, u32[]{:S(2)}, u32[]{:S(2)}) %collective-permute-start.29) | collective-permute-done | bytes 737312 | tf_op jit(solution)/shard_map/ppermute | solution.py:267
  165.5 1.2 fusion.refs_1_
  166.7 0.6 pad_add_fusion
  167.4 0.5 collective-permute-done.33.refs_9_
  167.8 0.4 copy-done.14
  168.2 42.5 %chain.2 = (f32[384,768]{1,0:T(8,128)}, f32[384,768]{1,0:T(8,128)}) custom-call(s32[2]{0:T(128)} %get-tuple-element.45.refs_0_, s32[80]{0:T(128)} %fusion.refs_1_, f32[5,96,384]{2,1,0:T(8,128)} %get-tuple-element.26.refs_2_, f32[5,96,384]{2,1,0:T(8,128)} %copy-done.11, f32[5,96,384]{2,1,0:T(8,128)} %copy-done.12, f32[5,96,384]{2,1,0:T(8,128)} %copy-done.13, ...), custom_call_target="tpu_custom_call" | custom-call | flops 21743271936 | bytes 20971520 | tf_op jit(solution)/shard_map/chain/pallas_call | solution.py:246
  210.8 1.5 collective-permute-start.34
  212.3 1.9 collective-permute-start.35
  214.2 31.9 %chain.3 = (f32[384,768]{1,0:T(8,128)}, f32[384,768]{1,0:T(8,128)}) custom-call(s32[2]{0:T(128)} %get-tuple-element.46.refs_0_, s32[80]{0:T(128)} %fusion.refs_1_, f32[5,96,384]{2,1,0:T(8,128)} %get-tuple-element.26.refs_2_, f32[5,96,384]{2,1,0:T(8,128)} %copy-done.11, f32[5,96,384]{2,1,0:T(8,128)} %copy-done.12, f32[5,96,384]{2,1,0:T(8,128)} %copy-done.13, ...), custom_call_target="tpu_custom_call" | custom-call | flops 21743271936 | bytes 20971520 | tf_op jit(solution)/shard_map/chain/pallas_call | solution.py:246
  246.1 1.9 collective-permute-start.36
  247.9 0.4 broadcast_in_dim.10
  248.5 26.9 %collective-permute-done.36 = f32[384,768]{1,0:T(8,128)} collective-permute-done((f32[384,768]{1,0:T(8,128)}, f32[384,768]{1,0:T(8,128)}, u32[]{:S(2)}, u32[]{:S(2)}) %collective-permute-start.36) | collective-permute-done | bytes 1179680 | tf_op jit(solution)/shard_map/ppermute | solution.py:267
  275.4 1.3 bitcast_dynamic-update-slice_fusion.1
  276.8 2.2 copy-done
  279.0 1.1 bitcast_dynamic-update-slice_fusion
  (78 shorter events, 1.2 us)
Async XLA Ops:
  1.0 12.5 %collective-permute-start = (f32[192,384]{1,0:T(8,128)S(1)}, f32[192,384]{1,0:T(8,128)S(1)}, u32[]{:S(2)}, u32[]{:S(2)}) collective-permute-start(f32[192,384]{1,0:T(8,128)S(1)} %constant_dynamic-slice_fusion), channel_id=1, source_target_pairs={{0,8},{8,16},{16,24},{24,0},{1,9},{9,17},{17,25},{25,1},{2,10},{10... | collective-permute-start | bytes 884744 | tf_op jit(solution)/shard_map/ppermute | solution.py:276
  4.9 8.0 %copy-start.7 = (f32[384]{0:T(512)S(1)}, f32[384]{0:T(512)}, u32[]{:S(2)}) copy-start(f32[384]{0:T(512)} %param.13) | copy-start | bytes 4612
  4.9 11.4 %copy-start.5 = (f32[384]{0:T(512)S(1)}, f32[384]{0:T(512)}, u32[]{:S(2)}) copy-start(f32[384]{0:T(512)} %param.12) | copy-start | bytes 4612
  4.9 11.4 %copy-start.6 = (f32[4]{0:T(128)S(1)}, f32[4]{0:T(128)}, u32[]{:S(2)}) copy-start(f32[4]{0:T(128)} %param.14) | copy-start | bytes 52
  13.5 10.3 %collective-permute-start.1 = (f32[192,384]{1,0:T(8,128)S(1)}, f32[192,384]{1,0:T(8,128)S(1)}, u32[]{:S(2)}, u32[]{:S(2)}) collective-permute-start(f32[192,384]{1,0:T(8,128)S(1)} %collective-permute-done), channel_id=1, source_target_pairs={{0,8},{8,16},{16,24},{24,0},{1,9},{9,17},{17,25},{25,1},{2,10},{10... | collective-permute-start | bytes 884744 | tf_op jit(solution)/shard_map/ppermute | solution.py:276
  31.4 9.4 %collective-permute-start.2 = (f32[192,384]{1,0:T(8,128)S(1)}, f32[192,384]{1,0:T(8,128)S(1)}, u32[]{:S(2)}, u32[]{:S(2)}) collective-permute-start(f32[192,384]{1,0:T(8,128)S(1)} %collective-permute-done.1), channel_id=1, source_target_pairs={{0,8},{8,16},{16,24},{24,0},{1,9},{9,17},{17,25},{25,1},{2,10},{10... | collective-permute-start | bytes 884744 | tf_op jit(solution)/shard_map/ppermute | solution.py:276
  32.5 34.3 %collective-permute-start.18 = (f32[192,384]{1,0:T(8,128)S(1)}, f32[192,384]{1,0:T(8,128)S(1)}, u32[]{:S(2)}, u32[]{:S(2)}) collective-permute-start(f32[192,384]{1,0:T(8,128)S(1)} %collective-permute-done), channel_id=1, source_target_pairs={{0,1},{1,0},{2,3},{3,2},{4,5},{5,4},{6,7},{7,6},{8,9},{9,8},{10,11... | collective-permute-start | bytes 884744 | tf_op jit(solution)/shard_map/ppermute | solution.py:267
  34.0 34.3 %collective-permute-start.19 = (f32[192,384]{1,0:T(8,128)S(1)}, f32[192,384]{1,0:T(8,128)S(1)}, u32[]{:S(2)}, u32[]{:S(2)}) collective-permute-start(f32[192,384]{1,0:T(8,128)S(1)} %collective-permute-done), channel_id=1, source_target_pairs={{0,4},{1,5},{2,6},{3,7},{4,0},{5,1},{6,2},{7,3},{8,12},{9,13},{10,... | collective-permute-start | bytes 884744 | tf_op jit(solution)/shard_map/ppermute | solution.py:267
  48.6 20.3 %collective-permute-start.3 = (f32[192,384]{1,0:T(8,128)S(1)}, f32[192,384]{1,0:T(8,128)S(1)}, u32[]{:S(2)}, u32[]{:S(2)}) collective-permute-start(f32[192,384]{1,0:T(8,128)S(1)} %constant_dynamic-slice_fusion.1), channel_id=1, source_target_pairs={{0,8},{8,16},{16,24},{24,0},{1,9},{9,17},{17,25},{25,1},{2,10},{10... | collective-permute-start | bytes 884744 | tf_op jit(solution)/shard_map/ppermute | solution.py:276
  48.6 20.2 %collective-permute-start.21 = (f32[192,384]{1,0:T(8,128)S(1)}, f32[192,384]{1,0:T(8,128)S(1)}, u32[]{:S(2)}, u32[]{:S(2)}) collective-permute-start(f32[192,384]{1,0:T(8,128)S(1)} %collective-permute-done.1), channel_id=1, source_target_pairs={{0,1},{1,0},{2,3},{3,2},{4,5},{5,4},{6,7},{7,6},{8,9},{9,8},{10,11... | collective-permute-start | bytes 884744 | tf_op jit(solution)/shard_map/ppermute | solution.py:267
  50.2 7.0 %collective-permute-start.15 = (f32[2,384]{1,0:T(2,128)S(1)}, f32[2,384]{1,0:T(2,128)S(1)}, u32[]{:S(2)}, u32[]{:S(2)}) collective-permute-start(f32[2,384]{1,0:T(2,128)S(1)} %pad_maximum_fusion.6), channel_id=1, source_target_pairs={{0,8},{8,16},{16,24},{24,0},{1,9},{9,17},{17,25},{25,1},{2,10},{10... | collective-permute-start | bytes 9224 | tf_op jit(solution)/shard_map/ppermute | solution.py:276
  57.2 4.5 %collective-permute-start.16 = (f32[2,384]{1,0:T(2,128)S(1)}, f32[2,384]{1,0:T(2,128)S(1)}, u32[]{:S(2)}, u32[]{:S(2)}) collective-permute-start(f32[2,384]{1,0:T(2,128)S(1)} %pad_maximum_fusion.6), channel_id=1, source_target_pairs={{0,16},{8,24},{16,0},{24,8},{1,17},{9,25},{17,1},{25,9},{2,18},{10... | collective-permute-start | bytes 9224 | tf_op jit(solution)/shard_map/ppermute | solution.py:276
  61.7 3.6 %collective-permute-start.17 = (f32[2,384]{1,0:T(2,128)S(1)}, f32[2,384]{1,0:T(2,128)S(1)}, u32[]{:S(2)}, u32[]{:S(2)}) collective-permute-start(f32[2,384]{1,0:T(2,128)S(1)} %pad_maximum_fusion.6), channel_id=1, source_target_pairs={{0,24},{8,0},{16,8},{24,16},{1,25},{9,1},{17,9},{25,17},{2,26},{10... | collective-permute-start | bytes 9224 | tf_op jit(solution)/shard_map/ppermute | solution.py:276
  65.3 6.7 %collective-permute-start.22 = (f32[192,384]{1,0:T(8,128)S(1)}, f32[192,384]{1,0:T(8,128)S(1)}, u32[]{:S(2)}, u32[]{:S(2)}) collective-permute-start(f32[192,384]{1,0:T(8,128)S(1)} %collective-permute-done.1), channel_id=1, source_target_pairs={{0,4},{1,5},{2,6},{3,7},{4,0},{5,1},{6,2},{7,3},{8,12},{9,13},{10,... | collective-permute-start | bytes 884744 | tf_op jit(solution)/shard_map/ppermute | solution.py:267
  66.8 6.7 %collective-permute-start.24 = (f32[192,384]{1,0:T(8,128)S(1)}, f32[192,384]{1,0:T(8,128)S(1)}, u32[]{:S(2)}, u32[]{:S(2)}) collective-permute-start(f32[192,384]{1,0:T(8,128)S(1)} %collective-permute-done.2), channel_id=1, source_target_pairs={{0,1},{1,0},{2,3},{3,2},{4,5},{5,4},{6,7},{7,6},{8,9},{9,8},{10,11... | collective-permute-start | bytes 884744 | tf_op jit(solution)/shard_map/ppermute | solution.py:267
  68.3 9.0 %collective-permute-start.25 = (f32[192,384]{1,0:T(8,128)S(1)}, f32[192,384]{1,0:T(8,128)S(1)}, u32[]{:S(2)}, u32[]{:S(2)}) collective-permute-start(f32[192,384]{1,0:T(8,128)S(1)} %collective-permute-done.2), channel_id=1, source_target_pairs={{0,4},{1,5},{2,6},{3,7},{4,0},{5,1},{6,2},{7,3},{8,12},{9,13},{10,... | collective-permute-start | bytes 884744 | tf_op jit(solution)/shard_map/ppermute | solution.py:267
  68.8 8.5 %collective-permute-start.7 = (f32[192,384]{1,0:T(8,128)S(1)}, f32[192,384]{1,0:T(8,128)S(1)}, u32[]{:S(2)}, u32[]{:S(2)}) collective-permute-start(f32[192,384]{1,0:T(8,128)S(1)} %collective-permute-done.3), channel_id=1, source_target_pairs={{0,8},{8,16},{16,24},{24,0},{1,9},{9,17},{17,25},{25,1},{2,10},{10... | collective-permute-start | bytes 884744 | tf_op jit(solution)/shard_map/ppermute | solution.py:276
  68.8 9.1 %collective-permute-start.4 = (f32[192,384]{1,0:T(8,128)S(1)}, f32[192,384]{1,0:T(8,128)S(1)}, u32[]{:S(2)}, u32[]{:S(2)}) collective-permute-start(f32[192,384]{1,0:T(8,128)S(1)} %collective-permute-done.3), channel_id=1, source_target_pairs={{0,1},{1,0},{2,3},{3,2},{4,5},{5,4},{6,7},{7,6},{8,9},{9,8},{10,11... | collective-permute-start | bytes 884744 | tf_op jit(solution)/shard_map/ppermute | solution.py:267
  69.5 21.0 %copy-start.1 = (f32[3,192,384]{2,1,0:T(8,128)}, f32[3,192,384]{2,1,0:T(8,128)S(1)}, u32[]{:S(2)}) copy-start(f32[3,192,384]{2,1,0:T(8,128)S(1)} %pad_maximum_fusion.3.refs_0_) | copy-start | bytes 2654212
  72.0 24.8 %collective-permute-start.20 = (f32[3,192,384]{2,1,0:T(8,128)S(1)}, f32[3,192,384]{2,1,0:T(8,128)S(1)}, u32[]{:S(2)}, u32[]{:S(2)}) collective-permute-start(f32[3,192,384]{2,1,0:T(8,128)S(1)} %pad_maximum_fusion.3.refs_0_), channel_id=1, source_target_pairs={{0,2},{1,3},{2,0},{3,1},{4,6},{5,7},{6,4},{7,5},{8,10},{9,11},{10,... | collective-permute-start | bytes 2654216 | tf_op jit(solution)/shard_map/ppermute | solution.py:267
  73.5 9.9 %collective-permute-start.5 = (f32[192,384]{1,0:T(8,128)S(1)}, f32[192,384]{1,0:T(8,128)S(1)}, u32[]{:S(2)}, u32[]{:S(2)}) collective-permute-start(f32[192,384]{1,0:T(8,128)S(1)} %collective-permute-done.3), channel_id=1, source_target_pairs={{0,4},{1,5},{2,6},{3,7},{4,0},{5,1},{6,2},{7,3},{8,12},{9,13},{10,... | collective-permute-start | bytes 884744 | tf_op jit(solution)/shard_map/ppermute | solution.py:267
  77.3 8.5 %collective-permute-start.11 = (f32[192,384]{1,0:T(8,128)S(1)}, f32[192,384]{1,0:T(8,128)S(1)}, u32[]{:S(2)}, u32[]{:S(2)}) collective-permute-start(f32[192,384]{1,0:T(8,128)S(1)} %collective-permute-done.7), channel_id=1, source_target_pairs={{0,8},{8,16},{16,24},{24,0},{1,9},{9,17},{17,25},{25,1},{2,10},{10... | collective-permute-start | bytes 884744 | tf_op jit(solution)/shard_map/ppermute | solution.py:276
  77.4 8.5 %collective-permute-start.8 = (f32[192,384]{1,0:T(8,128)S(1)}, f32[192,384]{1,0:T(8,128)S(1)}, u32[]{:S(2)}, u32[]{:S(2)}) collective-permute-start(f32[192,384]{1,0:T(8,128)S(1)} %collective-permute-done.7), channel_id=1, source_target_pairs={{0,1},{1,0},{2,3},{3,2},{4,5},{5,4},{6,7},{7,6},{8,9},{9,8},{10,11... | collective-permute-start | bytes 884744 | tf_op jit(solution)/shard_map/ppermute | solution.py:267
  77.9 9.9 %collective-permute-start.9 = (f32[192,384]{1,0:T(8,128)S(1)}, f32[192,384]{1,0:T(8,128)S(1)}, u32[]{:S(2)}, u32[]{:S(2)}) collective-permute-start(f32[192,384]{1,0:T(8,128)S(1)} %collective-permute-done.7), channel_id=1, source_target_pairs={{0,4},{1,5},{2,6},{3,7},{4,0},{5,1},{6,2},{7,3},{8,12},{9,13},{10,... | collective-permute-start | bytes 884744 | tf_op jit(solution)/shard_map/ppermute | solution.py:267
  79.5 17.3 %copy-start.2 = (f32[3,192,384]{2,1,0:T(8,128)}, f32[3,192,384]{2,1,0:T(8,128)S(1)}, u32[]{:S(2)}) copy-start(f32[3,192,384]{2,1,0:T(8,128)S(1)} %pad_maximum_fusion.4.refs_2_) | copy-start | bytes 2654212
  79.6 20.2 %copy-start.3 = (f32[3,192,384]{2,1,0:T(8,128)}, f32[3,192,384]{2,1,0:T(8,128)S(1)}, u32[]{:S(2)}) copy-start(f32[3,192,384]{2,1,0:T(8,128)S(1)} %pad_maximum_fusion.5.refs_4_) | copy-start | bytes 2654212
  83.5 14.5 %collective-permute-start.23 = (f32[3,192,384]{2,1,0:T(8,128)S(1)}, f32[3,192,384]{2,1,0:T(8,128)S(1)}, u32[]{:S(2)}, u32[]{:S(2)}) collective-permute-start(f32[3,192,384]{2,1,0:T(8,128)S(1)} %pad_maximum_fusion.4.refs_2_), channel_id=1, source_target_pairs={{0,2},{1,3},{2,0},{3,1},{4,6},{5,7},{6,4},{7,5},{8,10},{9,11},{10,... | collective-permute-start | bytes 2654216 | tf_op jit(solution)/shard_map/ppermute | solution.py:267
  85.9 12.1 %collective-permute-start.26 = (f32[3,192,384]{2,1,0:T(8,128)S(1)}, f32[3,192,384]{2,1,0:T(8,128)S(1)}, u32[]{:S(2)}, u32[]{:S(2)}) collective-permute-start(f32[3,192,384]{2,1,0:T(8,128)S(1)} %pad_maximum_fusion.5.refs_4_), channel_id=1, source_target_pairs={{0,2},{1,3},{2,0},{3,1},{4,6},{5,7},{6,4},{7,5},{8,10},{9,11},{10,... | collective-permute-start | bytes 2654216 | tf_op jit(solution)/shard_map/ppermute | solution.py:267
  85.9 9.4 %collective-permute-start.12 = (f32[192,384]{1,0:T(8,128)S(1)}, f32[192,384]{1,0:T(8,128)S(1)}, u32[]{:S(2)}, u32[]{:S(2)}) collective-permute-start(f32[192,384]{1,0:T(8,128)S(1)} %collective-permute-done.11), channel_id=1, source_target_pairs={{0,1},{1,0},{2,3},{3,2},{4,5},{5,4},{6,7},{7,6},{8,9},{9,8},{10,11... | collective-permute-start | bytes 884744 | tf_op jit(solution)/shard_map/ppermute | solution.py:267
  87.8 7.9 %collective-permute-start.13 = (f32[192,384]{1,0:T(8,128)S(1)}, f32[192,384]{1,0:T(8,128)S(1)}, u32[]{:S(2)}, u32[]{:S(2)}) collective-permute-start(f32[192,384]{1,0:T(8,128)S(1)} %collective-permute-done.11), channel_id=1, source_target_pairs={{0,4},{1,5},{2,6},{3,7},{4,0},{5,1},{6,2},{7,3},{8,12},{9,13},{10,... | collective-permute-start | bytes 884744 | tf_op jit(solution)/shard_map/ppermute | solution.py:267
  89.4 24.6 %copy-start.4 = (f32[3,192,384]{2,1,0:T(8,128)}, f32[3,192,384]{2,1,0:T(8,128)S(1)}, u32[]{:S(2)}) copy-start(f32[3,192,384]{2,1,0:T(8,128)S(1)} %pad_maximum_fusion.refs_0_) | copy-start | bytes 2654212
  95.3 18.8 %collective-permute-start.6 = (f32[3,192,384]{2,1,0:T(8,128)S(1)}, f32[3,192,384]{2,1,0:T(8,128)}, u32[]{:S(2)}, u32[]{:S(2)}) collective-permute-start(f32[3,192,384]{2,1,0:T(8,128)S(1)} %pad_maximum_fusion.refs_0_), channel_id=1, source_target_pairs={{0,2},{1,3},{2,0},{3,1},{4,6},{5,7},{6,4},{7,5},{8,10},{9,11},{10,... | collective-permute-start | bytes 2654216 | tf_op jit(solution)/shard_map/ppermute | solution.py:267
  95.7 18.4 %collective-permute-start.10 = (f32[3,192,384]{2,1,0:T(8,128)}, f32[3,192,384]{2,1,0:T(8,128)}, u32[]{:S(2)}, u32[]{:S(2)}) collective-permute-start(f32[3,192,384]{2,1,0:T(8,128)} %pad_maximum_fusion.1.refs_2_), channel_id=1, source_target_pairs={{0,2},{1,3},{2,0},{3,1},{4,6},{5,7},{6,4},{7,5},{8,10},{9,11},{10,... | collective-permute-start | bytes 2654216 | tf_op jit(solution)/shard_map/ppermute | solution.py:267
  96.8 3.0 %copy-start.8 = (f32[3,192,384]{2,1,0:T(8,128)}, f32[3,192,384]{2,1,0:T(8,128)S(1)}, u32[]{:S(2)}) copy-start(f32[3,192,384]{2,1,0:T(8,128)S(1)} %collective-permute-done.20.refs_1_) | copy-start | bytes 2654212
  96.8 17.3 %collective-permute-start.14 = (f32[3,192,384]{2,1,0:T(8,128)}, f32[3,192,384]{2,1,0:T(8,128)}, u32[]{:S(2)}, u32[]{:S(2)}) collective-permute-start(f32[3,192,384]{2,1,0:T(8,128)} %pad_maximum_fusion.2.refs_4_), channel_id=1, source_target_pairs={{0,2},{1,3},{2,0},{3,1},{4,6},{5,7},{6,4},{7,5},{8,10},{9,11},{10,... | collective-permute-start | bytes 2654216 | tf_op jit(solution)/shard_map/ppermute | solution.py:267
  98.0 0.9 copy-start.9
  98.9 0.9 copy-start.10
  129.6 18.9 %collective-permute-start.27 = (f32[5,96,384]{2,1,0:T(8,128)}, f32[5,96,384]{2,1,0:T(8,128)S(1)}, u32[]{:S(2)}, u32[]{:S(2)}) collective-permute-start(f32[5,96,384]{2,1,0:T(8,128)} %get-tuple-element.27), channel_id=1, source_target_pairs={{0,4},{1,5},{2,6},{3,7},{4,0},{5,1},{6,2},{7,3},{8,12},{9,13},{10,... | collective-permute-start | bytes 2211848 | tf_op jit(solution)/shard_map/ppermute | solution.py:267
  131.4 19.6 %collective-permute-start.28 = (f32[5,96,384]{2,1,0:T(8,128)}, f32[5,96,384]{2,1,0:T(8,128)S(1)}, u32[]{:S(2)}, u32[]{:S(2)}) collective-permute-start(f32[5,96,384]{2,1,0:T(8,128)} %get-tuple-element.28), channel_id=1, source_target_pairs={{0,1},{1,0},{2,3},{3,2},{4,5},{5,4},{6,7},{7,6},{8,9},{9,8},{10,11... | collective-permute-start | bytes 2211848 | tf_op jit(solution)/shard_map/ppermute | solution.py:267
  132.9 32.6 %collective-permute-start.29 = (f32[5,96,384]{2,1,0:T(8,128)}, f32[5,96,384]{2,1,0:T(8,128)S(1)}, u32[]{:S(2)}, u32[]{:S(2)}) collective-permute-start(f32[5,96,384]{2,1,0:T(8,128)} %get-tuple-element.29), channel_id=1, source_target_pairs={{0,5},{1,4},{2,7},{3,6},{4,1},{5,0},{6,3},{7,2},{8,13},{9,12},{10,... | collective-permute-start | bytes 2211848 | tf_op jit(solution)/shard_map/ppermute | solution.py:267
  133.1 34.2 %collective-permute-start.30 = (f32[5,96,384]{2,1,0:T(8,128)}, f32[5,96,384]{2,1,0:T(8,128)S(1)}, u32[]{:S(2)}, u32[]{:S(2)}) collective-permute-start(f32[5,96,384]{2,1,0:T(8,128)} %get-tuple-element.26.refs_2_), channel_id=1, source_target_pairs={{0,2},{1,3},{2,0},{3,1},{4,6},{5,7},{6,4},{7,5},{8,10},{9,11},{10,... | collective-permute-start | bytes 2211848 | tf_op jit(solution)/shard_map/ppermute | solution.py:267
  148.4 19.4 %copy-start.11 = (f32[5,96,384]{2,1,0:T(8,128)}, f32[5,96,384]{2,1,0:T(8,128)S(1)}, u32[]{:S(2)}) copy-start(f32[5,96,384]{2,1,0:T(8,128)S(1)} %collective-permute-done.27.refs_3_) | copy-start | bytes 2211844
  148.4 18.9 %collective-permute-start.31 = (f32[5,96,384]{2,1,0:T(8,128)S(1)}, f32[5,96,384]{2,1,0:T(8,128)}, u32[]{:S(2)}, u32[]{:S(2)}) collective-permute-start(f32[5,96,384]{2,1,0:T(8,128)S(1)} %collective-permute-done.27.refs_3_), channel_id=1, source_target_pairs={{0,2},{1,3},{2,0},{3,1},{4,6},{5,7},{6,4},{7,5},{8,10},{9,11},{10,... | collective-permute-start | bytes 2211848 | tf_op jit(solution)/shard_map/ppermute | solution.py:267
  150.9 16.9 %copy-start.12 = (f32[5,96,384]{2,1,0:T(8,128)}, f32[5,96,384]{2,1,0:T(8,128)S(1)}, u32[]{:S(2)}) copy-start(f32[5,96,384]{2,1,0:T(8,128)S(1)} %collective-permute-done.28.refs_4_) | copy-start | bytes 2211844
  150.9 16.4 %collective-permute-start.32 = (f32[5,96,384]{2,1,0:T(8,128)S(1)}, f32[5,96,384]{2,1,0:T(8,128)}, u32[]{:S(2)}, u32[]{:S(2)}) collective-permute-start(f32[5,96,384]{2,1,0:T(8,128)S(1)} %collective-permute-done.28.refs_4_), channel_id=1, source_target_pairs={{0,2},{1,3},{2,0},{3,1},{4,6},{5,7},{6,4},{7,5},{8,10},{9,11},{10,... | collective-permute-start | bytes 2211848 | tf_op jit(solution)/shard_map/ppermute | solution.py:267
  165.5 2.4 copy-start.13
  165.5 2.3 collective-permute-start.33
  167.3 0.9 copy-start.14
  210.8 37.2 %collective-permute-start.34 = (f32[384,768]{1,0:T(8,128)}, f32[384,768]{1,0:T(8,128)S(1)}, u32[]{:S(2)}, u32[]{:S(2)}) collective-permute-start(f32[384,768]{1,0:T(8,128)} %get-tuple-element.31), channel_id=1, source_target_pairs={{0,1},{1,0},{2,5},{3,4},{4,3},{5,2},{6,7},{7,6},{8,9},{9,8},{10,13... | collective-permute-start | bytes 3538952 | tf_op jit(solution)/shard_map/ppermute | solution.py:267
  212.3 36.1 %collective-permute-start.35 = (f32[384,768]{1,0:T(8,128)}, f32[384,768]{1,0:T(8,128)S(1)}, u32[]{:S(2)}, u32[]{:S(2)}) collective-permute-start(f32[384,768]{1,0:T(8,128)} %get-tuple-element.32), channel_id=1, source_target_pairs={{0,0},{1,1},{2,4},{3,5},{4,2},{5,3},{6,6},{7,7},{8,8},{9,9},{10,12... | collective-permute-start | bytes 3538952 | tf_op jit(solution)/shard_map/ppermute | solution.py:267
  246.1 29.3 %collective-permute-start.36 = (f32[384,768]{1,0:T(8,128)}, f32[384,768]{1,0:T(8,128)}, u32[]{:S(2)}, u32[]{:S(2)}) collective-permute-start(f32[384,768]{1,0:T(8,128)} %get-tuple-element.33), channel_id=1, source_target_pairs={{0,3},{1,2},{2,7},{3,6},{4,1},{5,0},{6,5},{7,4},{8,11},{9,10},{10,... | collective-permute-start | bytes 3538952 | tf_op jit(solution)/shard_map/ppermute | solution.py:267
  247.9 28.9 %collective-permute-start.37 = (f32[384,768]{1,0:T(8,128)}, f32[384,768]{1,0:T(8,128)S(1)}, u32[]{:S(2)}, u32[]{:S(2)}) collective-permute-start(f32[384,768]{1,0:T(8,128)} %get-tuple-element.34), channel_id=1, source_target_pairs={{0,2},{1,3},{2,6},{3,7},{4,0},{5,1},{6,4},{7,5},{8,10},{9,11},{10,... | collective-permute-start | bytes 3538952 | tf_op jit(solution)/shard_map/ppermute | solution.py:267
  276.8 2.2 copy-start

commit v3 on v2

--- a/solution.py
+++ b/solution.py
@@ -51,75 +51,89 @@
 
 def green_kernel(merged, first, last, meta, coef, *refs):
     refs = list(refs)
-    sources = [refs.pop(0) for _ in range(merged or 1)]
+    sources = [refs.pop(0) for _ in range(merged or 2)]
     factor = refs.pop(0)
     acc_in = None if first else refs.pop(0)
-    occ_in = refs.pop(0) if last else None
     outs = [refs.pop(0) for _ in range(coef.shape[0] if last else 1)]
-    c_buf, left, right, sem = refs
-    step = pl.program_id(0)
-    width = c_buf.shape[1]
-    times = factor.shape[0]
+    c_buf, left, right, occ, sem = refs
+    species, step = pl.program_id(0), pl.program_id(1)
+    width = c_buf.shape[2]
+    times = factor.shape[1]
     strip = left.shape[0] // times
-    size = c_buf.shape[0] // 3
-
-    @pl.when(step == 0)
+    size = c_buf.shape[1] // 3
+
+    def copies_of(s):
+        copies = []
+        for d in range(3):
+            if merged:
+                for k in range(d, merged, 3):
+                    rows, part = sources[k].shape[1:]
+                    start = pl.multiple_of(meta[k // 3 % 2], 16) + d * size
+                    here = c_buf.at[s, pl.ds(start, rows), pl.ds(k // 6 * part, part)]
+                    copies.append(pltpu.make_async_copy(sources[k].at[s], here, sem.at[s]))
+            else:
+                rows = pl.ds(pl.multiple_of(meta[2 + d], 16), size)
+                here = c_buf.at[s, pl.ds(d * size, size), :]
+                copies.append(pltpu.make_async_copy(sources[s].at[rows, :], here, sem.at[s]))
+        return copies
+
+    @pl.when(jnp.logical_and(species == 0, step == 0))
     def _():
-        copies = []
-        for k, source in enumerate(sources):
-            for s in range(3):
-                if merged:
-                    rows, part = source.shape[1:]
-                    start = pl.multiple_of(meta[k % 2], 16) + s * size
-                    here = c_buf.at[pl.ds(start, rows), pl.ds(k // 2 * part, part)]
-                    copies.append(pltpu.make_async_copy(source.at[s], here, sem))
-                else:
-                    start = pl.multiple_of(meta[2 + s], 16)
-                    here = c_buf.at[pl.ds(s * size, size), :]
-                    copies.append(pltpu.make_async_copy(source.at[pl.ds(start, size), :], here, sem))
-        for copy in copies:
-            copy.start()
-        for copy in copies:
-            copy.wait()
-        high, low = halves(c_buf[...])
-        right[:, :width] = high
-        right[:, width : 2 * width] = high
-        right[:, 2 * width :] = low
-
-    c = c_buf[pl.ds(pl.multiple_of(meta[5 + step], 16), strip), :]
+        for s in range(2):
+            for copy in copies_of(s):
+                copy.start()
+
+    for s in range(2):
+
+        @pl.when(jnp.logical_and(species == s, step == 0))
+        def _(s=s):
+            for copy in copies_of(s):
+                copy.wait()
+            high, low = halves(c_buf[s])
+            right[:, :width] = high
+            right[:, width : 2 * width] = high
+            right[:, 2 * width :] = low
+
+    c = c_buf[species, pl.ds(pl.multiple_of(meta[5 + step], 16), strip), :]
     for t in range(times):
-        high, low = halves(c * factor[t : t + 1, :])
+        high, low = halves(c * factor[species, t : t + 1, :])
         s = slice(t * strip, (t + 1) * strip)
         left[s, :width] = high
         left[s, width : 2 * width] = low
         left[s, 2 * width :] = high
 
     row = pl.multiple_of(meta[10 + step], 128)
-    green = dot_t(left[...], right[pl.ds(row, size), :])
-    green = green.reshape(1, times, strip, size)
+    green = dot_t(left[...], right[pl.ds(row, size), :]).reshape(times, strip, size)
     if not first:
-        green = green + acc_in[...]
+        green = green + acc_in[0, 0]
     if not last:
-        outs[0][...] = green
+        outs[0][0, 0] = green
     else:
-        pairs = [occ_in[0, t] * green[0, t] for t in range(times)]
-        for n, out in enumerate(outs):
-            total = coef[n, 0] * pairs[0]
-            for t in range(1, times):
-                total = total + coef[n, t] * pairs[t]
-            out[0] = total
-
-
-def green_call(name, sources, factor, meta, coef, size, acc=None, occ=None):
-    times, width = factor.shape
+
+        @pl.when(species == 0)
+        def _():
+            occ[step] = green
+
+        @pl.when(species == 1)
+        def _():
+            pairs = [occ[step, t] * green[t] for t in range(times)]
+            for n, out in enumerate(outs):
+                total = coef[n, 0] * pairs[0]
+                for t in range(1, times):
+                    total = total + coef[n, t] * pairs[t]
+                out[0] = total
+
+
+def green_call(name, sources, factor, meta, coef, size, acc=None, last=False):
+    _, times, width = factor.shape
     strip = size // 4
-    first, last = acc is None, occ is not None
-    merged = len(sources) if len(sources) > 1 else 0
-    acc_spec = pl.BlockSpec((1, times, strip, size), lambda n, *_: (n, 0, 0, 0))
-    part_spec = pl.BlockSpec((1, strip, size), lambda n, *_: (n, 0, 0))
+    first = acc is None
+    merged = 0 if first else len(sources)
+    acc_spec = pl.BlockSpec((1, 1, times, strip, size), lambda s, n, *_: (s, n, 0, 0, 0))
+    part_spec = pl.BlockSpec((1, strip, size), lambda s, n, *_: (s * n, 0, 0))
     args = list(sources) + [factor]
     specs = [pl.BlockSpec(memory_space=pl.ANY)] * len(sources)
-    specs += [pl.BlockSpec((times, width), lambda n, *_: (0, 0))]
+    specs += [pl.BlockSpec((2, times, width), lambda s, n, *_: (0, 0, 0))]
     aliases = {}
     if not first:
         if not last:
@@ -127,32 +141,31 @@
         args.append(acc)
         specs.append(acc_spec)
     if last:
-        args.append(occ)
-        specs.append(acc_spec)
         out_shape = [jax.ShapeDtypeStruct((5, strip, size), F32)] * coef.shape[0]
         out_specs = [part_spec] * coef.shape[0]
     else:
-        out_shape = jax.ShapeDtypeStruct((5, times, strip, size), F32)
+        out_shape = jax.ShapeDtypeStruct((2, 5, times, strip, size), F32)
         out_specs = acc_spec
     return pl.pallas_call(
         functools.partial(green_kernel, merged, first, last),
         grid_spec=pltpu.PrefetchScalarGridSpec(
             num_scalar_prefetch=2,
-            grid=(5,),
+            grid=(2, 5),
             in_specs=specs,
             out_specs=out_specs,
             scratch_shapes=[
-                pltpu.VMEM((3 * size, width), F32),
+                pltpu.VMEM((2, 3 * size, width), F32),
                 pltpu.VMEM((times * strip, 3 * width), BF16),
                 pltpu.VMEM((3 * size, 3 * width), BF16),
-                pltpu.SemaphoreType.DMA,
+                pltpu.VMEM((5 if last else 1, times, strip, size), F32),
+                pltpu.SemaphoreType.DMA((2,)),
             ],
         ),
         out_shape=out_shape,
         input_output_aliases=aliases,
         compiler_params=pltpu.CompilerParams(vmem_limit_bytes=VMEM_LIMIT),
         cost_estimate=pl.CostEstimate(
-            flops=6 * 5 * times * strip * size * width, bytes_accessed=12 << 20, transcendentals=0
+            flops=12 * 5 * times * strip * size * width, bytes_accessed=24 << 20, transcendentals=0
         ),
         name=name,
     )(meta, coef, *args)
@@ -161,7 +174,7 @@
 def chain_kernel(block, *refs):
     at, spots = refs[:2]
     parts, (v_high, v_low, near_ref, far_ref) = refs[2:10], refs[10:14]
-    vh, vl, pf, ph, plo, rh, rl, xf, xh, xl, sem_p, sem_v, sem_r = refs[14:]
+    vh, vl, pf, ph, plo, rh, rl, xf, xh, xl, buf, sem_p, sem_v, sem_r, sem_o = refs[14:]
     n = vh.shape[0]
     m = rh.shape[0]
     half = far_ref.shape[1]
@@ -227,26 +240,37 @@
         s = slice(b * block, (b + 1) * block)
         xh[:, s], xl[:, s] = halves(xf[:, s] + times_p(high, low, b))
     high, low = xh[...], xl[...]
-    near = pl.multiple_of(at[1] * half, 128)
-    far = pl.multiple_of((1 - at[1]) * half, 128)
-    for start, out in ((far, far_ref), (near, near_ref)):
-        out[...] = dot3(high, low, vh[:, pl.ds(start, half)], vl[:, pl.ds(start, half)])
+    out_copies = []
+    for h in range(n // half):
+        cols = slice(h * half, (h + 1) * half)
+        slot = at[1] ^ h
+        buf[slot] = dot3(high, low, vh[:, cols], vl[:, cols])
+        for k, out in enumerate((near_ref, far_ref)):
+            copy = pltpu.make_async_copy(buf.at[k], out, sem_o.at[h])
+
+            @pl.when(slot == k)
+            def _(copy=copy):
+                copy.start()
+
+        out_copies.append(copy)
+    for copy in out_copies:
+        copy.wait()
 
 
 def chain(at, spots, parts, v_high, v_low, rows, cols):
     n = v_high.shape[0]
-    block = 2 * TILE
+    block = cols
     big = pltpu.VMEM((n, n), BF16)
     strip = pltpu.VMEM((rows, n), BF16)
     smem, hbm = pl.BlockSpec(memory_space=pltpu.SMEM), pl.BlockSpec(memory_space=pl.ANY)
     scratch = [big, big, pltpu.VMEM((n, n), F32), big, big, strip, strip]
-    scratch += [pltpu.VMEM((rows, n), F32), strip, strip]
+    scratch += [pltpu.VMEM((rows, n), F32), strip, strip, pltpu.VMEM((n // cols, rows, cols), F32)]
     scratch += [pltpu.SemaphoreType.DMA, pltpu.SemaphoreType.DMA((2, n // block))]
-    scratch += [pltpu.SemaphoreType.DMA((2,))]
+    scratch += [pltpu.SemaphoreType.DMA((2,))] * 2
     return pl.pallas_call(
         functools.partial(chain_kernel, block),
         in_specs=[smem] * 2 + [hbm] * (len(parts) + 2),
-        out_specs=[pl.BlockSpec(memory_space=pltpu.VMEM)] * 2,
+        out_specs=[hbm] * 2,
         out_shape=[jax.ShapeDtypeStruct((rows, cols), F32)] * 2,
         scratch_shapes=scratch,
         compiler_params=pltpu.CompilerParams(vmem_limit_bytes=VMEM_LIMIT),
@@ -276,8 +300,12 @@
     return lax.ppermute(v, "tm", [(i, (i + steps) % size) for i in range(size)])
 
 
+def together(*values):
+    return lax.optimization_barrier(values)
+
+
 def after(v, *others):
-    return lax.optimization_barrier((v,) + others)[0]
+    return together(v, *others)[0]
 
 
 def tables_of(size):
@@ -324,7 +352,7 @@
     meta, spots = (jnp.array(t)[here] for t in tables_of(size))
 
     energies = jnp.stack([eps_occ, -eps_vir])
-    arriving = jnp.concatenate([ring(energies, t) for t in range(1, planes)], axis=1)
+    arriving = [ring(energies, t) for t in range(1, planes)]
 
     def factor(e):
         return jnp.exp(e[None, :] * tau[:, None])
@@ -337,30 +365,34 @@
 
     start = (2 * x + y) * size + core * 2 * strip
     common = (meta, coef, size)
-    own = [None, None]
-    sources = [[], []]
-    piece = None
-    v_high = v_low = None
-    for s, c in enumerate((c_occ, c_vir)):
-        before = piece
-        piece = lax.dynamic_slice_in_dim(c, start, 2 * strip, 0)
-        if before is not None:
-            piece = after(piece, before, own[1])
-        for t in range(1, planes):
-            arrived = piece = ring(piece)
-            if s == 0 and t == 1:
-                v_high, v_low = split(coulomb)
-                piece = after(piece, v_high)
-            elif s == 0 and t < 4:
-                args = (("green_occ_own", c_occ), ("green_vir_own", c_vir))[t - 2]
-                own[t - 2] = green_call(
-                    args[0], [after(args[1], arrived)], factor(energies[t - 2]), *common
-                )
-                piece = after(piece, own[t - 2])
-            sets = jnp.stack([arrived, over(arrived, 1, 0, 0), over(arrived, 0, 1, 0)])
-            sources[s] += [sets, over(sets, 0, 0, 1)]
-    occ = green_call("green_occ", sources[0], factor(arriving[0]), *common, own[0])
-    parts = green_call("green_vir", sources[1], factor(arriving[1]), *common, own[1], occ)
+    piece = jnp.stack([lax.dynamic_slice_in_dim(c, start, 2 * strip, 0) for c in (c_occ, c_vir)])
+    part = c_occ.shape[1]
+    v_high, v_low = split(coulomb)
+
+    def to_neighbours(v):
+        return [over(v, 1, 0, 0), over(v, 0, 1, 0)]
+
+    def with_other_core(near):
+        return near + [over(v, 0, 0, 1) for v in near]
+
+    arrived, v_high, v_low, *arriving = together(ring(piece), v_high, v_low, *arriving)
+    factors = jnp.stack([factor(e) for e in jnp.concatenate(arriving, axis=1)])
+    own = [after(c_occ, arrived), c_vir]
+    green = green_call("green_own", own, jnp.stack([factor(e) for e in energies]), *common)
+    near, sets = [arrived], []
+    for t in range(2, planes):
+        *near, arrived, green = together(*near, *to_neighbours(near[0]), ring(near[0]), green)
+        sets.append(with_other_core(near))
+        near = [arrived]
+        if t == 3:
+            sets[0] = list(together(*sets[0], arrived))[:-1]
+    *near, green = together(
+        *near,
+        *to_neighbours(near[0]),
+        green_call("green_first", sets[0], factors[:, :, :part], *common, green),
+    )
+    rest = sum(sets[1:], []) + with_other_core(near)
+    parts = green_call("green_rest", rest, factors[:, :, part:], *common, green, True)
 
     parts = [over(p, dx, dy, 0) if dx + dy else p for p, (dx, dy) in zip(parts, ways)]
     parts += [over(p, 0, 0, 1) for p in parts]
@@ -369,7 +401,7 @@
     for e in range(2):
         at = jnp.stack([(2 * core + (y ^ e)) * tile_rows, x]).astype(jnp.int32)
         near, far = chain(at, spots, parts, v_high, v_low, tile_rows, tile_cols)
-        for dx, value in ((1, far), (0, near)):
+        for dx, value in ((1 - e, (near, far)[1 - e]), (e, (near, far)[e])):
             value = move(value, lambda x, y, c, dx=dx, e=e: (x ^ dx, c, y ^ e))
             arrivals.append((2 * (x ^ dx) + (core ^ e), value))
     out = jnp.zeros((per_plane, tile_rows, tile_cols), F32)

time: 283 us -> 250 us (0.88)
  waiting for transfers between devices: 107 us -> 75 us
  Pallas kernels: 127 us -> 133 us
    ppermute x9 -> x6, waiting for transfers between devices: 32.3 us -> 3.02 us  [ring(): return lax.ppermute(v, 'tm', [(i, (i + steps) % size) for i in range(size)])]
    pallas_call x2, Pallas kernels: 74.4 us -> 79.7 us  [chain(): pl.pallas_call(functools.partial(chain_kernel, block), in_specs=[smem] *...]
    ppermute x29 -> x26, starting transfers between devices: 22.8 us -> 18.1 us  [move(): return lax.ppermute(v, ('row', 'col'), pairs)]
    ppermute x9 -> x6, starting transfers between devices: 5.22 us -> 8.65 us  [ring(): return lax.ppermute(v, 'tm', [(i, (i + steps) % size) for i in range(size)])]
    ppermute x29 -> x26, waiting for transfers between devices: 74.3 us -> 71.9 us  [move(): return lax.ppermute(v, ('row', 'col'), pairs)]
    pallas_call x4 -> x3, Pallas kernels: 45.1 us -> 45.1 us  [green_call(): pl.pallas_call(functools.partial(green_kernel, merged, first, last), grid...]
  transfers between devices with their start and end apart: 38 -> 32, of which waited for: 18 -> 13; matrix products, arithmetic and copies ran while one was open for 4% -> 4% of each run, Pallas kernels for 22% -> 27%
where the time goes in v3:
time: 250 us
  Pallas kernels  133 us (53%)
  waiting for transfers between devices  75 us (30%)
  starting transfers between devices  26.8 us (11%)
  local copies, waits for them, and re-layouts  9.2 us (4%)
  other arithmetic  5.56 us (2%)
    pallas_call x2, Pallas kernels, chain(): pl.pallas_call(functools.partial(chain_kernel, block), in_specs=[smem] *...  79.7 us
    ppermute x26, waiting for transfers between devices, move(): return lax.ppermute(v, ('row', 'col'), pairs)  71.9 us
    pallas_call x3, Pallas kernels, green_call(): pl.pallas_call(functools.partial(green_kernel, merged, first, last), grid...  45.1 us
    ppermute x26, starting transfers between devices, move(): return lax.ppermute(v, ('row', 'col'), pairs)  18.1 us
    ppermute x6, starting transfers between devices, ring(): return lax.ppermute(v, 'tm', [(i, (i + steps) % size) for i in range(size)])  8.65 us
    pallas_call x1, Pallas kernels, split(): pl.pallas_call(split_kernel, grid=(4,), in_specs=[spec], out_specs=[spec]...  7.87 us
  transfers between devices with their start and end apart: 32, of which 13 were waited for; matrix products, arithmetic and copies ran while one was open for 4% of the time, Pallas kernels for 27%

profile of v3, /device:TPU:0, one launch (start us, length us, event | category | flops | bytes accessed | tf_op | source)
XLA Modules:
  0.0 249.7 jit_solution(17505006280369061327)
XLA Ops:
  0.0 1.1 dynamic-slice_bitcast_fusion
  1.1 3.1 %collective-permute-start = (f32[2,192,384]{2,1,0:T(8,128)S(1)}, f32[2,192,384]{2,1,0:T(8,128)S(1)}, u32[]{:S(2)}, u32[]{:S(2)}) collective-permute-start(f32[2,192,384]{2,1,0:T(8,128)S(1)} %pad_maximum_fusion), channel_id=1, source_target_pairs={{0,8},{8,16},{16,24},{24,0},{1,9},{9,17},{17,25},{25,1},{2,10},{10... | collective-permute-start | bytes 1769480 | tf_op jit(solution)/shard_map/ppermute | solution.py:300
  4.2 0.7 neg.3
  4.9 0.7 stack.54
  5.6 1.6 collective-permute-start.1
  7.2 1.1 collective-permute-start.2
  8.3 2.8 %collective-permute-start.3 = (f32[2,384]{1,0:T(2,128)S(1)}, f32[2,384]{1,0:T(2,128)S(1)}, u32[]{:S(2)}, u32[]{:S(2)}) collective-permute-start(f32[2,384]{1,0:T(2,128)S(1)} %pad_maximum_fusion.4), channel_id=1, source_target_pairs={{0,24},{8,0},{16,8},{24,16},{1,25},{9,1},{17,9},{25,17},{2,26},{10... | collective-permute-start | bytes 9224 | tf_op jit(solution)/shard_map/ppermute | solution.py:300
  11.2 0.8 cosine_multiply_fusion
  12.0 0.8 multiply_exponential_fusion.3
  12.8 7.9 %split_coulomb.1 = (bf16[1536,1536]{1,0:T(8,128)(2,1)}, bf16[1536,1536]{1,0:T(8,128)(2,1)}) custom-call(f32[1536,1536]{1,0:T(8,128)} %v_ref.1), custom_call_target="tpu_custom_call" | custom-call | tf_op jit(solution)/shard_map/split_coulomb/pallas_call | solution.py:41
  20.7 1.6 collective-permute-start.4
  22.3 1.5 collective-permute-start.5
  23.8 1.3 fusion.1.meta
  25.0 0.6 maximum_multiply_fusion.coef
  25.6 0.6 pad_maximum_fusion.3.refs_2_
  26.2 11.8 %green_own.1.refs_7_ = f32[2,5,4,96,384]{4,3,2,1,0:T(8,128)} custom-call(s32[15]{0:T(128)} %fusion.1.meta, f32[4,4]{1,0:T(4,128)} %maximum_multiply_fusion.coef, f32[1536,384]{1,0:T(8,128)} %refs_0_, f32[1536,384]{1,0:T(8,128)} %refs_1_.1, f32[2,4,384]{2,1,0:T(4,128)} %pad_maximum_fusion.3.refs_2_), custom_call_target="tpu_custom_call" | custom-call | flops 3397386240 | bytes 25165824 | tf_op jit(solution)/shard_map/green_own/pallas_call | solution.py:149
  38.1 1.0 collective-permute-done.6.refs_0_
  39.1 0.5 collective-permute-start.7
  39.6 0.5 collective-permute-start.8
  40.2 0.5 collective-permute-start.16
  40.7 11.2 %collective-permute-done.7.refs_1_ = f32[2,192,384]{2,1,0:T(8,128)} collective-permute-done((f32[2,192,384]{2,1,0:T(8,128)}, f32[2,192,384]{2,1,0:T(8,128)}, u32[]{:S(2)}, u32[]{:S(2)}) %collective-permute-start.7) | collective-permute-done | bytes 589856 | tf_op jit(solution)/shard_map/ppermute | solution.py:291
  51.9 0.2 collective-permute-done.8.refs_2_
  52.1 2.0 collective-permute-done.9.refs_6_
  54.2 1.5 collective-permute-start.13
  55.7 1.5 collective-permute-start.14
  57.2 0.1 multiply_exponential_fusion.1
  57.3 0.7 pad_maximum_fusion.2.refs_6_
  58.1 0.4 collective-permute-start.11
  58.5 0.2 collective-permute-start.12
  58.7 0.2 copy-done.5
  58.9 0.2 copy-done.6
  59.1 14.2 %green_first.1.refs_13_ = f32[2,5,4,96,384]{4,3,2,1,0:T(8,128)} custom-call(s32[15]{0:T(128)} %fusion.1.meta, f32[4,4]{1,0:T(4,128)} %maximum_multiply_fusion.coef, f32[2,192,384]{2,1,0:T(8,128)} %copy-done.1, f32[2,192,384]{2,1,0:T(8,128)} %copy-done.2, f32[2,192,384]{2,1,0:T(8,128)} %copy-done.3, ...), custom_call_target="tpu_custom_call", output_to_operand_aliasing={{}: (9, {})} | custom-call | flops 3397386240 | bytes 25165824 | tf_op jit(solution)/shard_map/green_first/pallas_call | solution.py:149
  73.2 0.4 collective-permute-start.18
  73.7 0.2 collective-permute-start.19
  73.8 0.4 collective-permute-start.20
  74.2 0.6 pad_maximum_fusion.1.refs_12_
  74.8 0.7 collective-permute-done.18.refs_9_
  75.5 0.8 collective-permute-done.19.refs_10_
  76.4 0.8 collective-permute-done.20.refs_11_
  77.2 0.8 copy-done.15
  78.0 19.1 %green_rest.1 = (f32[5,96,384]{2,1,0:T(8,128)}, f32[5,96,384]{2,1,0:T(8,128)}, f32[5,96,384]{2,1,0:T(8,128)}, f32[5,96,384]{2,1,0:T(8,128)}) custom-call(s32[15]{0:T(128)} %fusion.1.meta, f32[4,4]{1,0:T(4,128)} %maximum_multiply_fusion.coef, f32[2,192,384]{2,1,0:T(8,128)} %collective-permute-done.6.refs_0_, f32[2,192,384]{2,1,0:T(8,128)} %collective-permute-done.7.refs_1_, ...), custom_call_target="tpu_custom_call" | custom-call | flops 6794772480 | bytes 25165824 | tf_op jit(solution)/shard_map/green_rest/pallas_call | solution.py:149
  97.1 0.6 collective-permute-start.21
  97.7 0.5 collective-permute-start.22
  98.3 2.4 collective-permute-start.23
  100.7 15.5 %collective-permute-done.21.refs_3_ = f32[5,96,384]{2,1,0:T(8,128)S(1)} collective-permute-done((f32[5,96,384]{2,1,0:T(8,128)}, f32[5,96,384]{2,1,0:T(8,128)S(1)}, u32[]{:S(2)}, u32[]{:S(2)}) %collective-permute-start.21) | collective-permute-done | bytes 737312 | tf_op jit(solution)/shard_map/ppermute | solution.py:291
  116.2 1.1 collective-permute-done.22.refs_4_
  117.3 15.9 %collective-permute-done.23.refs_5_ = f32[5,96,384]{2,1,0:T(8,128)S(1)} collective-permute-done((f32[5,96,384]{2,1,0:T(8,128)}, f32[5,96,384]{2,1,0:T(8,128)S(1)}, u32[]{:S(2)}, u32[]{:S(2)}) %collective-permute-start.23) | collective-permute-done | bytes 737312 | tf_op jit(solution)/shard_map/ppermute | solution.py:291
  133.1 1.3 fusion.refs_1_
  134.4 0.6 pad_add_fusion
  135.1 0.4 collective-permute-done.27.refs_9_
  135.5 0.4 copy-done.11
  135.9 46.3 %chain.2 = (f32[384,768]{1,0:T(8,128)}, f32[384,768]{1,0:T(8,128)}) custom-call(s32[2]{0:T(128)} %get-tuple-element.89.refs_0_, s32[80]{0:T(128)} %fusion.refs_1_, f32[5,96,384]{2,1,0:T(8,128)} %get-tuple-element.69.refs_2_, f32[5,96,384]{2,1,0:T(8,128)} %copy-done.8, f32[5,96,384]{2,1,0:T(8,128)} %copy-done.9, f32[5,96,384]{2,1,0:T(8,128)} %copy-done.10, ...), custom_call_target="tpu_custom_call" | custom-call | flops 21743271936 | bytes 20971520 | tf_op jit(solution)/shard_map/chain/pallas_call | solution.py:270
  182.2 0.6 collective-permute-start.28
  182.9 1.9 collective-permute-start.29
  184.8 33.5 %chain.3 = (f32[384,768]{1,0:T(8,128)}, f32[384,768]{1,0:T(8,128)}) custom-call(s32[2]{0:T(128)} %get-tuple-element.90.refs_0_, s32[80]{0:T(128)} %fusion.refs_1_, f32[5,96,384]{2,1,0:T(8,128)} %get-tuple-element.69.refs_2_, f32[5,96,384]{2,1,0:T(8,128)} %copy-done.8, f32[5,96,384]{2,1,0:T(8,128)} %copy-done.9, f32[5,96,384]{2,1,0:T(8,128)} %copy-done.10, ...), custom_call_target="tpu_custom_call" | custom-call | flops 21743271936 | bytes 20971520 | tf_op jit(solution)/shard_map/chain/pallas_call | solution.py:270
  218.3 1.7 collective-permute-start.30
  219.9 1.1 collective-permute-start.31
  221.1 0.4 broadcast_in_dim.10
  221.5 0.1 bitcast_dynamic-update-slice_fusion.2
  221.6 23.2 %collective-permute-done.30 = f32[384,768]{1,0:T(8,128)} collective-permute-done((f32[384,768]{1,0:T(8,128)}, f32[384,768]{1,0:T(8,128)}, u32[]{:S(2)}, u32[]{:S(2)}) %collective-permute-start.30) | collective-permute-done | bytes 1179680 | tf_op jit(solution)/shard_map/ppermute | solution.py:291
  244.8 1.3 bitcast_dynamic-update-slice_fusion.1
  246.2 2.0 collective-permute-done.31
  248.2 0.1 copy-done
  248.4 1.1 bitcast_dynamic-update-slice_fusion
  (64 shorter events, 0.3 us)
Async XLA Ops:
  1.1 19.5 %collective-permute-start = (f32[2,192,384]{2,1,0:T(8,128)S(1)}, f32[2,192,384]{2,1,0:T(8,128)S(1)}, u32[]{:S(2)}, u32[]{:S(2)}) collective-permute-start(f32[2,192,384]{2,1,0:T(8,128)S(1)} %pad_maximum_fusion), channel_id=1, source_target_pairs={{0,8},{8,16},{16,24},{24,0},{1,9},{9,17},{17,25},{25,1},{2,10},{10... | collective-permute-start | bytes 1769480 | tf_op jit(solution)/shard_map/ppermute | solution.py:300
  5.6 15.1 %collective-permute-start.1 = (f32[2,384]{1,0:T(2,128)S(1)}, f32[2,384]{1,0:T(2,128)S(1)}, u32[]{:S(2)}, u32[]{:S(2)}) collective-permute-start(f32[2,384]{1,0:T(2,128)S(1)} %pad_maximum_fusion.4), channel_id=1, source_target_pairs={{0,8},{8,16},{16,24},{24,0},{1,9},{9,17},{17,25},{25,1},{2,10},{10... | collective-permute-start | bytes 9224 | tf_op jit(solution)/shard_map/ppermute | solution.py:300
  7.2 13.4 %collective-permute-start.2 = (f32[2,384]{1,0:T(2,128)S(1)}, f32[2,384]{1,0:T(2,128)S(1)}, u32[]{:S(2)}, u32[]{:S(2)}) collective-permute-start(f32[2,384]{1,0:T(2,128)S(1)} %pad_maximum_fusion.4), channel_id=1, source_target_pairs={{0,16},{8,24},{16,0},{24,8},{1,17},{9,25},{17,1},{25,9},{2,18},{10... | collective-permute-start | bytes 9224 | tf_op jit(solution)/shard_map/ppermute | solution.py:300
  8.3 12.3 %collective-permute-start.3 = (f32[2,384]{1,0:T(2,128)S(1)}, f32[2,384]{1,0:T(2,128)S(1)}, u32[]{:S(2)}, u32[]{:S(2)}) collective-permute-start(f32[2,384]{1,0:T(2,128)S(1)} %pad_maximum_fusion.4), channel_id=1, source_target_pairs={{0,24},{8,0},{16,8},{24,16},{1,25},{9,1},{17,9},{25,17},{2,26},{10... | collective-permute-start | bytes 9224 | tf_op jit(solution)/shard_map/ppermute | solution.py:300
  20.7 19.4 %copy-start.1 = (f32[2,192,384]{2,1,0:T(8,128)}, f32[2,192,384]{2,1,0:T(8,128)S(1)}, u32[]{:S(2)}) copy-start(f32[2,192,384]{2,1,0:T(8,128)S(1)} %collective-permute-done.refs_0_) | copy-start | bytes 1769476
  20.7 17.4 %collective-permute-start.4 = (f32[2,192,384]{2,1,0:T(8,128)S(1)}, f32[2,192,384]{2,1,0:T(8,128)S(1)}, u32[]{:S(2)}, u32[]{:S(2)}) collective-permute-start(f32[2,192,384]{2,1,0:T(8,128)S(1)} %collective-permute-done.refs_0_), channel_id=1, source_target_pairs={{0,1},{1,0},{2,3},{3,2},{4,5},{5,4},{6,7},{7,6},{8,9},{9,8},{10,11... | collective-permute-start | bytes 1769480 | tf_op jit(solution)/shard_map/ppermute | solution.py:291
  22.3 15.8 %collective-permute-start.5 = (f32[2,192,384]{2,1,0:T(8,128)S(1)}, f32[2,192,384]{2,1,0:T(8,128)S(1)}, u32[]{:S(2)}, u32[]{:S(2)}) collective-permute-start(f32[2,192,384]{2,1,0:T(8,128)S(1)} %collective-permute-done.refs_0_), channel_id=1, source_target_pairs={{0,4},{1,5},{2,6},{3,7},{4,0},{5,1},{6,2},{7,3},{8,12},{9,13},{10,... | collective-permute-start | bytes 1769480 | tf_op jit(solution)/shard_map/ppermute | solution.py:291
  23.8 15.3 %collective-permute-start.6 = (f32[2,192,384]{2,1,0:T(8,128)S(1)}, f32[2,192,384]{2,1,0:T(8,128)}, u32[]{:S(2)}, u32[]{:S(2)}) collective-permute-start(f32[2,192,384]{2,1,0:T(8,128)S(1)} %collective-permute-done.refs_0_), channel_id=1, source_target_pairs={{0,8},{8,16},{16,24},{24,0},{1,9},{9,17},{17,25},{25,1},{2,10},{10... | collective-permute-start | bytes 1769480 | tf_op jit(solution)/shard_map/ppermute | solution.py:300
  26.2 31.0 %copy-start.7 = (f32[4]{0:T(128)S(1)}, f32[4]{0:T(128)}, u32[]{:S(2)}) copy-start(f32[4]{0:T(128)} %param.14) | copy-start | bytes 52
  38.1 20.6 %copy-start.2 = (f32[2,192,384]{2,1,0:T(8,128)}, f32[2,192,384]{2,1,0:T(8,128)S(1)}, u32[]{:S(2)}) copy-start(f32[2,192,384]{2,1,0:T(8,128)S(1)} %collective-permute-done.4.refs_1_) | copy-start | bytes 1769476
  38.1 20.6 %copy-start.3 = (f32[2,192,384]{2,1,0:T(8,128)}, f32[2,192,384]{2,1,0:T(8,128)S(1)}, u32[]{:S(2)}) copy-start(f32[2,192,384]{2,1,0:T(8,128)S(1)} %collective-permute-done.5.refs_2_) | copy-start | bytes 1769476
  39.1 12.8 %collective-permute-start.7 = (f32[2,192,384]{2,1,0:T(8,128)}, f32[2,192,384]{2,1,0:T(8,128)}, u32[]{:S(2)}, u32[]{:S(2)}) collective-permute-start(f32[2,192,384]{2,1,0:T(8,128)} %collective-permute-done.6.refs_0_), channel_id=1, source_target_pairs={{0,1},{1,0},{2,3},{3,2},{4,5},{5,4},{6,7},{7,6},{8,9},{9,8},{10,11... | collective-permute-start | bytes 1769480 | tf_op jit(solution)/shard_map/ppermute | solution.py:291
  39.6 12.5 %collective-permute-start.8 = (f32[2,192,384]{2,1,0:T(8,128)}, f32[2,192,384]{2,1,0:T(8,128)}, u32[]{:S(2)}, u32[]{:S(2)}) collective-permute-start(f32[2,192,384]{2,1,0:T(8,128)} %collective-permute-done.6.refs_0_), channel_id=1, source_target_pairs={{0,4},{1,5},{2,6},{3,7},{4,0},{5,1},{6,2},{7,3},{8,12},{9,13},{10,... | collective-permute-start | bytes 1769480 | tf_op jit(solution)/shard_map/ppermute | solution.py:291
  40.1 14.1 %collective-permute-start.9 = (f32[2,192,384]{2,1,0:T(8,128)}, f32[2,192,384]{2,1,0:T(8,128)}, u32[]{:S(2)}, u32[]{:S(2)}) collective-permute-start(f32[2,192,384]{2,1,0:T(8,128)} %collective-permute-done.6.refs_0_), channel_id=1, source_target_pairs={{0,8},{8,16},{16,24},{24,0},{1,9},{9,17},{17,25},{25,1},{2,10},{10... | collective-permute-start | bytes 1769480 | tf_op jit(solution)/shard_map/ppermute | solution.py:300
  40.1 17.1 %collective-permute-start.15 = (f32[2,192,384]{2,1,0:T(8,128)S(1)}, f32[2,192,384]{2,1,0:T(8,128)S(1)}, u32[]{:S(2)}, u32[]{:S(2)}) collective-permute-start(f32[2,192,384]{2,1,0:T(8,128)S(1)} %collective-permute-done.refs_0_), channel_id=1, source_target_pairs={{0,2},{1,3},{2,0},{3,1},{4,6},{5,7},{6,4},{7,5},{8,10},{9,11},{10,... | collective-permute-start | bytes 1769480 | tf_op jit(solution)/shard_map/ppermute | solution.py:291
  40.2 17.9 %collective-permute-start.16 = (f32[2,192,384]{2,1,0:T(8,128)S(1)}, f32[2,192,384]{2,1,0:T(8,128)S(1)}, u32[]{:S(2)}, u32[]{:S(2)}) collective-permute-start(f32[2,192,384]{2,1,0:T(8,128)S(1)} %collective-permute-done.4.refs_1_), channel_id=1, source_target_pairs={{0,2},{1,3},{2,0},{3,1},{4,6},{5,7},{6,4},{7,5},{8,10},{9,11},{10,... | collective-permute-start | bytes 1769480 | tf_op jit(solution)/shard_map/ppermute | solution.py:291
  51.9 6.2 %collective-permute-start.17 = (f32[2,192,384]{2,1,0:T(8,128)S(1)}, f32[2,192,384]{2,1,0:T(8,128)S(1)}, u32[]{:S(2)}, u32[]{:S(2)}) collective-permute-start(f32[2,192,384]{2,1,0:T(8,128)S(1)} %collective-permute-done.5.refs_2_), channel_id=1, source_target_pairs={{0,2},{1,3},{2,0},{3,1},{4,6},{5,7},{6,4},{7,5},{8,10},{9,11},{10,... | collective-permute-start | bytes 1769480 | tf_op jit(solution)/shard_map/ppermute | solution.py:291
  54.2 19.0 %collective-permute-start.13 = (f32[2,192,384]{2,1,0:T(8,128)}, f32[2,192,384]{2,1,0:T(8,128)}, u32[]{:S(2)}, u32[]{:S(2)}) collective-permute-start(f32[2,192,384]{2,1,0:T(8,128)} %collective-permute-done.9.refs_6_), channel_id=1, source_target_pairs={{0,1},{1,0},{2,3},{3,2},{4,5},{5,4},{6,7},{7,6},{8,9},{9,8},{10,11... | collective-permute-start | bytes 1769480 | tf_op jit(solution)/shard_map/ppermute | solution.py:291
  55.7 17.6 %collective-permute-start.14 = (f32[2,192,384]{2,1,0:T(8,128)}, f32[2,192,384]{2,1,0:T(8,128)}, u32[]{:S(2)}, u32[]{:S(2)}) collective-permute-start(f32[2,192,384]{2,1,0:T(8,128)} %collective-permute-done.9.refs_6_), channel_id=1, source_target_pairs={{0,4},{1,5},{2,6},{3,7},{4,0},{5,1},{6,2},{7,3},{8,12},{9,13},{10,... | collective-permute-start | bytes 1769480 | tf_op jit(solution)/shard_map/ppermute | solution.py:291
  57.2 1.5 copy-start.4
  57.2 16.6 %collective-permute-start.10 = (f32[2,192,384]{2,1,0:T(8,128)}, f32[2,192,384]{2,1,0:T(8,128)S(1)}, u32[]{:S(2)}, u32[]{:S(2)}) collective-permute-start(f32[2,192,384]{2,1,0:T(8,128)} %collective-permute-done.6.refs_0_), channel_id=1, source_target_pairs={{0,2},{1,3},{2,0},{3,1},{4,6},{5,7},{6,4},{7,5},{8,10},{9,11},{10,... | collective-permute-start | bytes 1769480 | tf_op jit(solution)/shard_map/ppermute | solution.py:291
  58.1 0.8 copy-start.5
  58.1 1.0 copy-start.6
  58.1 16.7 %collective-permute-start.11 = (f32[2,192,384]{2,1,0:T(8,128)}, f32[2,192,384]{2,1,0:T(8,128)}, u32[]{:S(2)}, u32[]{:S(2)}) collective-permute-start(f32[2,192,384]{2,1,0:T(8,128)} %collective-permute-done.7.refs_1_), channel_id=1, source_target_pairs={{0,2},{1,3},{2,0},{3,1},{4,6},{5,7},{6,4},{7,5},{8,10},{9,11},{10,... | collective-permute-start | bytes 1769480 | tf_op jit(solution)/shard_map/ppermute | solution.py:291
  58.5 16.3 %collective-permute-start.12 = (f32[2,192,384]{2,1,0:T(8,128)}, f32[2,192,384]{2,1,0:T(8,128)}, u32[]{:S(2)}, u32[]{:S(2)}) collective-permute-start(f32[2,192,384]{2,1,0:T(8,128)} %collective-permute-done.8.refs_2_), channel_id=1, source_target_pairs={{0,2},{1,3},{2,0},{3,1},{4,6},{5,7},{6,4},{7,5},{8,10},{9,11},{10,... | collective-permute-start | bytes 1769480 | tf_op jit(solution)/shard_map/ppermute | solution.py:291
  73.2 2.3 collective-permute-start.18
  73.7 2.7 %collective-permute-start.19 = (f32[2,192,384]{2,1,0:T(8,128)}, f32[2,192,384]{2,1,0:T(8,128)S(1)}, u32[]{:S(2)}, u32[]{:S(2)}) collective-permute-start(f32[2,192,384]{2,1,0:T(8,128)} %collective-permute-done.13.refs_7_), channel_id=1, source_target_pairs={{0,2},{1,3},{2,0},{3,1},{4,6},{5,7},{6,4},{7,5},{8,10},{9,11},{10,... | collective-permute-start | bytes 1769480 | tf_op jit(solution)/shard_map/ppermute | solution.py:291
  73.8 3.4 %copy-start.12 = (f32[2,192,384]{2,1,0:T(8,128)}, f32[2,192,384]{2,1,0:T(8,128)S(1)}, u32[]{:S(2)}) copy-start(f32[2,192,384]{2,1,0:T(8,128)S(1)} %collective-permute-done.10.refs_3_) | copy-start | bytes 1769476
  73.8 3.4 %collective-permute-start.20 = (f32[2,192,384]{2,1,0:T(8,128)}, f32[2,192,384]{2,1,0:T(8,128)S(1)}, u32[]{:S(2)}, u32[]{:S(2)}) collective-permute-start(f32[2,192,384]{2,1,0:T(8,128)} %collective-permute-done.14.refs_8_), channel_id=1, source_target_pairs={{0,2},{1,3},{2,0},{3,1},{4,6},{5,7},{6,4},{7,5},{8,10},{9,11},{10,... | collective-permute-start | bytes 1769480 | tf_op jit(solution)/shard_map/ppermute | solution.py:291
  75.5 1.7 copy-start.13
  76.4 0.9 copy-start.14
  77.2 0.8 copy-start.15
  97.1 19.0 %collective-permute-start.21 = (f32[5,96,384]{2,1,0:T(8,128)}, f32[5,96,384]{2,1,0:T(8,128)S(1)}, u32[]{:S(2)}, u32[]{:S(2)}) collective-permute-start(f32[5,96,384]{2,1,0:T(8,128)} %get-tuple-element.70), channel_id=1, source_target_pairs={{0,4},{1,5},{2,6},{3,7},{4,0},{5,1},{6,2},{7,3},{8,12},{9,13},{10,... | collective-permute-start | bytes 2211848 | tf_op jit(solution)/shard_map/ppermute | solution.py:291
  97.7 19.6 %collective-permute-start.22 = (f32[5,96,384]{2,1,0:T(8,128)}, f32[5,96,384]{2,1,0:T(8,128)S(1)}, u32[]{:S(2)}, u32[]{:S(2)}) collective-permute-start(f32[5,96,384]{2,1,0:T(8,128)} %get-tuple-element.71), channel_id=1, source_target_pairs={{0,1},{1,0},{2,3},{3,2},{4,5},{5,4},{6,7},{7,6},{8,9},{9,8},{10,11... | collective-permute-start | bytes 2211848 | tf_op jit(solution)/shard_map/ppermute | solution.py:291
  98.3 34.9 %collective-permute-start.23 = (f32[5,96,384]{2,1,0:T(8,128)}, f32[5,96,384]{2,1,0:T(8,128)S(1)}, u32[]{:S(2)}, u32[]{:S(2)}) collective-permute-start(f32[5,96,384]{2,1,0:T(8,128)} %get-tuple-element.72), channel_id=1, source_target_pairs={{0,5},{1,4},{2,7},{3,6},{4,1},{5,0},{6,3},{7,2},{8,13},{9,12},{10,... | collective-permute-start | bytes 2211848 | tf_op jit(solution)/shard_map/ppermute | solution.py:291
  100.7 34.4 %collective-permute-start.24 = (f32[5,96,384]{2,1,0:T(8,128)}, f32[5,96,384]{2,1,0:T(8,128)S(1)}, u32[]{:S(2)}, u32[]{:S(2)}) collective-permute-start(f32[5,96,384]{2,1,0:T(8,128)} %get-tuple-element.69.refs_2_), channel_id=1, source_target_pairs={{0,2},{1,3},{2,0},{3,1},{4,6},{5,7},{6,4},{7,5},{8,10},{9,11},{10,... | collective-permute-start | bytes 2211848 | tf_op jit(solution)/shard_map/ppermute | solution.py:291
  116.2 19.3 %copy-start.8 = (f32[5,96,384]{2,1,0:T(8,128)}, f32[5,96,384]{2,1,0:T(8,128)S(1)}, u32[]{:S(2)}) copy-start(f32[5,96,384]{2,1,0:T(8,128)S(1)} %collective-permute-done.21.refs_3_) | copy-start | bytes 2211844
  116.2 18.9 %collective-permute-start.25 = (f32[5,96,384]{2,1,0:T(8,128)S(1)}, f32[5,96,384]{2,1,0:T(8,128)}, u32[]{:S(2)}, u32[]{:S(2)}) collective-permute-start(f32[5,96,384]{2,1,0:T(8,128)S(1)} %collective-permute-done.21.refs_3_), channel_id=1, source_target_pairs={{0,2},{1,3},{2,0},{3,1},{4,6},{5,7},{6,4},{7,5},{8,10},{9,11},{10,... | collective-permute-start | bytes 2211848 | tf_op jit(solution)/shard_map/ppermute | solution.py:291
  117.3 18.2 %copy-start.9 = (f32[5,96,384]{2,1,0:T(8,128)}, f32[5,96,384]{2,1,0:T(8,128)S(1)}, u32[]{:S(2)}) copy-start(f32[5,96,384]{2,1,0:T(8,128)S(1)} %collective-permute-done.22.refs_4_) | copy-start | bytes 2211844
  117.3 17.8 %collective-permute-start.26 = (f32[5,96,384]{2,1,0:T(8,128)S(1)}, f32[5,96,384]{2,1,0:T(8,128)}, u32[]{:S(2)}, u32[]{:S(2)}) collective-permute-start(f32[5,96,384]{2,1,0:T(8,128)S(1)} %collective-permute-done.22.refs_4_), channel_id=1, source_target_pairs={{0,2},{1,3},{2,0},{3,1},{4,6},{5,7},{6,4},{7,5},{8,10},{9,11},{10,... | collective-permute-start | bytes 2211848 | tf_op jit(solution)/shard_map/ppermute | solution.py:291
  133.1 2.4 copy-start.10
  133.1 2.3 collective-permute-start.27
  135.1 0.9 copy-start.11
  182.2 38.8 %collective-permute-start.28 = (f32[384,768]{1,0:T(8,128)}, f32[384,768]{1,0:T(8,128)S(1)}, u32[]{:S(2)}, u32[]{:S(2)}) collective-permute-start(f32[384,768]{1,0:T(8,128)} %get-tuple-element.75), channel_id=1, source_target_pairs={{0,1},{1,0},{2,5},{3,4},{4,3},{5,2},{6,7},{7,6},{8,9},{9,8},{10,13... | collective-permute-start | bytes 3538952 | tf_op jit(solution)/shard_map/ppermute | solution.py:291
  182.9 38.6 %collective-permute-start.29 = (f32[384,768]{1,0:T(8,128)}, f32[384,768]{1,0:T(8,128)S(1)}, u32[]{:S(2)}, u32[]{:S(2)}) collective-permute-start(f32[384,768]{1,0:T(8,128)} %get-tuple-element.76), channel_id=1, source_target_pairs={{0,0},{1,1},{2,4},{3,5},{4,2},{5,3},{6,6},{7,7},{8,8},{9,9},{10,12... | collective-permute-start | bytes 3538952 | tf_op jit(solution)/shard_map/ppermute | solution.py:291
  218.3 26.6 %collective-permute-start.30 = (f32[384,768]{1,0:T(8,128)}, f32[384,768]{1,0:T(8,128)}, u32[]{:S(2)}, u32[]{:S(2)}) collective-permute-start(f32[384,768]{1,0:T(8,128)} %get-tuple-element.77), channel_id=1, source_target_pairs={{0,2},{1,3},{2,6},{3,7},{4,0},{5,1},{6,4},{7,5},{8,10},{9,11},{10,... | collective-permute-start | bytes 3538952 | tf_op jit(solution)/shard_map/ppermute | solution.py:291
  219.9 28.3 %collective-permute-start.31 = (f32[384,768]{1,0:T(8,128)}, f32[384,768]{1,0:T(8,128)S(1)}, u32[]{:S(2)}, u32[]{:S(2)}) collective-permute-start(f32[384,768]{1,0:T(8,128)} %get-tuple-element.78), channel_id=1, source_target_pairs={{0,3},{1,2},{2,7},{3,6},{4,1},{5,0},{6,5},{7,4},{8,11},{9,10},{10,... | collective-permute-start | bytes 3538952 | tf_op jit(solution)/shard_map/ppermute | solution.py:291
  246.2 2.2 copy-start

commit v4 on v3

--- a/solution.py
+++ b/solution.py
@@ -174,15 +174,15 @@
 def chain_kernel(block, *refs):
     at, spots = refs[:2]
     parts, (v_high, v_low, near_ref, far_ref) = refs[2:10], refs[10:14]
-    vh, vl, pf, ph, plo, rh, rl, xf, xh, xl, buf, sem_p, sem_v, sem_r, sem_o = refs[14:]
-    n = vh.shape[0]
-    m = rh.shape[0]
-    half = far_ref.shape[1]
+    pf, wh, wl, lh, ll, xf, sem_p, sem_v, sem_r, sem_o = refs[14:]
+    n = pf.shape[0]
+    m = lh.shape[1]
+    blocks = n // block
     count, strip, size = parts[0].shape
     row = pl.multiple_of(at[0], 16)
     row_copies = [
-        pltpu.make_async_copy(v_high.at[pl.ds(row, m), :], rh, sem_r.at[0]),
-        pltpu.make_async_copy(v_low.at[pl.ds(row, m), :], rl, sem_r.at[1]),
+        pltpu.make_async_copy(v_high.at[pl.ds(row, m), :], lh.at[0], sem_r.at[0]),
+        pltpu.make_async_copy(v_low.at[pl.ds(row, m), :], ll.at[0], sem_r.at[1]),
     ]
     p_copies = []
     for k, part in enumerate(parts):
@@ -191,92 +191,86 @@
             j = pl.multiple_of(spots[2 * (k * count + t) + 1], 128)
             there = pf.at[pl.ds(i, strip), pl.ds(j, size)]
             p_copies.append(pltpu.make_async_copy(part.at[t], there, sem_p))
-    v_copies = []
-    for b in range(n // block):
-        cols = pl.ds(b * block, block)
-        v_copies.append(
-            [
-                pltpu.make_async_copy(v_high.at[:, cols], vh.at[:, cols], sem_v.at[0, b]),
-                pltpu.make_async_copy(v_low.at[:, cols], vl.at[:, cols], sem_v.at[1, b]),
-            ]
-        )
+
+    def v_copies(b):
+        cols = pl.ds(pl.multiple_of(b * block, block), block)
+        return [
+            pltpu.make_async_copy(v_high.at[:, cols], wh.at[1, :, cols], sem_v.at[0, b]),
+            pltpu.make_async_copy(v_low.at[:, cols], wl.at[1, :, cols], sem_v.at[1, b]),
+        ]
+
     for copy in p_copies + row_copies:
         copy.start()
     for copy in p_copies + row_copies:
         copy.wait()
-    for pair in v_copies:
-        for copy in pair:
+    for b in range(blocks):
+        for copy in v_copies(b):
             copy.start()
-    for b in range(n // block):
-        s = slice(b * block, (b + 1) * block)
-        for g in range(size, n, size):
-            if s.start < g < s.stop:
-                pf[g : s.stop, s.start : g] = pf[s.start : g, g : s.stop].T
-        ph[: s.stop, s], plo[: s.stop, s] = halves(pf[: s.stop, s])
-
-    def times_p(high, low, b):
-        s = slice(b * block, (b + 1) * block)
-        r = dot3(high[:, : s.stop], low[:, : s.stop], ph[: s.stop, s], plo[: s.stop, s])
-        if s.stop < n:
-            h, lo = high[:, s.stop :], low[:, s.stop :]
-            ph_t, pl_t = ph[s, s.stop :], plo[s, s.stop :]
-            r = r + dot_t(h, ph_t) + dot_t(lo, ph_t) + dot_t(h, pl_t)
-        return r
-
-    high, low = rh[...], rl[...]
-    for b in range(n // block):
-        s = slice(b * block, (b + 1) * block)
-        r = times_p(high, low, b)
-        xf[:, s] = r
-        xh[:, s], xl[:, s] = halves(r)
-    high, low = xh[...], xl[...]
-    for b in range(n // block):
-        for copy in v_copies[b]:
-            copy.wait()
-        s = slice(b * block, (b + 1) * block)
-        rh[:, s], rl[:, s] = halves(dot3(high, low, vh[:, s], vl[:, s]))
-    high, low = rh[...], rl[...]
-    for b in range(n // block):
-        s = slice(b * block, (b + 1) * block)
-        xh[:, s], xl[:, s] = halves(xf[:, s] + times_p(high, low, b))
-    high, low = xh[...], xl[...]
-    out_copies = []
-    for h in range(n // half):
-        cols = slice(h * half, (h + 1) * half)
-        slot = at[1] ^ h
-        buf[slot] = dot3(high, low, vh[:, cols], vl[:, cols])
-        for k, out in enumerate((near_ref, far_ref)):
-            copy = pltpu.make_async_copy(buf.at[k], out, sem_o.at[h])
-
-            @pl.when(slot == k)
-            def _(copy=copy):
-                copy.start()
-
-        out_copies.append(copy)
-    for copy in out_copies:
-        copy.wait()
+
+    def mirror(j, _):
+        def one(i, _):
+            rows, cols = (pl.ds(pl.multiple_of(s * size, 128), size) for s in (i, j))
+            pf[cols, rows] = pf[rows, cols].T
+            return 0
+
+        return lax.fori_loop(0, j, one, 0)
+
+    lax.fori_loop(1, n // size, mirror, 0)
+
+    def split_rows(i, _):
+        rows = pl.ds(pl.multiple_of(i * 128, 128), 128)
+        wh[0, rows], wl[0, rows] = halves(pf[rows, :])
+        return 0
+
+    lax.fori_loop(0, n // 128, split_rows, 0)
+
+    def body(k, _):
+        stage, b = lax.div(k, blocks), lax.rem(k, blocks)
+        this = lax.rem(stage, 2)
+        cols = pl.ds(pl.multiple_of(b * block, block), block)
+
+        @pl.when(stage == 1)
+        def _():
+            for copy in v_copies(b):
+                copy.wait()
+
+        r = dot3(lh[this], ll[this], wh[this, :, cols], wl[this, :, cols])
+        r = r + jnp.where(stage == 2, xf[this, :, cols], 0.0)
+        xf[this, :, cols] = r
+        lh[1 - this, :, cols], ll[1 - this, :, cols] = halves(r)
+
+        @pl.when(stage == 3)
+        def _():
+            src = xf.at[1, :, cols]
+            for out, mine in ((near_ref, True), (far_ref, False)):
+
+                @pl.when((at[1] == b) == mine)
+                def _(out=out):
+                    pltpu.make_async_copy(src, out, sem_o.at[b]).start()
+
+        return 0
+
+    lax.fori_loop(0, 4 * blocks, body, 0)
+    for h in range(blocks):
+        pltpu.make_async_copy(xf.at[1, :, : block], near_ref, sem_o.at[h]).wait()
 
 
 def chain(at, spots, parts, v_high, v_low, rows, cols):
     n = v_high.shape[0]
-    block = cols
-    big = pltpu.VMEM((n, n), BF16)
-    strip = pltpu.VMEM((rows, n), BF16)
+    blocks = n // cols
     smem, hbm = pl.BlockSpec(memory_space=pltpu.SMEM), pl.BlockSpec(memory_space=pl.ANY)
-    scratch = [big, big, pltpu.VMEM((n, n), F32), big, big, strip, strip]
-    scratch += [pltpu.VMEM((rows, n), F32), strip, strip, pltpu.VMEM((n // cols, rows, cols), F32)]
-    scratch += [pltpu.SemaphoreType.DMA, pltpu.SemaphoreType.DMA((2, n // block))]
-    scratch += [pltpu.SemaphoreType.DMA((2,))] * 2
+    scratch = [pltpu.VMEM((n, n), F32)] + [pltpu.VMEM((2, n, n), BF16)] * 2
+    scratch += [pltpu.VMEM((2, rows, n), BF16)] * 2 + [pltpu.VMEM((2, rows, n), F32)]
+    scratch += [pltpu.SemaphoreType.DMA, pltpu.SemaphoreType.DMA((2, blocks))]
+    scratch += [pltpu.SemaphoreType.DMA((2,)), pltpu.SemaphoreType.DMA((blocks,))]
     return pl.pallas_call(
-        functools.partial(chain_kernel, block),
+        functools.partial(chain_kernel, cols),
         in_specs=[smem] * 2 + [hbm] * (len(parts) + 2),
         out_specs=[hbm] * 2,
         out_shape=[jax.ShapeDtypeStruct((rows, cols), F32)] * 2,
         scratch_shapes=scratch,
         compiler_params=pltpu.CompilerParams(vmem_limit_bytes=VMEM_LIMIT),
-        cost_estimate=pl.CostEstimate(
-            flops=24 * rows * n * n, bytes_accessed=20 << 20, transcendentals=0
-        ),
+        cost_estimate=pl.CostEstimate(flops=24 * rows * n * n, bytes_accessed=20 << 20, transcendentals=0),
         name="chain",
     )(at, spots, *parts, v_high, v_low)
 

time: 250 us -> 235 us (0.940)
  Pallas kernels: 133 us -> 117 us
    pallas_call x2, Pallas kernels: 79.7 us -> 64.3 us  [chain(): pl.pallas_call(functools.partial(chain_kernel, cols), in_specs=[smem] * 2...]
  transfers between devices with their start and end apart: 32 -> 32, of which waited for: 13 -> 13; matrix products, arithmetic and copies ran while one was open for 4% -> 5% of each run, Pallas kernels for 27% -> 28%
where the time goes in v4:
time: 235 us; the launch traced here: 233 us
  Pallas kernels  117 us (50%)
  waiting for transfers between devices  74.8 us (32%)
  starting transfers between devices  26.9 us (11%)
  local copies, waits for them, and re-layouts  9.06 us (4%)
  other arithmetic  5.56 us (2%)
    ppermute x26, waiting for transfers between devices, move(): return lax.ppermute(v, ('row', 'col'), pairs)  71.8 us
    pallas_call x2, Pallas kernels, chain(): pl.pallas_call(functools.partial(chain_kernel, cols), in_specs=[smem] * 2...  64.3 us
    pallas_call x3, Pallas kernels, green_call(): pl.pallas_call(functools.partial(green_kernel, merged, first, last), grid...  44.7 us
    ppermute x26, starting transfers between devices, move(): return lax.ppermute(v, ('row', 'col'), pairs)  18.3 us
    ppermute x6, starting transfers between devices, ring(): return lax.ppermute(v, 'tm', [(i, (i + steps) % size) for i in range(size)])  8.65 us
    pallas_call x1, Pallas kernels, split(): pl.pallas_call(split_kernel, grid=(4,), in_specs=[spec], out_specs=[spec]...  7.87 us
  transfers between devices with their start and end apart: 32, of which 13 were waited for; matrix products, arithmetic and copies ran while one was open for 5% of the time, Pallas kernels for 28%

profile of v4, /device:TPU:0, one launch (start us, length us, event | category | flops | bytes accessed | tf_op | source)
XLA Modules:
  0.0 233.5 jit_solution(6023541351837524175)
XLA Ops:
  0.0 1.1 dynamic-slice_bitcast_fusion
  1.1 3.1 %collective-permute-start = (f32[2,192,384]{2,1,0:T(8,128)S(1)}, f32[2,192,384]{2,1,0:T(8,128)S(1)}, u32[]{:S(2)}, u32[]{:S(2)}) collective-permute-start(f32[2,192,384]{2,1,0:T(8,128)S(1)} %pad_maximum_fusion), channel_id=1, source_target_pairs={{0,8},{8,16},{16,24},{24,0},{1,9},{9,17},{17,25},{25,1},{2,10},{10... | collective-permute-start | bytes 1769480 | tf_op jit(solution)/shard_map/ppermute | solution.py:294
  4.2 0.7 neg.3
  4.9 0.7 stack.54
  5.6 1.6 collective-permute-start.1
  7.2 1.1 collective-permute-start.2
  8.3 2.8 %collective-permute-start.3 = (f32[2,384]{1,0:T(2,128)S(1)}, f32[2,384]{1,0:T(2,128)S(1)}, u32[]{:S(2)}, u32[]{:S(2)}) collective-permute-start(f32[2,384]{1,0:T(2,128)S(1)} %pad_maximum_fusion.4), channel_id=1, source_target_pairs={{0,24},{8,0},{16,8},{24,16},{1,25},{9,1},{17,9},{25,17},{2,26},{10... | collective-permute-start | bytes 9224 | tf_op jit(solution)/shard_map/ppermute | solution.py:294
  11.2 0.8 cosine_multiply_fusion
  12.0 0.8 multiply_exponential_fusion.3
  12.8 7.9 %split_coulomb.1 = (bf16[1536,1536]{1,0:T(8,128)(2,1)}, bf16[1536,1536]{1,0:T(8,128)(2,1)}) custom-call(f32[1536,1536]{1,0:T(8,128)} %v_ref.1), custom_call_target="tpu_custom_call" | custom-call | tf_op jit(solution)/shard_map/split_coulomb/pallas_call | solution.py:41
  20.7 1.6 collective-permute-start.4
  22.3 1.5 collective-permute-start.5
  23.8 1.3 fusion.1.meta
  25.0 0.6 maximum_multiply_fusion.coef
  25.6 0.6 pad_maximum_fusion.3.refs_2_
  26.2 11.8 %green_own.1.refs_7_ = f32[2,5,4,96,384]{4,3,2,1,0:T(8,128)} custom-call(s32[15]{0:T(128)} %fusion.1.meta, f32[4,4]{1,0:T(4,128)} %maximum_multiply_fusion.coef, f32[1536,384]{1,0:T(8,128)} %refs_0_, f32[1536,384]{1,0:T(8,128)} %refs_1_.1, f32[2,4,384]{2,1,0:T(4,128)} %pad_maximum_fusion.3.refs_2_), custom_call_target="tpu_custom_call" | custom-call | flops 3397386240 | bytes 25165824 | tf_op jit(solution)/shard_map/green_own/pallas_call | solution.py:149
  38.1 1.0 collective-permute-done.6.refs_0_
  39.1 0.5 collective-permute-start.7
  39.6 0.5 collective-permute-start.8
  40.2 0.5 collective-permute-start.16
  40.7 11.2 %collective-permute-done.7.refs_1_ = f32[2,192,384]{2,1,0:T(8,128)} collective-permute-done((f32[2,192,384]{2,1,0:T(8,128)}, f32[2,192,384]{2,1,0:T(8,128)}, u32[]{:S(2)}, u32[]{:S(2)}) %collective-permute-start.7) | collective-permute-done | bytes 589856 | tf_op jit(solution)/shard_map/ppermute | solution.py:285
  51.9 0.2 collective-permute-done.8.refs_2_
  52.1 2.0 collective-permute-done.9.refs_6_
  54.2 1.5 collective-permute-start.13
  55.7 1.5 collective-permute-start.14
  57.2 0.1 multiply_exponential_fusion.1
  57.3 0.7 pad_maximum_fusion.2.refs_6_
  58.1 0.4 collective-permute-start.11
  58.5 0.2 collective-permute-start.12
  58.7 0.2 copy-done.5
  58.9 0.2 copy-done.6
  59.1 14.2 %green_first.1.refs_13_ = f32[2,5,4,96,384]{4,3,2,1,0:T(8,128)} custom-call(s32[15]{0:T(128)} %fusion.1.meta, f32[4,4]{1,0:T(4,128)} %maximum_multiply_fusion.coef, f32[2,192,384]{2,1,0:T(8,128)} %copy-done.1, f32[2,192,384]{2,1,0:T(8,128)} %copy-done.2, f32[2,192,384]{2,1,0:T(8,128)} %copy-done.3, ...), custom_call_target="tpu_custom_call", output_to_operand_aliasing={{}: (9, {})} | custom-call | flops 3397386240 | bytes 25165824 | tf_op jit(solution)/shard_map/green_first/pallas_call | solution.py:149
  73.2 0.4 collective-permute-start.18
  73.7 0.2 collective-permute-start.19
  73.8 0.4 collective-permute-start.20
  74.2 0.6 pad_maximum_fusion.1.refs_12_
  74.8 0.7 collective-permute-done.18.refs_9_
  75.5 0.8 collective-permute-done.19.refs_10_
  76.4 0.8 collective-permute-done.20.refs_11_
  77.2 0.8 copy-done.15
  78.0 18.7 %green_rest.1 = (f32[5,96,384]{2,1,0:T(8,128)}, f32[5,96,384]{2,1,0:T(8,128)}, f32[5,96,384]{2,1,0:T(8,128)}, f32[5,96,384]{2,1,0:T(8,128)}) custom-call(s32[15]{0:T(128)} %fusion.1.meta, f32[4,4]{1,0:T(4,128)} %maximum_multiply_fusion.coef, f32[2,192,384]{2,1,0:T(8,128)} %collective-permute-done.6.refs_0_, f32[2,192,384]{2,1,0:T(8,128)} %collective-permute-done.7.refs_1_, ...), custom_call_target="tpu_custom_call" | custom-call | flops 6794772480 | bytes 25165824 | tf_op jit(solution)/shard_map/green_rest/pallas_call | solution.py:149
  96.8 0.6 collective-permute-start.21
  97.4 0.5 collective-permute-start.22
  97.9 2.4 %collective-permute-start.23 = (f32[5,96,384]{2,1,0:T(8,128)}, f32[5,96,384]{2,1,0:T(8,128)S(1)}, u32[]{:S(2)}, u32[]{:S(2)}) collective-permute-start(f32[5,96,384]{2,1,0:T(8,128)} %get-tuple-element.72), channel_id=1, source_target_pairs={{0,5},{1,4},{2,7},{3,6},{4,1},{5,0},{6,3},{7,2},{8,13},{9,12},{10,... | collective-permute-start | bytes 2211848 | tf_op jit(solution)/shard_map/ppermute | solution.py:285
  100.3 15.5 %collective-permute-done.21.refs_3_ = f32[5,96,384]{2,1,0:T(8,128)S(1)} collective-permute-done((f32[5,96,384]{2,1,0:T(8,128)}, f32[5,96,384]{2,1,0:T(8,128)S(1)}, u32[]{:S(2)}, u32[]{:S(2)}) %collective-permute-start.21) | collective-permute-done | bytes 737312 | tf_op jit(solution)/shard_map/ppermute | solution.py:285
  115.8 1.1 collective-permute-done.22.refs_4_
  116.9 15.8 %collective-permute-done.23.refs_5_ = f32[5,96,384]{2,1,0:T(8,128)S(1)} collective-permute-done((f32[5,96,384]{2,1,0:T(8,128)}, f32[5,96,384]{2,1,0:T(8,128)S(1)}, u32[]{:S(2)}, u32[]{:S(2)}) %collective-permute-start.23) | collective-permute-done | bytes 737312 | tf_op jit(solution)/shard_map/ppermute | solution.py:285
  132.8 1.3 fusion.refs_1_
  134.1 0.6 pad_add_fusion
  134.7 0.4 collective-permute-done.27.refs_9_
  135.1 0.4 copy-done.11
  135.6 32.1 %chain.2 = (f32[384,768]{1,0:T(8,128)}, f32[384,768]{1,0:T(8,128)}) custom-call(s32[2]{0:T(128)} %get-tuple-element.89.refs_0_, s32[80]{0:T(128)} %fusion.refs_1_, f32[5,96,384]{2,1,0:T(8,128)} %get-tuple-element.69.refs_2_, f32[5,96,384]{2,1,0:T(8,128)} %copy-done.8, f32[5,96,384]{2,1,0:T(8,128)} %copy-done.9, f32[5,96,384]{2,1,0:T(8,128)} %copy-done.10, ...), custom_call_target="tpu_custom_call" | custom-call | flops 21743271936 | bytes 20971520 | tf_op jit(solution)/shard_map/chain/pallas_call | solution.py:266
  167.7 0.6 collective-permute-start.28
  168.4 1.9 collective-permute-start.29
  170.3 32.1 %chain.3 = (f32[384,768]{1,0:T(8,128)}, f32[384,768]{1,0:T(8,128)}) custom-call(s32[2]{0:T(128)} %get-tuple-element.90.refs_0_, s32[80]{0:T(128)} %fusion.refs_1_, f32[5,96,384]{2,1,0:T(8,128)} %get-tuple-element.69.refs_2_, f32[5,96,384]{2,1,0:T(8,128)} %copy-done.8, f32[5,96,384]{2,1,0:T(8,128)} %copy-done.9, f32[5,96,384]{2,1,0:T(8,128)} %copy-done.10, ...), custom_call_target="tpu_custom_call" | custom-call | flops 21743271936 | bytes 20971520 | tf_op jit(solution)/shard_map/chain/pallas_call | solution.py:266
  202.4 1.9 collective-permute-start.30
  204.3 1.1 collective-permute-start.31
  205.4 0.4 broadcast_in_dim.10
  205.8 0.1 bitcast_dynamic-update-slice_fusion.3
  205.9 0.1 bitcast_dynamic-update-slice_fusion.2
  206.0 22.8 %collective-permute-done.30 = f32[384,768]{1,0:T(8,128)} collective-permute-done((f32[384,768]{1,0:T(8,128)}, f32[384,768]{1,0:T(8,128)}, u32[]{:S(2)}, u32[]{:S(2)}) %collective-permute-start.30) | collective-permute-done | bytes 1179680 | tf_op jit(solution)/shard_map/ppermute | solution.py:285
  228.8 1.3 bitcast_dynamic-update-slice_fusion.1
  230.1 2.2 collective-permute-done.31
  232.4 1.1 bitcast_dynamic-update-slice_fusion
  (64 shorter events, 0.3 us)
Async XLA Ops:
  1.1 19.5 %collective-permute-start = (f32[2,192,384]{2,1,0:T(8,128)S(1)}, f32[2,192,384]{2,1,0:T(8,128)S(1)}, u32[]{:S(2)}, u32[]{:S(2)}) collective-permute-start(f32[2,192,384]{2,1,0:T(8,128)S(1)} %pad_maximum_fusion), channel_id=1, source_target_pairs={{0,8},{8,16},{16,24},{24,0},{1,9},{9,17},{17,25},{25,1},{2,10},{10... | collective-permute-start | bytes 1769480 | tf_op jit(solution)/shard_map/ppermute | solution.py:294
  5.6 15.1 %collective-permute-start.1 = (f32[2,384]{1,0:T(2,128)S(1)}, f32[2,384]{1,0:T(2,128)S(1)}, u32[]{:S(2)}, u32[]{:S(2)}) collective-permute-start(f32[2,384]{1,0:T(2,128)S(1)} %pad_maximum_fusion.4), channel_id=1, source_target_pairs={{0,8},{8,16},{16,24},{24,0},{1,9},{9,17},{17,25},{25,1},{2,10},{10... | collective-permute-start | bytes 9224 | tf_op jit(solution)/shard_map/ppermute | solution.py:294
  7.2 13.4 %collective-permute-start.2 = (f32[2,384]{1,0:T(2,128)S(1)}, f32[2,384]{1,0:T(2,128)S(1)}, u32[]{:S(2)}, u32[]{:S(2)}) collective-permute-start(f32[2,384]{1,0:T(2,128)S(1)} %pad_maximum_fusion.4), channel_id=1, source_target_pairs={{0,16},{8,24},{16,0},{24,8},{1,17},{9,25},{17,1},{25,9},{2,18},{10... | collective-permute-start | bytes 9224 | tf_op jit(solution)/shard_map/ppermute | solution.py:294
  8.3 12.3 %collective-permute-start.3 = (f32[2,384]{1,0:T(2,128)S(1)}, f32[2,384]{1,0:T(2,128)S(1)}, u32[]{:S(2)}, u32[]{:S(2)}) collective-permute-start(f32[2,384]{1,0:T(2,128)S(1)} %pad_maximum_fusion.4), channel_id=1, source_target_pairs={{0,24},{8,0},{16,8},{24,16},{1,25},{9,1},{17,9},{25,17},{2,26},{10... | collective-permute-start | bytes 9224 | tf_op jit(solution)/shard_map/ppermute | solution.py:294
  20.7 19.4 %copy-start.1 = (f32[2,192,384]{2,1,0:T(8,128)}, f32[2,192,384]{2,1,0:T(8,128)S(1)}, u32[]{:S(2)}) copy-start(f32[2,192,384]{2,1,0:T(8,128)S(1)} %collective-permute-done.refs_0_) | copy-start | bytes 1769476
  20.7 17.4 %collective-permute-start.4 = (f32[2,192,384]{2,1,0:T(8,128)S(1)}, f32[2,192,384]{2,1,0:T(8,128)S(1)}, u32[]{:S(2)}, u32[]{:S(2)}) collective-permute-start(f32[2,192,384]{2,1,0:T(8,128)S(1)} %collective-permute-done.refs_0_), channel_id=1, source_target_pairs={{0,1},{1,0},{2,3},{3,2},{4,5},{5,4},{6,7},{7,6},{8,9},{9,8},{10,11... | collective-permute-start | bytes 1769480 | tf_op jit(solution)/shard_map/ppermute | solution.py:285
  22.3 15.8 %collective-permute-start.5 = (f32[2,192,384]{2,1,0:T(8,128)S(1)}, f32[2,192,384]{2,1,0:T(8,128)S(1)}, u32[]{:S(2)}, u32[]{:S(2)}) collective-permute-start(f32[2,192,384]{2,1,0:T(8,128)S(1)} %collective-permute-done.refs_0_), channel_id=1, source_target_pairs={{0,4},{1,5},{2,6},{3,7},{4,0},{5,1},{6,2},{7,3},{8,12},{9,13},{10,... | collective-permute-start | bytes 1769480 | tf_op jit(solution)/shard_map/ppermute | solution.py:285
  23.8 15.3 %collective-permute-start.6 = (f32[2,192,384]{2,1,0:T(8,128)S(1)}, f32[2,192,384]{2,1,0:T(8,128)}, u32[]{:S(2)}, u32[]{:S(2)}) collective-permute-start(f32[2,192,384]{2,1,0:T(8,128)S(1)} %collective-permute-done.refs_0_), channel_id=1, source_target_pairs={{0,8},{8,16},{16,24},{24,0},{1,9},{9,17},{17,25},{25,1},{2,10},{10... | collective-permute-start | bytes 1769480 | tf_op jit(solution)/shard_map/ppermute | solution.py:294
  26.2 31.0 %copy-start.7 = (f32[4]{0:T(128)S(1)}, f32[4]{0:T(128)}, u32[]{:S(2)}) copy-start(f32[4]{0:T(128)} %param.14) | copy-start | bytes 52
  38.1 20.6 %copy-start.2 = (f32[2,192,384]{2,1,0:T(8,128)}, f32[2,192,384]{2,1,0:T(8,128)S(1)}, u32[]{:S(2)}) copy-start(f32[2,192,384]{2,1,0:T(8,128)S(1)} %collective-permute-done.4.refs_1_) | copy-start | bytes 1769476
  38.1 20.6 %copy-start.3 = (f32[2,192,384]{2,1,0:T(8,128)}, f32[2,192,384]{2,1,0:T(8,128)S(1)}, u32[]{:S(2)}) copy-start(f32[2,192,384]{2,1,0:T(8,128)S(1)} %collective-permute-done.5.refs_2_) | copy-start | bytes 1769476
  39.1 12.8 %collective-permute-start.7 = (f32[2,192,384]{2,1,0:T(8,128)}, f32[2,192,384]{2,1,0:T(8,128)}, u32[]{:S(2)}, u32[]{:S(2)}) collective-permute-start(f32[2,192,384]{2,1,0:T(8,128)} %collective-permute-done.6.refs_0_), channel_id=1, source_target_pairs={{0,1},{1,0},{2,3},{3,2},{4,5},{5,4},{6,7},{7,6},{8,9},{9,8},{10,11... | collective-permute-start | bytes 1769480 | tf_op jit(solution)/shard_map/ppermute | solution.py:285
  39.6 12.5 %collective-permute-start.8 = (f32[2,192,384]{2,1,0:T(8,128)}, f32[2,192,384]{2,1,0:T(8,128)}, u32[]{:S(2)}, u32[]{:S(2)}) collective-permute-start(f32[2,192,384]{2,1,0:T(8,128)} %collective-permute-done.6.refs_0_), channel_id=1, source_target_pairs={{0,4},{1,5},{2,6},{3,7},{4,0},{5,1},{6,2},{7,3},{8,12},{9,13},{10,... | collective-permute-start | bytes 1769480 | tf_op jit(solution)/shard_map/ppermute | solution.py:285
  40.1 14.1 %collective-permute-start.9 = (f32[2,192,384]{2,1,0:T(8,128)}, f32[2,192,384]{2,1,0:T(8,128)}, u32[]{:S(2)}, u32[]{:S(2)}) collective-permute-start(f32[2,192,384]{2,1,0:T(8,128)} %collective-permute-done.6.refs_0_), channel_id=1, source_target_pairs={{0,8},{8,16},{16,24},{24,0},{1,9},{9,17},{17,25},{25,1},{2,10},{10... | collective-permute-start | bytes 1769480 | tf_op jit(solution)/shard_map/ppermute | solution.py:294
  40.1 17.1 %collective-permute-start.15 = (f32[2,192,384]{2,1,0:T(8,128)S(1)}, f32[2,192,384]{2,1,0:T(8,128)S(1)}, u32[]{:S(2)}, u32[]{:S(2)}) collective-permute-start(f32[2,192,384]{2,1,0:T(8,128)S(1)} %collective-permute-done.refs_0_), channel_id=1, source_target_pairs={{0,2},{1,3},{2,0},{3,1},{4,6},{5,7},{6,4},{7,5},{8,10},{9,11},{10,... | collective-permute-start | bytes 1769480 | tf_op jit(solution)/shard_map/ppermute | solution.py:285
  40.2 17.9 %collective-permute-start.16 = (f32[2,192,384]{2,1,0:T(8,128)S(1)}, f32[2,192,384]{2,1,0:T(8,128)S(1)}, u32[]{:S(2)}, u32[]{:S(2)}) collective-permute-start(f32[2,192,384]{2,1,0:T(8,128)S(1)} %collective-permute-done.4.refs_1_), channel_id=1, source_target_pairs={{0,2},{1,3},{2,0},{3,1},{4,6},{5,7},{6,4},{7,5},{8,10},{9,11},{10,... | collective-permute-start | bytes 1769480 | tf_op jit(solution)/shard_map/ppermute | solution.py:285
  51.9 6.2 %collective-permute-start.17 = (f32[2,192,384]{2,1,0:T(8,128)S(1)}, f32[2,192,384]{2,1,0:T(8,128)S(1)}, u32[]{:S(2)}, u32[]{:S(2)}) collective-permute-start(f32[2,192,384]{2,1,0:T(8,128)S(1)} %collective-permute-done.5.refs_2_), channel_id=1, source_target_pairs={{0,2},{1,3},{2,0},{3,1},{4,6},{5,7},{6,4},{7,5},{8,10},{9,11},{10,... | collective-permute-start | bytes 1769480 | tf_op jit(solution)/shard_map/ppermute | solution.py:285
  54.2 19.0 %collective-permute-start.13 = (f32[2,192,384]{2,1,0:T(8,128)}, f32[2,192,384]{2,1,0:T(8,128)}, u32[]{:S(2)}, u32[]{:S(2)}) collective-permute-start(f32[2,192,384]{2,1,0:T(8,128)} %collective-permute-done.9.refs_6_), channel_id=1, source_target_pairs={{0,1},{1,0},{2,3},{3,2},{4,5},{5,4},{6,7},{7,6},{8,9},{9,8},{10,11... | collective-permute-start | bytes 1769480 | tf_op jit(solution)/shard_map/ppermute | solution.py:285
  55.7 17.6 %collective-permute-start.14 = (f32[2,192,384]{2,1,0:T(8,128)}, f32[2,192,384]{2,1,0:T(8,128)}, u32[]{:S(2)}, u32[]{:S(2)}) collective-permute-start(f32[2,192,384]{2,1,0:T(8,128)} %collective-permute-done.9.refs_6_), channel_id=1, source_target_pairs={{0,4},{1,5},{2,6},{3,7},{4,0},{5,1},{6,2},{7,3},{8,12},{9,13},{10,... | collective-permute-start | bytes 1769480 | tf_op jit(solution)/shard_map/ppermute | solution.py:285
  57.2 1.5 copy-start.4
  57.2 16.6 %collective-permute-start.10 = (f32[2,192,384]{2,1,0:T(8,128)}, f32[2,192,384]{2,1,0:T(8,128)S(1)}, u32[]{:S(2)}, u32[]{:S(2)}) collective-permute-start(f32[2,192,384]{2,1,0:T(8,128)} %collective-permute-done.6.refs_0_), channel_id=1, source_target_pairs={{0,2},{1,3},{2,0},{3,1},{4,6},{5,7},{6,4},{7,5},{8,10},{9,11},{10,... | collective-permute-start | bytes 1769480 | tf_op jit(solution)/shard_map/ppermute | solution.py:285
  58.1 0.8 copy-start.5
  58.1 1.0 copy-start.6
  58.1 16.7 %collective-permute-start.11 = (f32[2,192,384]{2,1,0:T(8,128)}, f32[2,192,384]{2,1,0:T(8,128)}, u32[]{:S(2)}, u32[]{:S(2)}) collective-permute-start(f32[2,192,384]{2,1,0:T(8,128)} %collective-permute-done.7.refs_1_), channel_id=1, source_target_pairs={{0,2},{1,3},{2,0},{3,1},{4,6},{5,7},{6,4},{7,5},{8,10},{9,11},{10,... | collective-permute-start | bytes 1769480 | tf_op jit(solution)/shard_map/ppermute | solution.py:285
  58.5 16.3 %collective-permute-start.12 = (f32[2,192,384]{2,1,0:T(8,128)}, f32[2,192,384]{2,1,0:T(8,128)}, u32[]{:S(2)}, u32[]{:S(2)}) collective-permute-start(f32[2,192,384]{2,1,0:T(8,128)} %collective-permute-done.8.refs_2_), channel_id=1, source_target_pairs={{0,2},{1,3},{2,0},{3,1},{4,6},{5,7},{6,4},{7,5},{8,10},{9,11},{10,... | collective-permute-start | bytes 1769480 | tf_op jit(solution)/shard_map/ppermute | solution.py:285
  73.2 2.3 collective-permute-start.18
  73.7 2.7 %collective-permute-start.19 = (f32[2,192,384]{2,1,0:T(8,128)}, f32[2,192,384]{2,1,0:T(8,128)S(1)}, u32[]{:S(2)}, u32[]{:S(2)}) collective-permute-start(f32[2,192,384]{2,1,0:T(8,128)} %collective-permute-done.13.refs_7_), channel_id=1, source_target_pairs={{0,2},{1,3},{2,0},{3,1},{4,6},{5,7},{6,4},{7,5},{8,10},{9,11},{10,... | collective-permute-start | bytes 1769480 | tf_op jit(solution)/shard_map/ppermute | solution.py:285
  73.8 3.4 %copy-start.12 = (f32[2,192,384]{2,1,0:T(8,128)}, f32[2,192,384]{2,1,0:T(8,128)S(1)}, u32[]{:S(2)}) copy-start(f32[2,192,384]{2,1,0:T(8,128)S(1)} %collective-permute-done.10.refs_3_) | copy-start | bytes 1769476
  73.8 3.4 %collective-permute-start.20 = (f32[2,192,384]{2,1,0:T(8,128)}, f32[2,192,384]{2,1,0:T(8,128)S(1)}, u32[]{:S(2)}, u32[]{:S(2)}) collective-permute-start(f32[2,192,384]{2,1,0:T(8,128)} %collective-permute-done.14.refs_8_), channel_id=1, source_target_pairs={{0,2},{1,3},{2,0},{3,1},{4,6},{5,7},{6,4},{7,5},{8,10},{9,11},{10,... | collective-permute-start | bytes 1769480 | tf_op jit(solution)/shard_map/ppermute | solution.py:285
  75.5 1.7 copy-start.13
  76.4 0.9 copy-start.14
  77.2 0.8 copy-start.15
  96.8 19.0 %collective-permute-start.21 = (f32[5,96,384]{2,1,0:T(8,128)}, f32[5,96,384]{2,1,0:T(8,128)S(1)}, u32[]{:S(2)}, u32[]{:S(2)}) collective-permute-start(f32[5,96,384]{2,1,0:T(8,128)} %get-tuple-element.70), channel_id=1, source_target_pairs={{0,4},{1,5},{2,6},{3,7},{4,0},{5,1},{6,2},{7,3},{8,12},{9,13},{10,... | collective-permute-start | bytes 2211848 | tf_op jit(solution)/shard_map/ppermute | solution.py:285
  97.4 19.6 %collective-permute-start.22 = (f32[5,96,384]{2,1,0:T(8,128)}, f32[5,96,384]{2,1,0:T(8,128)S(1)}, u32[]{:S(2)}, u32[]{:S(2)}) collective-permute-start(f32[5,96,384]{2,1,0:T(8,128)} %get-tuple-element.71), channel_id=1, source_target_pairs={{0,1},{1,0},{2,3},{3,2},{4,5},{5,4},{6,7},{7,6},{8,9},{9,8},{10,11... | collective-permute-start | bytes 2211848 | tf_op jit(solution)/shard_map/ppermute | solution.py:285
  97.9 34.9 %collective-permute-start.23 = (f32[5,96,384]{2,1,0:T(8,128)}, f32[5,96,384]{2,1,0:T(8,128)S(1)}, u32[]{:S(2)}, u32[]{:S(2)}) collective-permute-start(f32[5,96,384]{2,1,0:T(8,128)} %get-tuple-element.72), channel_id=1, source_target_pairs={{0,5},{1,4},{2,7},{3,6},{4,1},{5,0},{6,3},{7,2},{8,13},{9,12},{10,... | collective-permute-start | bytes 2211848 | tf_op jit(solution)/shard_map/ppermute | solution.py:285
  100.3 34.4 %collective-permute-start.24 = (f32[5,96,384]{2,1,0:T(8,128)}, f32[5,96,384]{2,1,0:T(8,128)S(1)}, u32[]{:S(2)}, u32[]{:S(2)}) collective-permute-start(f32[5,96,384]{2,1,0:T(8,128)} %get-tuple-element.69.refs_2_), channel_id=1, source_target_pairs={{0,2},{1,3},{2,0},{3,1},{4,6},{5,7},{6,4},{7,5},{8,10},{9,11},{10,... | collective-permute-start | bytes 2211848 | tf_op jit(solution)/shard_map/ppermute | solution.py:285
  115.8 19.3 %copy-start.8 = (f32[5,96,384]{2,1,0:T(8,128)}, f32[5,96,384]{2,1,0:T(8,128)S(1)}, u32[]{:S(2)}) copy-start(f32[5,96,384]{2,1,0:T(8,128)S(1)} %collective-permute-done.21.refs_3_) | copy-start | bytes 2211844
  115.8 18.9 %collective-permute-start.25 = (f32[5,96,384]{2,1,0:T(8,128)S(1)}, f32[5,96,384]{2,1,0:T(8,128)}, u32[]{:S(2)}, u32[]{:S(2)}) collective-permute-start(f32[5,96,384]{2,1,0:T(8,128)S(1)} %collective-permute-done.21.refs_3_), channel_id=1, source_target_pairs={{0,2},{1,3},{2,0},{3,1},{4,6},{5,7},{6,4},{7,5},{8,10},{9,11},{10,... | collective-permute-start | bytes 2211848 | tf_op jit(solution)/shard_map/ppermute | solution.py:285
  116.9 18.2 %copy-start.9 = (f32[5,96,384]{2,1,0:T(8,128)}, f32[5,96,384]{2,1,0:T(8,128)S(1)}, u32[]{:S(2)}) copy-start(f32[5,96,384]{2,1,0:T(8,128)S(1)} %collective-permute-done.22.refs_4_) | copy-start | bytes 2211844
  116.9 17.8 %collective-permute-start.26 = (f32[5,96,384]{2,1,0:T(8,128)S(1)}, f32[5,96,384]{2,1,0:T(8,128)}, u32[]{:S(2)}, u32[]{:S(2)}) collective-permute-start(f32[5,96,384]{2,1,0:T(8,128)S(1)} %collective-permute-done.22.refs_4_), channel_id=1, source_target_pairs={{0,2},{1,3},{2,0},{3,1},{4,6},{5,7},{6,4},{7,5},{8,10},{9,11},{10,... | collective-permute-start | bytes 2211848 | tf_op jit(solution)/shard_map/ppermute | solution.py:285
  132.8 2.4 %copy-start.10 = (f32[5,96,384]{2,1,0:T(8,128)}, f32[5,96,384]{2,1,0:T(8,128)S(1)}, u32[]{:S(2)}) copy-start(f32[5,96,384]{2,1,0:T(8,128)S(1)} %collective-permute-done.23.refs_5_) | copy-start | bytes 2211844
  132.8 2.3 %collective-permute-start.27 = (f32[5,96,384]{2,1,0:T(8,128)S(1)}, f32[5,96,384]{2,1,0:T(8,128)}, u32[]{:S(2)}, u32[]{:S(2)}) collective-permute-start(f32[5,96,384]{2,1,0:T(8,128)S(1)} %collective-permute-done.23.refs_5_), channel_id=1, source_target_pairs={{0,2},{1,3},{2,0},{3,1},{4,6},{5,7},{6,4},{7,5},{8,10},{9,11},{10,... | collective-permute-start | bytes 2211848 | tf_op jit(solution)/shard_map/ppermute | solution.py:285
  134.7 0.9 copy-start.11
  167.7 37.7 %collective-permute-start.28 = (f32[384,768]{1,0:T(8,128)}, f32[384,768]{1,0:T(8,128)S(1)}, u32[]{:S(2)}, u32[]{:S(2)}) collective-permute-start(f32[384,768]{1,0:T(8,128)} %get-tuple-element.75), channel_id=1, source_target_pairs={{0,1},{1,0},{2,5},{3,4},{4,3},{5,2},{6,7},{7,6},{8,9},{9,8},{10,13... | collective-permute-start | bytes 3538952 | tf_op jit(solution)/shard_map/ppermute | solution.py:285
  168.4 37.5 %collective-permute-start.29 = (f32[384,768]{1,0:T(8,128)}, f32[384,768]{1,0:T(8,128)S(1)}, u32[]{:S(2)}, u32[]{:S(2)}) collective-permute-start(f32[384,768]{1,0:T(8,128)} %get-tuple-element.76), channel_id=1, source_target_pairs={{0,0},{1,1},{2,4},{3,5},{4,2},{5,3},{6,6},{7,7},{8,8},{9,9},{10,12... | collective-permute-start | bytes 3538952 | tf_op jit(solution)/shard_map/ppermute | solution.py:285
  202.4 26.4 %collective-permute-start.30 = (f32[384,768]{1,0:T(8,128)}, f32[384,768]{1,0:T(8,128)}, u32[]{:S(2)}, u32[]{:S(2)}) collective-permute-start(f32[384,768]{1,0:T(8,128)} %get-tuple-element.77), channel_id=1, source_target_pairs={{0,2},{1,3},{2,6},{3,7},{4,0},{5,1},{6,4},{7,5},{8,10},{9,11},{10,... | collective-permute-start | bytes 3538952 | tf_op jit(solution)/shard_map/ppermute | solution.py:285
  204.3 28.1 %collective-permute-start.31 = (f32[384,768]{1,0:T(8,128)}, f32[384,768]{1,0:T(8,128)S(1)}, u32[]{:S(2)}, u32[]{:S(2)}) collective-permute-start(f32[384,768]{1,0:T(8,128)} %get-tuple-element.78), channel_id=1, source_target_pairs={{0,3},{1,2},{2,7},{3,6},{4,1},{5,0},{6,5},{7,4},{8,11},{9,10},{10,... | collective-permute-start | bytes 3538952 | tf_op jit(solution)/shard_map/ppermute | solution.py:285
  230.1 2.2 copy-start

commit v5 on v4

--- a/solution.py
+++ b/solution.py
@@ -12,6 +12,7 @@
 F32, BF16 = jnp.float32, jnp.bfloat16
 VMEM_LIMIT = 60 << 20
 TILE = 256
+SOME = 2
 
 
 def halves(x):
@@ -49,14 +50,15 @@
     )(v)
 
 
-def green_kernel(merged, first, last, meta, coef, *refs):
+def green_kernel(merged, first, last, step0, meta, coef, *refs):
     refs = list(refs)
     sources = [refs.pop(0) for _ in range(merged or 2)]
     factor = refs.pop(0)
     acc_in = None if first else refs.pop(0)
     outs = [refs.pop(0) for _ in range(coef.shape[0] if last else 1)]
     c_buf, left, right, occ, sem = refs
-    species, step = pl.program_id(0), pl.program_id(1)
+    species, here = pl.program_id(0), pl.program_id(1)
+    step = here + step0
     width = c_buf.shape[2]
     times = factor.shape[1]
     strip = left.shape[0] // times
@@ -69,15 +71,15 @@
                 for k in range(d, merged, 3):
                     rows, part = sources[k].shape[1:]
                     start = pl.multiple_of(meta[k // 3 % 2], 16) + d * size
-                    here = c_buf.at[s, pl.ds(start, rows), pl.ds(k // 6 * part, part)]
-                    copies.append(pltpu.make_async_copy(sources[k].at[s], here, sem.at[s]))
+                    there = c_buf.at[s, pl.ds(start, rows), pl.ds(k // 6 * part, part)]
+                    copies.append(pltpu.make_async_copy(sources[k].at[s], there, sem.at[s]))
             else:
                 rows = pl.ds(pl.multiple_of(meta[2 + d], 16), size)
-                here = c_buf.at[s, pl.ds(d * size, size), :]
-                copies.append(pltpu.make_async_copy(sources[s].at[rows, :], here, sem.at[s]))
+                there = c_buf.at[s, pl.ds(d * size, size), :]
+                copies.append(pltpu.make_async_copy(sources[s].at[rows, :], there, sem.at[s]))
         return copies
 
-    @pl.when(jnp.logical_and(species == 0, step == 0))
+    @pl.when(jnp.logical_and(species == 0, here == 0))
     def _():
         for s in range(2):
             for copy in copies_of(s):
@@ -85,7 +87,7 @@
 
     for s in range(2):
 
-        @pl.when(jnp.logical_and(species == s, step == 0))
+        @pl.when(jnp.logical_and(species == s, here == 0))
         def _(s=s):
             for copy in copies_of(s):
                 copy.wait()
@@ -112,11 +114,11 @@
 
         @pl.when(species == 0)
         def _():
-            occ[step] = green
+            occ[here] = green
 
         @pl.when(species == 1)
         def _():
-            pairs = [occ[step, t] * green[t] for t in range(times)]
+            pairs = [occ[here, t] * green[t] for t in range(times)]
             for n, out in enumerate(outs):
                 total = coef[n, 0] * pairs[0]
                 for t in range(1, times):
@@ -124,12 +126,13 @@
                 out[0] = total
 
 
-def green_call(name, sources, factor, meta, coef, size, acc=None, last=False):
+def green_call(name, sources, factor, meta, coef, size, acc=None, last=False, strips=range(5)):
     _, times, width = factor.shape
     strip = size // 4
     first = acc is None
     merged = 0 if first else len(sources)
-    acc_spec = pl.BlockSpec((1, 1, times, strip, size), lambda s, n, *_: (s, n, 0, 0, 0))
+    n0 = strips[0]
+    acc_spec = pl.BlockSpec((1, 1, times, strip, size), lambda s, n, *_: (s, n + n0, 0, 0, 0))
     part_spec = pl.BlockSpec((1, strip, size), lambda s, n, *_: (s * n, 0, 0))
     args = list(sources) + [factor]
     specs = [pl.BlockSpec(memory_space=pl.ANY)] * len(sources)
@@ -141,23 +144,23 @@
         args.append(acc)
         specs.append(acc_spec)
     if last:
-        out_shape = [jax.ShapeDtypeStruct((5, strip, size), F32)] * coef.shape[0]
+        out_shape = [jax.ShapeDtypeStruct((len(strips), strip, size), F32)] * coef.shape[0]
         out_specs = [part_spec] * coef.shape[0]
     else:
         out_shape = jax.ShapeDtypeStruct((2, 5, times, strip, size), F32)
         out_specs = acc_spec
     return pl.pallas_call(
-        functools.partial(green_kernel, merged, first, last),
+        functools.partial(green_kernel, merged, first, last, n0),
         grid_spec=pltpu.PrefetchScalarGridSpec(
             num_scalar_prefetch=2,
-            grid=(2, 5),
+            grid=(2, len(strips)),
             in_specs=specs,
             out_specs=out_specs,
             scratch_shapes=[
                 pltpu.VMEM((2, 3 * size, width), F32),
                 pltpu.VMEM((times * strip, 3 * width), BF16),
                 pltpu.VMEM((3 * size, 3 * width), BF16),
-                pltpu.VMEM((5 if last else 1, times, strip, size), F32),
+                pltpu.VMEM((len(strips) if last else 1, times, strip, size), F32),
                 pltpu.SemaphoreType.DMA((2,)),
             ],
         ),
@@ -173,23 +176,24 @@
 
 def chain_kernel(block, *refs):
     at, spots = refs[:2]
-    parts, (v_high, v_low, near_ref, far_ref) = refs[2:10], refs[10:14]
-    pf, wh, wl, lh, ll, xf, sem_p, sem_v, sem_r, sem_o = refs[14:]
+    parts, (v_high, v_low, near_ref, far_ref) = refs[2:-14], refs[-14:-10]
+    pf, wh, wl, lh, ll, xf, sem_p, sem_v, sem_r, sem_o = refs[-10:]
     n = pf.shape[0]
     m = lh.shape[1]
     blocks = n // block
-    count, strip, size = parts[0].shape
+    size = parts[0].shape[2]
     row = pl.multiple_of(at[0], 16)
     row_copies = [
         pltpu.make_async_copy(v_high.at[pl.ds(row, m), :], lh.at[0], sem_r.at[0]),
         pltpu.make_async_copy(v_low.at[pl.ds(row, m), :], ll.at[0], sem_r.at[1]),
     ]
     p_copies = []
-    for k, part in enumerate(parts):
-        for t in range(count):
-            i = pl.multiple_of(spots[2 * (k * count + t)], 16)
-            j = pl.multiple_of(spots[2 * (k * count + t) + 1], 128)
-            there = pf.at[pl.ds(i, strip), pl.ds(j, size)]
+    for part in parts:
+        for t in range(part.shape[0]):
+            k = len(p_copies)
+            i = pl.multiple_of(spots[2 * k], 16)
+            j = pl.multiple_of(spots[2 * k + 1], 128)
+            there = pf.at[pl.ds(i, part.shape[1]), pl.ds(j, size)]
             p_copies.append(pltpu.make_async_copy(part.at[t], there, sem_p))
 
     def v_copies(b):
@@ -201,7 +205,7 @@
 
     for copy in p_copies + row_copies:
         copy.start()
-    for copy in p_copies + row_copies:
+    for copy in p_copies:
         copy.wait()
     for b in range(blocks):
         for copy in v_copies(b):
@@ -223,6 +227,9 @@
         return 0
 
     lax.fori_loop(0, n // 128, split_rows, 0)
+
+    for copy in row_copies:
+        copy.wait()
 
     def body(k, _):
         stage, b = lax.div(k, blocks), lax.rem(k, blocks)
@@ -302,7 +309,7 @@
     return together(v, *others)[0]
 
 
-def tables_of(size):
+def tables_of(size, tile_rows):
     strip = size // 4
     devices = [(x, y, c) for y in range(2) for c in range(2) for x in range(2)]
 
@@ -311,11 +318,11 @@
 
     def spots(x, y, c):
         cross = y ^ (1 - x)
-        left = [2 * x + y, 2 * x + y, y, 2 * x, cross]
-        right = [2 * x + y, 2 * x + y, 2 + y, 2 * x + 1, 3 - cross]
-        return [(a * size + t * strip, b * size) for a, b, t in zip(left, right, strips(x, y, c))]
-
-    meta, places = [], []
+        left = [2 * x + y, y, 2 * x, cross]
+        right = [2 * x + y, 2 + y, 2 * x + 1, 3 - cross]
+        return [(a * size + t * strip, b * size) for a, b, t in zip(left, right, strips(x, y, c)[:1] + strips(x, y, c)[2:])]
+
+    meta, places, at = [], [], []
     for x, y, c in devices:
         sets = [2 * x + y, 2 * (1 - x) + y, 2 * x + 1 - y]
         left, right = [0, 0, x, 2 * y, 2 - x], [0, 0, 1 - x, 2 - 2 * y, 1 + x]
@@ -325,11 +332,12 @@
             + [s * size + t * strip for s, t in zip(left, strips(x, y, c))]
             + [s * size for s in right]
         )
+        at.append([[(2 * c + (y ^ e)) * tile_rows, x] for e in range(2)])
         places.append(
             [spots(x ^ dx, y ^ dy, c ^ dc) for dc in range(2) for dx in range(2) for dy in range(2)]
         )
     flat = np.array(places, np.int32).reshape(len(devices), -1)
-    return np.array(meta, np.int32), flat
+    return np.array(meta, np.int32), flat, np.array(at, np.int32)
 
 
 def on_plane(c_occ, c_vir, eps_occ, eps_vir, tau, tweight, omega, coulomb):
@@ -343,7 +351,8 @@
     strip = size // 4
     ways = [(dx, dy) for dx in range(2) for dy in range(2)]
     here = (2 * y + core) * cols_n + x
-    meta, spots = (jnp.array(t)[here] for t in tables_of(size))
+    meta_of, spots_of, at_of = tables_of(size, tile_rows)
+    meta = jnp.array(meta_of)[here]
 
     energies = jnp.stack([eps_occ, -eps_vir])
     arriving = [ring(energies, t) for t in range(1, planes)]
@@ -386,15 +395,25 @@
         green_call("green_first", sets[0], factors[:, :, :part], *common, green),
     )
     rest = sum(sets[1:], []) + with_other_core(near)
-    parts = green_call("green_rest", rest, factors[:, :, part:], *common, green, True)
-
-    parts = [over(p, dx, dy, 0) if dx + dy else p for p, (dx, dy) in zip(parts, ways)]
+    rest = functools.partial(green_call, "green_rest", rest, factors[:, :, part:], *common)
+
+    def to_chips(parts):
+        return [over(p, dx, dy, 0) if dx + dy else p for p, (dx, dy) in zip(parts, ways)]
+
+    some = rest(green, True, range(SOME))
+    more = rest(after(green, *some), True, range(SOME, 5))
+    both = together(*to_chips(some), *more)
+    some, more = both[: len(ways)], both[len(ways) :]
+    here, _ = together(here, more[0])
+    spots, at = jnp.array(spots_of)[here], jnp.array(at_of)[here]
+    more, spots, at = together(to_chips(more), spots, at)
+    some = [p.reshape(1, SOME * strip, size) for p in some]
+    parts = [p for pair in zip(some, more) for p in pair]
     parts += [over(p, 0, 0, 1) for p in parts]
 
     arrivals = []
     for e in range(2):
-        at = jnp.stack([(2 * core + (y ^ e)) * tile_rows, x]).astype(jnp.int32)
-        near, far = chain(at, spots, parts, v_high, v_low, tile_rows, tile_cols)
+        near, far = chain(at[e], spots, parts, v_high, v_low, tile_rows, tile_cols)
         for dx, value in ((1 - e, (near, far)[1 - e]), (e, (near, far)[e])):
             value = move(value, lambda x, y, c, dx=dx, e=e: (x ^ dx, c, y ^ e))
             arrivals.append((2 * (x ^ dx) + (core ^ e), value))

time: 235 us -> 233 us (level)
  waiting for transfers between devices: 74.8 us -> 61 us
  Pallas kernels: 117 us -> 123 us
  starting transfers between devices: 26.9 us -> 31.9 us
    ppermute x26 -> x33, waiting for transfers between devices: 71.8 us -> 58 us  [move(): return lax.ppermute(v, ('row', 'col'), pairs)]
    pallas_call x3 -> x4, Pallas kernels: 44.7 us -> 50.6 us  [green_call(): pl.pallas_call(functools.partial(green_kernel, merged, first, last, n0),...]
    ppermute x26 -> x33, starting transfers between devices: 18.3 us -> 23.3 us  [move(): return lax.ppermute(v, ('row', 'col'), pairs)]
  transfers between devices with their start and end apart: 32 -> 39, of which waited for: 13 -> 13; matrix products, arithmetic and copies ran while one was open for 5% -> 5% of each run, Pallas kernels for 28% -> 34%
where the time goes in v5:
time: 233 us; the launch traced here: 232 us
  Pallas kernels  123 us (53%)
  waiting for transfers between devices  61 us (26%)
  starting transfers between devices  31.9 us (14%)
  local copies, waits for them, and re-layouts  10.9 us (5%)
  other arithmetic  4.94 us (2%)
    pallas_call x2, Pallas kernels, chain(): pl.pallas_call(functools.partial(chain_kernel, cols), in_specs=[smem] * 2...  64 us
    ppermute x33, waiting for transfers between devices, move(): return lax.ppermute(v, ('row', 'col'), pairs)  58 us
    pallas_call x4, Pallas kernels, green_call(): pl.pallas_call(functools.partial(green_kernel, merged, first, last, n0),...  50.6 us
    ppermute x33, starting transfers between devices, move(): return lax.ppermute(v, ('row', 'col'), pairs)  23.3 us
    ppermute x6, starting transfers between devices, ring(): return lax.ppermute(v, 'tm', [(i, (i + steps) % size) for i in range(size)])  8.69 us
    pallas_call x1, Pallas kernels, split(): pl.pallas_call(split_kernel, grid=(4,), in_specs=[spec], out_specs=[spec]...  7.89 us
  transfers between devices with their start and end apart: 39, of which 13 were waited for; matrix products, arithmetic and copies ran while one was open for 5% of the time, Pallas kernels for 34%

profile of v5, /device:TPU:0, one launch (start us, length us, event | category | flops | bytes accessed | tf_op | source)
XLA Modules:
  0.0 231.7 jit_solution(605324068941138120)
XLA Ops:
  0.0 1.1 dynamic-slice_bitcast_fusion
  1.1 3.1 %collective-permute-start = (f32[2,192,384]{2,1,0:T(8,128)S(1)}, f32[2,192,384]{2,1,0:T(8,128)S(1)}, u32[]{:S(2)}, u32[]{:S(2)}) collective-permute-start(f32[2,192,384]{2,1,0:T(8,128)S(1)} %pad_maximum_fusion), channel_id=1, source_target_pairs={{0,8},{8,16},{16,24},{24,0},{1,9},{9,17},{17,25},{25,1},{2,10},{10... | collective-permute-start | bytes 1769480 | tf_op jit(solution)/shard_map/ppermute | solution.py:301
  4.2 0.7 neg.3
  4.9 0.7 stack.35
  5.6 1.6 collective-permute-start.1
  7.2 1.1 collective-permute-start.2
  8.3 2.8 %collective-permute-start.3 = (f32[2,384]{1,0:T(2,128)S(1)}, f32[2,384]{1,0:T(2,128)S(1)}, u32[]{:S(2)}, u32[]{:S(2)}) collective-permute-start(f32[2,384]{1,0:T(2,128)S(1)} %pad_maximum_fusion.4), channel_id=1, source_target_pairs={{0,24},{8,0},{16,8},{24,16},{1,25},{9,1},{17,9},{25,17},{2,26},{10... | collective-permute-start | bytes 9224 | tf_op jit(solution)/shard_map/ppermute | solution.py:301
  11.2 0.8 cosine_multiply_fusion
  12.0 0.8 multiply_exponential_fusion.3
  12.8 7.9 %split_coulomb.1 = (bf16[1536,1536]{1,0:T(8,128)(2,1)}, bf16[1536,1536]{1,0:T(8,128)(2,1)}) custom-call(f32[1536,1536]{1,0:T(8,128)} %v_ref.1), custom_call_target="tpu_custom_call" | custom-call | tf_op jit(solution)/shard_map/split_coulomb/pallas_call | solution.py:42
  20.7 1.6 collective-permute-start.4
  22.3 1.5 collective-permute-start.5
  23.8 1.3 fusion.1.meta
  25.1 0.6 maximum_multiply_fusion.coef
  25.7 0.6 pad_maximum_fusion.3.refs_2_
  26.3 11.8 %green_own.1.refs_7_ = f32[2,5,4,96,384]{4,3,2,1,0:T(8,128)} custom-call(s32[15]{0:T(128)} %fusion.1.meta, f32[4,4]{1,0:T(4,128)} %maximum_multiply_fusion.coef, f32[1536,384]{1,0:T(8,128)} %refs_0_, f32[1536,384]{1,0:T(8,128)} %refs_1_.1, f32[2,4,384]{2,1,0:T(4,128)} %pad_maximum_fusion.3.refs_2_), custom_call_target="tpu_custom_call" | custom-call | flops 3397386240 | bytes 25165824 | tf_op jit(solution)/shard_map/green_own/pallas_call | solution.py:152
  38.2 0.9 collective-permute-done.6.refs_0_
  39.1 0.5 collective-permute-start.7
  39.6 0.5 collective-permute-start.8
  40.2 0.6 collective-permute-start.16
  40.8 11.2 %collective-permute-done.7.refs_1_ = f32[2,192,384]{2,1,0:T(8,128)} collective-permute-done((f32[2,192,384]{2,1,0:T(8,128)}, f32[2,192,384]{2,1,0:T(8,128)}, u32[]{:S(2)}, u32[]{:S(2)}) %collective-permute-start.7) | collective-permute-done | bytes 589856 | tf_op jit(solution)/shard_map/ppermute | solution.py:292
  52.2 2.1 collective-permute-done.9.refs_6_
  54.3 1.5 collective-permute-start.13
  55.7 1.5 collective-permute-start.14
  57.4 0.7 pad_maximum_fusion.2.refs_6_
  58.1 0.4 collective-permute-start.11
  59.1 14.1 %green_first.1.refs_13_ = f32[2,5,4,96,384]{4,3,2,1,0:T(8,128)} custom-call(s32[15]{0:T(128)} %fusion.1.meta, f32[4,4]{1,0:T(4,128)} %maximum_multiply_fusion.coef, f32[2,192,384]{2,1,0:T(8,128)} %copy-done.1, f32[2,192,384]{2,1,0:T(8,128)} %copy-done.2, f32[2,192,384]{2,1,0:T(8,128)} %copy-done.3, ...), custom_call_target="tpu_custom_call", output_to_operand_aliasing={{}: (9, {})} | custom-call | flops 3397386240 | bytes 25165824 | tf_op jit(solution)/shard_map/green_first/pallas_call | solution.py:152
  73.3 0.4 collective-permute-start.18
  73.9 0.4 collective-permute-start.20
  74.3 0.6 pad_maximum_fusion.1.refs_12_
  74.9 0.7 collective-permute-done.18.refs_9_
  75.6 0.8 collective-permute-done.19.refs_10_
  76.4 0.8 collective-permute-done.20.refs_11_
  77.3 0.8 copy-done.11
  78.1 11.0 %green_rest.2 = (f32[2,96,384]{2,1,0:T(8,128)}, f32[2,96,384]{2,1,0:T(8,128)}, f32[2,96,384]{2,1,0:T(8,128)}, f32[2,96,384]{2,1,0:T(8,128)}) custom-call(s32[15]{0:T(128)} %fusion.1.meta, f32[4,4]{1,0:T(4,128)} %maximum_multiply_fusion.coef, f32[2,192,384]{2,1,0:T(8,128)} %collective-permute-done.6.refs_0_, f32[2,192,384]{2,1,0:T(8,128)} %collective-permute-done.7.refs_1_, ...), custom_call_target="tpu_custom_call" | custom-call | flops 6794772480 | bytes 25165824 | tf_op jit(solution)/shard_map/green_rest/pallas_call | solution.py:152
  89.1 0.6 collective-permute-start.21
  89.7 0.5 collective-permute-start.22
  90.2 2.5 %collective-permute-start.23 = (f32[2,96,384]{2,1,0:T(8,128)}, f32[2,96,384]{2,1,0:T(8,128)S(1)}, u32[]{:S(2)}, u32[]{:S(2)}) collective-permute-start(f32[2,96,384]{2,1,0:T(8,128)} %get-tuple-element.92), channel_id=1, source_target_pairs={{0,5},{1,4},{2,7},{3,6},{4,1},{5,0},{6,3},{7,2},{8,13},{9,12},{10,... | collective-permute-start | bytes 884744 | tf_op jit(solution)/shard_map/ppermute | solution.py:292
  92.7 13.7 %green_rest.3 = (f32[3,96,384]{2,1,0:T(8,128)}, f32[3,96,384]{2,1,0:T(8,128)}, f32[3,96,384]{2,1,0:T(8,128)}, f32[3,96,384]{2,1,0:T(8,128)}) custom-call(s32[15]{0:T(128)} %fusion.1.meta, f32[4,4]{1,0:T(4,128)} %maximum_multiply_fusion.coef, f32[2,192,384]{2,1,0:T(8,128)} %collective-permute-done.6.refs_0_, f32[2,192,384]{2,1,0:T(8,128)} %collective-permute-done.7.refs_1_, ...), custom_call_target="tpu_custom_call" | custom-call | flops 6794772480 | bytes 25165824 | tf_op jit(solution)/shard_map/green_rest/pallas_call | solution.py:152
  106.4 0.6 collective-permute-start.24
  107.0 0.5 collective-permute-start.25
  107.5 2.5 %collective-permute-start.26 = (f32[3,96,384]{2,1,0:T(8,128)}, f32[3,96,384]{2,1,0:T(8,128)S(1)}, u32[]{:S(2)}, u32[]{:S(2)}) collective-permute-start(f32[3,96,384]{2,1,0:T(8,128)} %get-tuple-element.101), channel_id=1, source_target_pairs={{0,5},{1,4},{2,7},{3,6},{4,1},{5,0},{6,3},{7,2},{8,13},{9,12},{10,... | collective-permute-start | bytes 1327112 | tf_op jit(solution)/shard_map/ppermute | solution.py:292
  110.0 0.5 collective-permute-start.29
  110.5 8.4 %collective-permute-done.24.refs_5_ = f32[3,96,384]{2,1,0:T(8,128)S(1)} collective-permute-done((f32[3,96,384]{2,1,0:T(8,128)}, f32[3,96,384]{2,1,0:T(8,128)S(1)}, u32[]{:S(2)}, u32[]{:S(2)}) %collective-permute-start.24) | collective-permute-done | bytes 442400 | tf_op jit(solution)/shard_map/ppermute | solution.py:292
  118.9 1.2 fusion.2.refs_1_
  120.2 0.7 fusion
  120.8 8.1 %collective-permute-done.26.refs_9_ = f32[3,96,384]{2,1,0:T(8,128)S(1)} collective-permute-done((f32[3,96,384]{2,1,0:T(8,128)}, f32[3,96,384]{2,1,0:T(8,128)S(1)}, u32[]{:S(2)}, u32[]{:S(2)}) %collective-permute-start.26) | collective-permute-done | bytes 442400 | tf_op jit(solution)/shard_map/ppermute | solution.py:292
  129.0 0.5 collective-permute-start.30
  129.5 0.5 collective-permute-start.34
  130.1 0.6 slice_bitcast_fusion
  130.7 1.7 collective-permute-done.33.refs_16_
  132.4 0.6 collective-permute-done.34.refs_17_
  133.8 32.0 %chain.2 = (f32[384,768]{1,0:T(8,128)}, f32[384,768]{1,0:T(8,128)}) custom-call(s32[2]{0:T(128)} %get-tuple-element.126.refs_0_, s32[64]{0:T(128)} %fusion.2.refs_1_, f32[1,192,384]{2,1,0:T(8,128)} %bitcast.26, f32[3,96,384]{2,1,0:T(8,128)} %get-tuple-element.106.refs_3_, f32[1,192,384]{2,1,0:T(8,128)} %bitcast.30, f32[3,96,384]{2,1,0:T(8,128)} %copy-done.12, ...), custom_call_target="tpu_custom_call" | custom-call | flops 21743271936 | bytes 20971520 | tf_op jit(solution)/shard_map/chain/pallas_call | solution.py:273
  165.8 0.6 collective-permute-start.35
  166.5 1.9 collective-permute-start.36
  168.4 32.0 %chain.3 = (f32[384,768]{1,0:T(8,128)}, f32[384,768]{1,0:T(8,128)}) custom-call(s32[2]{0:T(128)} %get-tuple-element.125.refs_0_, s32[64]{0:T(128)} %fusion.2.refs_1_, f32[1,192,384]{2,1,0:T(8,128)} %bitcast.27, f32[3,96,384]{2,1,0:T(8,128)} %get-tuple-element.106.refs_3_, f32[1,192,384]{2,1,0:T(8,128)} %bitcast.31, f32[3,96,384]{2,1,0:T(8,128)} %copy-done.12, ...), custom_call_target="tpu_custom_call" | custom-call | flops 21743271936 | bytes 20971520 | tf_op jit(solution)/shard_map/chain/pallas_call | solution.py:273
  200.4 1.6 collective-permute-start.37
  202.0 1.2 collective-permute-start.38
  203.2 0.4 broadcast_in_dim.10
  203.7 23.4 %collective-permute-done.37 = f32[384,768]{1,0:T(8,128)} collective-permute-done((f32[384,768]{1,0:T(8,128)}, f32[384,768]{1,0:T(8,128)}, u32[]{:S(2)}, u32[]{:S(2)}) %collective-permute-start.37) | collective-permute-done | bytes 1179680 | tf_op jit(solution)/shard_map/ppermute | solution.py:292
  227.1 1.3 bitcast_dynamic-update-slice_fusion.1
  228.4 1.9 collective-permute-done.38
  230.4 0.2 copy-done
  230.6 1.1 bitcast_dynamic-update-slice_fusion
  (98 shorter events, 2.3 us)
Async XLA Ops:
  1.1 19.6 %collective-permute-start = (f32[2,192,384]{2,1,0:T(8,128)S(1)}, f32[2,192,384]{2,1,0:T(8,128)S(1)}, u32[]{:S(2)}, u32[]{:S(2)}) collective-permute-start(f32[2,192,384]{2,1,0:T(8,128)S(1)} %pad_maximum_fusion), channel_id=1, source_target_pairs={{0,8},{8,16},{16,24},{24,0},{1,9},{9,17},{17,25},{25,1},{2,10},{10... | collective-permute-start | bytes 1769480 | tf_op jit(solution)/shard_map/ppermute | solution.py:301
  5.6 15.1 %collective-permute-start.1 = (f32[2,384]{1,0:T(2,128)S(1)}, f32[2,384]{1,0:T(2,128)S(1)}, u32[]{:S(2)}, u32[]{:S(2)}) collective-permute-start(f32[2,384]{1,0:T(2,128)S(1)} %pad_maximum_fusion.4), channel_id=1, source_target_pairs={{0,8},{8,16},{16,24},{24,0},{1,9},{9,17},{17,25},{25,1},{2,10},{10... | collective-permute-start | bytes 9224 | tf_op jit(solution)/shard_map/ppermute | solution.py:301
  7.2 13.5 %collective-permute-start.2 = (f32[2,384]{1,0:T(2,128)S(1)}, f32[2,384]{1,0:T(2,128)S(1)}, u32[]{:S(2)}, u32[]{:S(2)}) collective-permute-start(f32[2,384]{1,0:T(2,128)S(1)} %pad_maximum_fusion.4), channel_id=1, source_target_pairs={{0,16},{8,24},{16,0},{24,8},{1,17},{9,25},{17,1},{25,9},{2,18},{10... | collective-permute-start | bytes 9224 | tf_op jit(solution)/shard_map/ppermute | solution.py:301
  8.3 12.4 %collective-permute-start.3 = (f32[2,384]{1,0:T(2,128)S(1)}, f32[2,384]{1,0:T(2,128)S(1)}, u32[]{:S(2)}, u32[]{:S(2)}) collective-permute-start(f32[2,384]{1,0:T(2,128)S(1)} %pad_maximum_fusion.4), channel_id=1, source_target_pairs={{0,24},{8,0},{16,8},{24,16},{1,25},{9,1},{17,9},{25,17},{2,26},{10... | collective-permute-start | bytes 9224 | tf_op jit(solution)/shard_map/ppermute | solution.py:301
  20.7 19.5 %copy-start.1 = (f32[2,192,384]{2,1,0:T(8,128)}, f32[2,192,384]{2,1,0:T(8,128)S(1)}, u32[]{:S(2)}) copy-start(f32[2,192,384]{2,1,0:T(8,128)S(1)} %collective-permute-done.refs_0_) | copy-start | bytes 1769476
  20.7 17.4 %collective-permute-start.4 = (f32[2,192,384]{2,1,0:T(8,128)S(1)}, f32[2,192,384]{2,1,0:T(8,128)S(1)}, u32[]{:S(2)}, u32[]{:S(2)}) collective-permute-start(f32[2,192,384]{2,1,0:T(8,128)S(1)} %collective-permute-done.refs_0_), channel_id=1, source_target_pairs={{0,1},{1,0},{2,3},{3,2},{4,5},{5,4},{6,7},{7,6},{8,9},{9,8},{10,11... | collective-permute-start | bytes 1769480 | tf_op jit(solution)/shard_map/ppermute | solution.py:292
  22.3 15.9 %collective-permute-start.5 = (f32[2,192,384]{2,1,0:T(8,128)S(1)}, f32[2,192,384]{2,1,0:T(8,128)S(1)}, u32[]{:S(2)}, u32[]{:S(2)}) collective-permute-start(f32[2,192,384]{2,1,0:T(8,128)S(1)} %collective-permute-done.refs_0_), channel_id=1, source_target_pairs={{0,4},{1,5},{2,6},{3,7},{4,0},{5,1},{6,2},{7,3},{8,12},{9,13},{10,... | collective-permute-start | bytes 1769480 | tf_op jit(solution)/shard_map/ppermute | solution.py:292
  23.8 15.3 %collective-permute-start.6 = (f32[2,192,384]{2,1,0:T(8,128)S(1)}, f32[2,192,384]{2,1,0:T(8,128)}, u32[]{:S(2)}, u32[]{:S(2)}) collective-permute-start(f32[2,192,384]{2,1,0:T(8,128)S(1)} %collective-permute-done.refs_0_), channel_id=1, source_target_pairs={{0,8},{8,16},{16,24},{24,0},{1,9},{9,17},{17,25},{25,1},{2,10},{10... | collective-permute-start | bytes 1769480 | tf_op jit(solution)/shard_map/ppermute | solution.py:301
  26.3 31.0 %copy-start.7 = (f32[4]{0:T(128)S(1)}, f32[4]{0:T(128)}, u32[]{:S(2)}) copy-start(f32[4]{0:T(128)} %param.15) | copy-start | bytes 52
  38.1 20.6 %copy-start.2 = (f32[2,192,384]{2,1,0:T(8,128)}, f32[2,192,384]{2,1,0:T(8,128)S(1)}, u32[]{:S(2)}) copy-start(f32[2,192,384]{2,1,0:T(8,128)S(1)} %collective-permute-done.4.refs_1_) | copy-start | bytes 1769476
  38.2 20.6 %copy-start.3 = (f32[2,192,384]{2,1,0:T(8,128)}, f32[2,192,384]{2,1,0:T(8,128)S(1)}, u32[]{:S(2)}) copy-start(f32[2,192,384]{2,1,0:T(8,128)S(1)} %collective-permute-done.5.refs_2_) | copy-start | bytes 1769476
  39.1 12.8 %collective-permute-start.7 = (f32[2,192,384]{2,1,0:T(8,128)}, f32[2,192,384]{2,1,0:T(8,128)}, u32[]{:S(2)}, u32[]{:S(2)}) collective-permute-start(f32[2,192,384]{2,1,0:T(8,128)} %collective-permute-done.6.refs_0_), channel_id=1, source_target_pairs={{0,1},{1,0},{2,3},{3,2},{4,5},{5,4},{6,7},{7,6},{8,9},{9,8},{10,11... | collective-permute-start | bytes 1769480 | tf_op jit(solution)/shard_map/ppermute | solution.py:292
  39.6 12.6 %collective-permute-start.8 = (f32[2,192,384]{2,1,0:T(8,128)}, f32[2,192,384]{2,1,0:T(8,128)}, u32[]{:S(2)}, u32[]{:S(2)}) collective-permute-start(f32[2,192,384]{2,1,0:T(8,128)} %collective-permute-done.6.refs_0_), channel_id=1, source_target_pairs={{0,4},{1,5},{2,6},{3,7},{4,0},{5,1},{6,2},{7,3},{8,12},{9,13},{10,... | collective-permute-start | bytes 1769480 | tf_op jit(solution)/shard_map/ppermute | solution.py:292
  40.1 14.1 %collective-permute-start.9 = (f32[2,192,384]{2,1,0:T(8,128)}, f32[2,192,384]{2,1,0:T(8,128)}, u32[]{:S(2)}, u32[]{:S(2)}) collective-permute-start(f32[2,192,384]{2,1,0:T(8,128)} %collective-permute-done.6.refs_0_), channel_id=1, source_target_pairs={{0,8},{8,16},{16,24},{24,0},{1,9},{9,17},{17,25},{25,1},{2,10},{10... | collective-permute-start | bytes 1769480 | tf_op jit(solution)/shard_map/ppermute | solution.py:301
  40.2 17.1 %collective-permute-start.15 = (f32[2,192,384]{2,1,0:T(8,128)S(1)}, f32[2,192,384]{2,1,0:T(8,128)S(1)}, u32[]{:S(2)}, u32[]{:S(2)}) collective-permute-start(f32[2,192,384]{2,1,0:T(8,128)S(1)} %collective-permute-done.refs_0_), channel_id=1, source_target_pairs={{0,2},{1,3},{2,0},{3,1},{4,6},{5,7},{6,4},{7,5},{8,10},{9,11},{10,... | collective-permute-start | bytes 1769480 | tf_op jit(solution)/shard_map/ppermute | solution.py:292
  40.2 17.9 %collective-permute-start.16 = (f32[2,192,384]{2,1,0:T(8,128)S(1)}, f32[2,192,384]{2,1,0:T(8,128)S(1)}, u32[]{:S(2)}, u32[]{:S(2)}) collective-permute-start(f32[2,192,384]{2,1,0:T(8,128)S(1)} %collective-permute-done.4.refs_1_), channel_id=1, source_target_pairs={{0,2},{1,3},{2,0},{3,1},{4,6},{5,7},{6,4},{7,5},{8,10},{9,11},{10,... | collective-permute-start | bytes 1769480 | tf_op jit(solution)/shard_map/ppermute | solution.py:292
  51.9 6.2 %collective-permute-start.17 = (f32[2,192,384]{2,1,0:T(8,128)S(1)}, f32[2,192,384]{2,1,0:T(8,128)S(1)}, u32[]{:S(2)}, u32[]{:S(2)}) collective-permute-start(f32[2,192,384]{2,1,0:T(8,128)S(1)} %collective-permute-done.5.refs_2_), channel_id=1, source_target_pairs={{0,2},{1,3},{2,0},{3,1},{4,6},{5,7},{6,4},{7,5},{8,10},{9,11},{10,... | collective-permute-start | bytes 1769480 | tf_op jit(solution)/shard_map/ppermute | solution.py:292
  54.3 19.0 %collective-permute-start.13 = (f32[2,192,384]{2,1,0:T(8,128)}, f32[2,192,384]{2,1,0:T(8,128)}, u32[]{:S(2)}, u32[]{:S(2)}) collective-permute-start(f32[2,192,384]{2,1,0:T(8,128)} %collective-permute-done.9.refs_6_), channel_id=1, source_target_pairs={{0,1},{1,0},{2,3},{3,2},{4,5},{5,4},{6,7},{7,6},{8,9},{9,8},{10,11... | collective-permute-start | bytes 1769480 | tf_op jit(solution)/shard_map/ppermute | solution.py:292
  55.7 17.6 %collective-permute-start.14 = (f32[2,192,384]{2,1,0:T(8,128)}, f32[2,192,384]{2,1,0:T(8,128)}, u32[]{:S(2)}, u32[]{:S(2)}) collective-permute-start(f32[2,192,384]{2,1,0:T(8,128)} %collective-permute-done.9.refs_6_), channel_id=1, source_target_pairs={{0,4},{1,5},{2,6},{3,7},{4,0},{5,1},{6,2},{7,3},{8,12},{9,13},{10,... | collective-permute-start | bytes 1769480 | tf_op jit(solution)/shard_map/ppermute | solution.py:292
  57.3 1.4 copy-start.4
  57.3 16.6 %collective-permute-start.10 = (f32[2,192,384]{2,1,0:T(8,128)}, f32[2,192,384]{2,1,0:T(8,128)S(1)}, u32[]{:S(2)}, u32[]{:S(2)}) collective-permute-start(f32[2,192,384]{2,1,0:T(8,128)} %collective-permute-done.6.refs_0_), channel_id=1, source_target_pairs={{0,2},{1,3},{2,0},{3,1},{4,6},{5,7},{6,4},{7,5},{8,10},{9,11},{10,... | collective-permute-start | bytes 1769480 | tf_op jit(solution)/shard_map/ppermute | solution.py:292
  58.1 0.8 copy-start.5
  58.1 1.0 copy-start.6
  58.1 16.7 %collective-permute-start.11 = (f32[2,192,384]{2,1,0:T(8,128)}, f32[2,192,384]{2,1,0:T(8,128)}, u32[]{:S(2)}, u32[]{:S(2)}) collective-permute-start(f32[2,192,384]{2,1,0:T(8,128)} %collective-permute-done.7.refs_1_), channel_id=1, source_target_pairs={{0,2},{1,3},{2,0},{3,1},{4,6},{5,7},{6,4},{7,5},{8,10},{9,11},{10,... | collective-permute-start | bytes 1769480 | tf_op jit(solution)/shard_map/ppermute | solution.py:292
  58.6 16.3 %collective-permute-start.12 = (f32[2,192,384]{2,1,0:T(8,128)}, f32[2,192,384]{2,1,0:T(8,128)}, u32[]{:S(2)}, u32[]{:S(2)}) collective-permute-start(f32[2,192,384]{2,1,0:T(8,128)} %collective-permute-done.8.refs_2_), channel_id=1, source_target_pairs={{0,2},{1,3},{2,0},{3,1},{4,6},{5,7},{6,4},{7,5},{8,10},{9,11},{10,... | collective-permute-start | bytes 1769480 | tf_op jit(solution)/shard_map/ppermute | solution.py:292
  73.3 2.3 collective-permute-start.18
  73.7 2.7 %collective-permute-start.19 = (f32[2,192,384]{2,1,0:T(8,128)}, f32[2,192,384]{2,1,0:T(8,128)S(1)}, u32[]{:S(2)}, u32[]{:S(2)}) collective-permute-start(f32[2,192,384]{2,1,0:T(8,128)} %collective-permute-done.13.refs_7_), channel_id=1, source_target_pairs={{0,2},{1,3},{2,0},{3,1},{4,6},{5,7},{6,4},{7,5},{8,10},{9,11},{10,... | collective-permute-start | bytes 1769480 | tf_op jit(solution)/shard_map/ppermute | solution.py:292
  73.9 3.4 %copy-start.8 = (f32[2,192,384]{2,1,0:T(8,128)}, f32[2,192,384]{2,1,0:T(8,128)S(1)}, u32[]{:S(2)}) copy-start(f32[2,192,384]{2,1,0:T(8,128)S(1)} %collective-permute-done.10.refs_3_) | copy-start | bytes 1769476
  73.9 3.4 %collective-permute-start.20 = (f32[2,192,384]{2,1,0:T(8,128)}, f32[2,192,384]{2,1,0:T(8,128)S(1)}, u32[]{:S(2)}, u32[]{:S(2)}) collective-permute-start(f32[2,192,384]{2,1,0:T(8,128)} %collective-permute-done.14.refs_8_), channel_id=1, source_target_pairs={{0,2},{1,3},{2,0},{3,1},{4,6},{5,7},{6,4},{7,5},{8,10},{9,11},{10,... | collective-permute-start | bytes 1769480 | tf_op jit(solution)/shard_map/ppermute | solution.py:292
  75.6 1.7 copy-start.9
  76.4 0.9 copy-start.10
  77.3 0.8 copy-start.11
  89.1 17.3 %collective-permute-start.21 = (f32[2,96,384]{2,1,0:T(8,128)}, f32[2,96,384]{2,1,0:T(8,128)S(1)}, u32[]{:S(2)}, u32[]{:S(2)}) collective-permute-start(f32[2,96,384]{2,1,0:T(8,128)} %get-tuple-element.90), channel_id=1, source_target_pairs={{0,4},{1,5},{2,6},{3,7},{4,0},{5,1},{6,2},{7,3},{8,12},{9,13},{10,... | collective-permute-start | bytes 884744 | tf_op jit(solution)/shard_map/ppermute | solution.py:292
  89.7 16.7 %collective-permute-start.22 = (f32[2,96,384]{2,1,0:T(8,128)}, f32[2,96,384]{2,1,0:T(8,128)S(1)}, u32[]{:S(2)}, u32[]{:S(2)}) collective-permute-start(f32[2,96,384]{2,1,0:T(8,128)} %get-tuple-element.91), channel_id=1, source_target_pairs={{0,1},{1,0},{2,3},{3,2},{4,5},{5,4},{6,7},{7,6},{8,9},{9,8},{10,11... | collective-permute-start | bytes 884744 | tf_op jit(solution)/shard_map/ppermute | solution.py:292
  90.2 16.2 %collective-permute-start.23 = (f32[2,96,384]{2,1,0:T(8,128)}, f32[2,96,384]{2,1,0:T(8,128)S(1)}, u32[]{:S(2)}, u32[]{:S(2)}) collective-permute-start(f32[2,96,384]{2,1,0:T(8,128)} %get-tuple-element.92), channel_id=1, source_target_pairs={{0,5},{1,4},{2,7},{3,6},{4,1},{5,0},{6,3},{7,2},{8,13},{9,12},{10,... | collective-permute-start | bytes 884744 | tf_op jit(solution)/shard_map/ppermute | solution.py:292
  92.7 17.3 %copy-start.19 = (f32[2,96,384]{2,1,0:T(8,128)S(1)}, f32[2,96,384]{2,1,0:T(8,128)}, u32[]{:S(2)}) copy-start(f32[2,96,384]{2,1,0:T(8,128)} %get-tuple-element.105) | copy-start | bytes 884740
  106.4 26.7 %copy-start.20 = (f32[2,96,384]{2,1,0:T(8,128)}, f32[2,96,384]{2,1,0:T(8,128)S(1)}, u32[]{:S(2)}) copy-start(f32[2,96,384]{2,1,0:T(8,128)S(1)} %collective-permute-done.21) | copy-start | bytes 884740
  106.4 26.7 %copy-start.21 = (f32[2,96,384]{2,1,0:T(8,128)}, f32[2,96,384]{2,1,0:T(8,128)S(1)}, u32[]{:S(2)}) copy-start(f32[2,96,384]{2,1,0:T(8,128)S(1)} %collective-permute-done.22) | copy-start | bytes 884740
  106.4 3.6 %copy-start.22 = (f32[2,96,384]{2,1,0:T(8,128)}, f32[2,96,384]{2,1,0:T(8,128)S(1)}, u32[]{:S(2)}) copy-start(f32[2,96,384]{2,1,0:T(8,128)S(1)} %collective-permute-done.23) | copy-start | bytes 884740
  106.4 12.5 %collective-permute-start.24 = (f32[3,96,384]{2,1,0:T(8,128)}, f32[3,96,384]{2,1,0:T(8,128)S(1)}, u32[]{:S(2)}, u32[]{:S(2)}) collective-permute-start(f32[3,96,384]{2,1,0:T(8,128)} %get-tuple-element.99), channel_id=1, source_target_pairs={{0,4},{1,5},{2,6},{3,7},{4,0},{5,1},{6,2},{7,3},{8,12},{9,13},{10,... | collective-permute-start | bytes 1327112 | tf_op jit(solution)/shard_map/ppermute | solution.py:292
  107.0 13.9 %collective-permute-start.25 = (f32[3,96,384]{2,1,0:T(8,128)}, f32[3,96,384]{2,1,0:T(8,128)S(1)}, u32[]{:S(2)}, u32[]{:S(2)}) collective-permute-start(f32[3,96,384]{2,1,0:T(8,128)} %get-tuple-element.100), channel_id=1, source_target_pairs={{0,1},{1,0},{2,3},{3,2},{4,5},{5,4},{6,7},{7,6},{8,9},{9,8},{10,11... | collective-permute-start | bytes 1327112 | tf_op jit(solution)/shard_map/ppermute | solution.py:292
  107.5 21.4 %collective-permute-start.26 = (f32[3,96,384]{2,1,0:T(8,128)}, f32[3,96,384]{2,1,0:T(8,128)S(1)}, u32[]{:S(2)}, u32[]{:S(2)}) collective-permute-start(f32[3,96,384]{2,1,0:T(8,128)} %get-tuple-element.101), channel_id=1, source_target_pairs={{0,5},{1,4},{2,7},{3,6},{4,1},{5,0},{6,3},{7,2},{8,13},{9,12},{10,... | collective-permute-start | bytes 1327112 | tf_op jit(solution)/shard_map/ppermute | solution.py:292
  110.0 19.5 %collective-permute-start.27 = (f32[1,192,384]{2,1,0:T(8,128)S(1)}, f32[1,192,384]{2,1,0:T(8,128)}, u32[]{:S(2)}, u32[]{:S(2)}) collective-permute-start(f32[1,192,384]{2,1,0:T(8,128)S(1)} %bitcast.28), channel_id=1, source_target_pairs={{0,2},{1,3},{2,0},{3,1},{4,6},{5,7},{6,4},{7,5},{8,10},{9,11},{10,... | collective-permute-start | bytes 884744 | tf_op jit(solution)/shard_map/ppermute | solution.py:292
  110.0 19.5 %collective-permute-start.29 = (f32[1,192,384]{2,1,0:T(8,128)S(1)}, f32[1,192,384]{2,1,0:T(8,128)}, u32[]{:S(2)}, u32[]{:S(2)}) collective-permute-start(f32[1,192,384]{2,1,0:T(8,128)S(1)} %bitcast.29), channel_id=1, source_target_pairs={{0,2},{1,3},{2,0},{3,1},{4,6},{5,7},{6,4},{7,5},{8,10},{9,11},{10,... | collective-permute-start | bytes 884744 | tf_op jit(solution)/shard_map/ppermute | solution.py:292
  118.9 14.2 %copy-start.12 = (f32[3,96,384]{2,1,0:T(8,128)}, f32[3,96,384]{2,1,0:T(8,128)S(1)}, u32[]{:S(2)}) copy-start(f32[3,96,384]{2,1,0:T(8,128)S(1)} %collective-permute-done.24.refs_5_) | copy-start | bytes 1327108
  118.9 11.1 %collective-permute-start.31 = (f32[1,192,384]{2,1,0:T(8,128)S(1)}, f32[1,192,384]{2,1,0:T(8,128)S(1)}, u32[]{:S(2)}, u32[]{:S(2)}) collective-permute-start(f32[1,192,384]{2,1,0:T(8,128)S(1)} %bitcast.32), channel_id=1, source_target_pairs={{0,2},{1,3},{2,0},{3,1},{4,6},{5,7},{6,4},{7,5},{8,10},{9,11},{10,... | collective-permute-start | bytes 884744 | tf_op jit(solution)/shard_map/ppermute | solution.py:292
  120.8 12.3 %copy-start.13 = (f32[3,96,384]{2,1,0:T(8,128)}, f32[3,96,384]{2,1,0:T(8,128)S(1)}, u32[]{:S(2)}) copy-start(f32[3,96,384]{2,1,0:T(8,128)S(1)} %collective-permute-done.25.refs_7_) | copy-start | bytes 1327108
  129.0 4.2 %copy-start.14 = (f32[3,96,384]{2,1,0:T(8,128)}, f32[3,96,384]{2,1,0:T(8,128)S(1)}, u32[]{:S(2)}) copy-start(f32[3,96,384]{2,1,0:T(8,128)S(1)} %collective-permute-done.26.refs_9_) | copy-start | bytes 1327108
  129.0 3.4 %collective-permute-start.28 = (f32[3,96,384]{2,1,0:T(8,128)}, f32[3,96,384]{2,1,0:T(8,128)S(1)}, u32[]{:S(2)}, u32[]{:S(2)}) collective-permute-start(f32[3,96,384]{2,1,0:T(8,128)} %get-tuple-element.106.refs_3_), channel_id=1, source_target_pairs={{0,2},{1,3},{2,0},{3,1},{4,6},{5,7},{6,4},{7,5},{8,10},{9,11},{10,... | collective-permute-start | bytes 1327112 | tf_op jit(solution)/shard_map/ppermute | solution.py:292
  129.0 3.4 %collective-permute-start.30 = (f32[3,96,384]{2,1,0:T(8,128)S(1)}, f32[3,96,384]{2,1,0:T(8,128)S(1)}, u32[]{:S(2)}, u32[]{:S(2)}) collective-permute-start(f32[3,96,384]{2,1,0:T(8,128)S(1)} %collective-permute-done.24.refs_5_), channel_id=1, source_target_pairs={{0,2},{1,3},{2,0},{3,1},{4,6},{5,7},{6,4},{7,5},{8,10},{9,11},{10,... | collective-permute-start | bytes 1327112 | tf_op jit(solution)/shard_map/ppermute | solution.py:292
  129.5 3.0 %collective-permute-start.32 = (f32[3,96,384]{2,1,0:T(8,128)S(1)}, f32[3,96,384]{2,1,0:T(8,128)S(1)}, u32[]{:S(2)}, u32[]{:S(2)}) collective-permute-start(f32[3,96,384]{2,1,0:T(8,128)S(1)} %collective-permute-done.25.refs_7_), channel_id=1, source_target_pairs={{0,2},{1,3},{2,0},{3,1},{4,6},{5,7},{6,4},{7,5},{8,10},{9,11},{10,... | collective-permute-start | bytes 1327112 | tf_op jit(solution)/shard_map/ppermute | solution.py:292
  129.5 3.6 %collective-permute-start.34 = (f32[3,96,384]{2,1,0:T(8,128)S(1)}, f32[3,96,384]{2,1,0:T(8,128)S(1)}, u32[]{:S(2)}, u32[]{:S(2)}) collective-permute-start(f32[3,96,384]{2,1,0:T(8,128)S(1)} %collective-permute-done.26.refs_9_), channel_id=1, source_target_pairs={{0,2},{1,3},{2,0},{3,1},{4,6},{5,7},{6,4},{7,5},{8,10},{9,11},{10,... | collective-permute-start | bytes 1327112 | tf_op jit(solution)/shard_map/ppermute | solution.py:292
  130.0 3.1 %copy-start.23 = (f32[1,192,384]{2,1,0:T(8,128)}, f32[1,192,384]{2,1,0:T(8,128)S(1)}, u32[]{:S(2)}) copy-start(f32[1,192,384]{2,1,0:T(8,128)S(1)} %collective-permute-done.31.refs_14_) | copy-start | bytes 884740
  130.0 2.4 %collective-permute-start.33 = (f32[1,192,384]{2,1,0:T(8,128)}, f32[1,192,384]{2,1,0:T(8,128)S(1)}, u32[]{:S(2)}, u32[]{:S(2)}) collective-permute-start(f32[1,192,384]{2,1,0:T(8,128)} %bitcast.35), channel_id=1, source_target_pairs={{0,2},{1,3},{2,0},{3,1},{4,6},{5,7},{6,4},{7,5},{8,10},{9,11},{10,... | collective-permute-start | bytes 884744 | tf_op jit(solution)/shard_map/ppermute | solution.py:292
  132.4 0.7 copy-start.24
  132.4 0.9 copy-start.15
  132.4 1.0 copy-start.16
  132.4 1.2 copy-start.17
  133.1 0.8 copy-start.18
  165.8 37.3 %collective-permute-start.35 = (f32[384,768]{1,0:T(8,128)}, f32[384,768]{1,0:T(8,128)S(1)}, u32[]{:S(2)}, u32[]{:S(2)}) collective-permute-start(f32[384,768]{1,0:T(8,128)} %get-tuple-element.115), channel_id=1, source_target_pairs={{0,1},{1,0},{2,5},{3,4},{4,3},{5,2},{6,7},{7,6},{8,9},{9,8},{10,13... | collective-permute-start | bytes 3538952 | tf_op jit(solution)/shard_map/ppermute | solution.py:292
  166.5 37.1 %collective-permute-start.36 = (f32[384,768]{1,0:T(8,128)}, f32[384,768]{1,0:T(8,128)S(1)}, u32[]{:S(2)}, u32[]{:S(2)}) collective-permute-start(f32[384,768]{1,0:T(8,128)} %get-tuple-element.116), channel_id=1, source_target_pairs={{0,0},{1,1},{2,4},{3,5},{4,2},{5,3},{6,6},{7,7},{8,8},{9,9},{10,12... | collective-permute-start | bytes 3538952 | tf_op jit(solution)/shard_map/ppermute | solution.py:292
  200.4 26.7 %collective-permute-start.37 = (f32[384,768]{1,0:T(8,128)}, f32[384,768]{1,0:T(8,128)}, u32[]{:S(2)}, u32[]{:S(2)}) collective-permute-start(f32[384,768]{1,0:T(8,128)} %get-tuple-element.117), channel_id=1, source_target_pairs={{0,2},{1,3},{2,6},{3,7},{4,0},{5,1},{6,4},{7,5},{8,10},{9,11},{10,... | collective-permute-start | bytes 3538952 | tf_op jit(solution)/shard_map/ppermute | solution.py:292
  202.0 28.4 %collective-permute-start.38 = (f32[384,768]{1,0:T(8,128)}, f32[384,768]{1,0:T(8,128)S(1)}, u32[]{:S(2)}, u32[]{:S(2)}) collective-permute-start(f32[384,768]{1,0:T(8,128)} %get-tuple-element.118), channel_id=1, source_target_pairs={{0,3},{1,2},{2,7},{3,6},{4,1},{5,0},{6,5},{7,4},{8,11},{9,10},{10,... | collective-permute-start | bytes 3538952 | tf_op jit(solution)/shard_map/ppermute | solution.py:292
  228.4 2.2 copy-start

commit v6 on v5

--- a/solution.py
+++ b/solution.py
@@ -79,18 +79,18 @@
                 copies.append(pltpu.make_async_copy(sources[s].at[rows, :], there, sem.at[s]))
         return copies
 
-    @pl.when(jnp.logical_and(species == 0, here == 0))
-    def _():
-        for s in range(2):
-            for copy in copies_of(s):
-                copy.start()
-
     for s in range(2):
 
         @pl.when(jnp.logical_and(species == s, here == 0))
         def _(s=s):
+            if s == 0:
+                for copy in copies_of(0):
+                    copy.start()
             for copy in copies_of(s):
                 copy.wait()
+            if s == 0:
+                for copy in copies_of(1):
+                    copy.start()
             high, low = halves(c_buf[s])
             right[:, :width] = high
             right[:, width : 2 * width] = high

time: 233 us -> 233 us (level)
  no operation moved by 1% of the time
where the time goes in v6:
time: 233 us; the launch traced here: 232 us
  Pallas kernels  123 us (53%)
  waiting for transfers between devices  61 us (26%)
  starting transfers between devices  32 us (14%)
  local copies, waits for them, and re-layouts  10.9 us (5%)
  other arithmetic  4.94 us (2%)
    pallas_call x2, Pallas kernels, chain(): pl.pallas_call(functools.partial(chain_kernel, cols), in_specs=[smem] * 2...  64 us
    ppermute x33, waiting for transfers between devices, move(): return lax.ppermute(v, ('row', 'col'), pairs)  58 us
    pallas_call x4, Pallas kernels, green_call(): pl.pallas_call(functools.partial(green_kernel, merged, first, last, n0),...  50.7 us
    ppermute x33, starting transfers between devices, move(): return lax.ppermute(v, ('row', 'col'), pairs)  23.3 us
    ppermute x6, starting transfers between devices, ring(): return lax.ppermute(v, 'tm', [(i, (i + steps) % size) for i in range(size)])  8.69 us
    pallas_call x1, Pallas kernels, split(): pl.pallas_call(split_kernel, grid=(4,), in_specs=[spec], out_specs=[spec]...  7.89 us
  transfers between devices with their start and end apart: 39, of which 13 were waited for; matrix products, arithmetic and copies ran while one was open for 5% of the time, Pallas kernels for 34%

profile of v6, /device:TPU:0, one launch (start us, length us, event | category | flops | bytes accessed | tf_op | source)
XLA Modules:
  0.0 231.8 jit_solution(12569203746824639244)
XLA Ops:
  0.0 1.1 dynamic-slice_bitcast_fusion
  1.1 3.1 %collective-permute-start = (f32[2,192,384]{2,1,0:T(8,128)S(1)}, f32[2,192,384]{2,1,0:T(8,128)S(1)}, u32[]{:S(2)}, u32[]{:S(2)}) collective-permute-start(f32[2,192,384]{2,1,0:T(8,128)S(1)} %pad_maximum_fusion), channel_id=1, source_target_pairs={{0,8},{8,16},{16,24},{24,0},{1,9},{9,17},{17,25},{25,1},{2,10},{10... | collective-permute-start | bytes 1769480 | tf_op jit(solution)/shard_map/ppermute | solution.py:301
  4.2 0.7 neg.3
  4.9 0.7 stack.35
  5.6 1.6 collective-permute-start.1
  7.2 1.1 collective-permute-start.2
  8.3 2.8 %collective-permute-start.3 = (f32[2,384]{1,0:T(2,128)S(1)}, f32[2,384]{1,0:T(2,128)S(1)}, u32[]{:S(2)}, u32[]{:S(2)}) collective-permute-start(f32[2,384]{1,0:T(2,128)S(1)} %pad_maximum_fusion.4), channel_id=1, source_target_pairs={{0,24},{8,0},{16,8},{24,16},{1,25},{9,1},{17,9},{25,17},{2,26},{10... | collective-permute-start | bytes 9224 | tf_op jit(solution)/shard_map/ppermute | solution.py:301
  11.2 0.8 cosine_multiply_fusion
  12.0 0.8 multiply_exponential_fusion.3
  12.8 7.9 %split_coulomb.1 = (bf16[1536,1536]{1,0:T(8,128)(2,1)}, bf16[1536,1536]{1,0:T(8,128)(2,1)}) custom-call(f32[1536,1536]{1,0:T(8,128)} %v_ref.1), custom_call_target="tpu_custom_call" | custom-call | tf_op jit(solution)/shard_map/split_coulomb/pallas_call | solution.py:42
  20.7 1.6 collective-permute-start.4
  22.3 1.5 collective-permute-start.5
  23.8 1.3 fusion.1.meta
  25.1 0.6 maximum_multiply_fusion.coef
  25.7 0.6 pad_maximum_fusion.3.refs_2_
  26.3 11.8 %green_own.1.refs_7_ = f32[2,5,4,96,384]{4,3,2,1,0:T(8,128)} custom-call(s32[15]{0:T(128)} %fusion.1.meta, f32[4,4]{1,0:T(4,128)} %maximum_multiply_fusion.coef, f32[1536,384]{1,0:T(8,128)} %refs_0_, f32[1536,384]{1,0:T(8,128)} %refs_1_.1, f32[2,4,384]{2,1,0:T(4,128)} %pad_maximum_fusion.3.refs_2_), custom_call_target="tpu_custom_call" | custom-call | flops 3397386240 | bytes 25165824 | tf_op jit(solution)/shard_map/green_own/pallas_call | solution.py:152
  38.2 0.9 collective-permute-done.6.refs_0_
  39.1 0.5 collective-permute-start.7
  39.6 0.5 collective-permute-start.8
  40.2 0.6 collective-permute-start.16
  40.8 11.2 %collective-permute-done.7.refs_1_ = f32[2,192,384]{2,1,0:T(8,128)} collective-permute-done((f32[2,192,384]{2,1,0:T(8,128)}, f32[2,192,384]{2,1,0:T(8,128)}, u32[]{:S(2)}, u32[]{:S(2)}) %collective-permute-start.7) | collective-permute-done | bytes 589856 | tf_op jit(solution)/shard_map/ppermute | solution.py:292
  52.2 2.1 collective-permute-done.9.refs_6_
  54.3 1.5 collective-permute-start.13
  55.7 1.5 collective-permute-start.14
  57.4 0.7 pad_maximum_fusion.2.refs_6_
  58.1 0.4 collective-permute-start.11
  59.1 14.2 %green_first.1.refs_13_ = f32[2,5,4,96,384]{4,3,2,1,0:T(8,128)} custom-call(s32[15]{0:T(128)} %fusion.1.meta, f32[4,4]{1,0:T(4,128)} %maximum_multiply_fusion.coef, f32[2,192,384]{2,1,0:T(8,128)} %copy-done.1, f32[2,192,384]{2,1,0:T(8,128)} %copy-done.2, f32[2,192,384]{2,1,0:T(8,128)} %copy-done.3, ...), custom_call_target="tpu_custom_call", output_to_operand_aliasing={{}: (9, {})} | custom-call | flops 3397386240 | bytes 25165824 | tf_op jit(solution)/shard_map/green_first/pallas_call | solution.py:152
  73.4 0.4 collective-permute-start.18
  73.9 0.4 collective-permute-start.20
  74.3 0.6 pad_maximum_fusion.1.refs_12_
  74.9 0.7 collective-permute-done.18.refs_9_
  75.6 0.8 collective-permute-done.19.refs_10_
  76.5 0.8 collective-permute-done.20.refs_11_
  77.3 0.8 copy-done.11
  78.2 11.0 %green_rest.2 = (f32[2,96,384]{2,1,0:T(8,128)}, f32[2,96,384]{2,1,0:T(8,128)}, f32[2,96,384]{2,1,0:T(8,128)}, f32[2,96,384]{2,1,0:T(8,128)}) custom-call(s32[15]{0:T(128)} %fusion.1.meta, f32[4,4]{1,0:T(4,128)} %maximum_multiply_fusion.coef, f32[2,192,384]{2,1,0:T(8,128)} %collective-permute-done.6.refs_0_, f32[2,192,384]{2,1,0:T(8,128)} %collective-permute-done.7.refs_1_, ...), custom_call_target="tpu_custom_call" | custom-call | flops 6794772480 | bytes 25165824 | tf_op jit(solution)/shard_map/green_rest/pallas_call | solution.py:152
  89.1 0.6 collective-permute-start.21
  89.7 0.5 collective-permute-start.22
  90.3 2.5 %collective-permute-start.23 = (f32[2,96,384]{2,1,0:T(8,128)}, f32[2,96,384]{2,1,0:T(8,128)S(1)}, u32[]{:S(2)}, u32[]{:S(2)}) collective-permute-start(f32[2,96,384]{2,1,0:T(8,128)} %get-tuple-element.92), channel_id=1, source_target_pairs={{0,5},{1,4},{2,7},{3,6},{4,1},{5,0},{6,3},{7,2},{8,13},{9,12},{10,... | collective-permute-start | bytes 884744 | tf_op jit(solution)/shard_map/ppermute | solution.py:292
  92.7 13.7 %green_rest.3 = (f32[3,96,384]{2,1,0:T(8,128)}, f32[3,96,384]{2,1,0:T(8,128)}, f32[3,96,384]{2,1,0:T(8,128)}, f32[3,96,384]{2,1,0:T(8,128)}) custom-call(s32[15]{0:T(128)} %fusion.1.meta, f32[4,4]{1,0:T(4,128)} %maximum_multiply_fusion.coef, f32[2,192,384]{2,1,0:T(8,128)} %collective-permute-done.6.refs_0_, f32[2,192,384]{2,1,0:T(8,128)} %collective-permute-done.7.refs_1_, ...), custom_call_target="tpu_custom_call" | custom-call | flops 6794772480 | bytes 25165824 | tf_op jit(solution)/shard_map/green_rest/pallas_call | solution.py:152
  106.5 0.6 collective-permute-start.24
  107.0 0.5 collective-permute-start.25
  107.6 2.5 %collective-permute-start.26 = (f32[3,96,384]{2,1,0:T(8,128)}, f32[3,96,384]{2,1,0:T(8,128)S(1)}, u32[]{:S(2)}, u32[]{:S(2)}) collective-permute-start(f32[3,96,384]{2,1,0:T(8,128)} %get-tuple-element.101), channel_id=1, source_target_pairs={{0,5},{1,4},{2,7},{3,6},{4,1},{5,0},{6,3},{7,2},{8,13},{9,12},{10,... | collective-permute-start | bytes 1327112 | tf_op jit(solution)/shard_map/ppermute | solution.py:292
  110.0 0.5 collective-permute-start.29
  110.5 8.4 %collective-permute-done.24.refs_5_ = f32[3,96,384]{2,1,0:T(8,128)S(1)} collective-permute-done((f32[3,96,384]{2,1,0:T(8,128)}, f32[3,96,384]{2,1,0:T(8,128)S(1)}, u32[]{:S(2)}, u32[]{:S(2)}) %collective-permute-start.24) | collective-permute-done | bytes 442400 | tf_op jit(solution)/shard_map/ppermute | solution.py:292
  119.0 1.2 fusion.2.refs_1_
  120.2 0.7 fusion
  120.9 8.1 %collective-permute-done.26.refs_9_ = f32[3,96,384]{2,1,0:T(8,128)S(1)} collective-permute-done((f32[3,96,384]{2,1,0:T(8,128)}, f32[3,96,384]{2,1,0:T(8,128)S(1)}, u32[]{:S(2)}, u32[]{:S(2)}) %collective-permute-start.26) | collective-permute-done | bytes 442400 | tf_op jit(solution)/shard_map/ppermute | solution.py:292
  129.0 0.5 collective-permute-start.30
  129.5 0.5 collective-permute-start.34
  130.1 0.6 slice_bitcast_fusion
  130.7 1.7 collective-permute-done.33.refs_16_
  132.5 0.6 collective-permute-done.34.refs_17_
  133.9 32.0 %chain.2 = (f32[384,768]{1,0:T(8,128)}, f32[384,768]{1,0:T(8,128)}) custom-call(s32[2]{0:T(128)} %get-tuple-element.126.refs_0_, s32[64]{0:T(128)} %fusion.2.refs_1_, f32[1,192,384]{2,1,0:T(8,128)} %bitcast.26, f32[3,96,384]{2,1,0:T(8,128)} %get-tuple-element.106.refs_3_, f32[1,192,384]{2,1,0:T(8,128)} %bitcast.30, f32[3,96,384]{2,1,0:T(8,128)} %copy-done.12, ...), custom_call_target="tpu_custom_call" | custom-call | flops 21743271936 | bytes 20971520 | tf_op jit(solution)/shard_map/chain/pallas_call | solution.py:273
  165.9 0.6 collective-permute-start.35
  166.5 1.9 collective-permute-start.36
  168.5 32.0 %chain.3 = (f32[384,768]{1,0:T(8,128)}, f32[384,768]{1,0:T(8,128)}) custom-call(s32[2]{0:T(128)} %get-tuple-element.125.refs_0_, s32[64]{0:T(128)} %fusion.2.refs_1_, f32[1,192,384]{2,1,0:T(8,128)} %bitcast.27, f32[3,96,384]{2,1,0:T(8,128)} %get-tuple-element.106.refs_3_, f32[1,192,384]{2,1,0:T(8,128)} %bitcast.31, f32[3,96,384]{2,1,0:T(8,128)} %copy-done.12, ...), custom_call_target="tpu_custom_call" | custom-call | flops 21743271936 | bytes 20971520 | tf_op jit(solution)/shard_map/chain/pallas_call | solution.py:273
  200.5 1.6 collective-permute-start.37
  202.0 1.2 collective-permute-start.38
  203.2 0.4 broadcast_in_dim.10
  203.8 23.4 %collective-permute-done.37 = f32[384,768]{1,0:T(8,128)} collective-permute-done((f32[384,768]{1,0:T(8,128)}, f32[384,768]{1,0:T(8,128)}, u32[]{:S(2)}, u32[]{:S(2)}) %collective-permute-start.37) | collective-permute-done | bytes 1179680 | tf_op jit(solution)/shard_map/ppermute | solution.py:292
  227.1 1.3 bitcast_dynamic-update-slice_fusion.1
  228.5 1.9 collective-permute-done.38
  230.4 0.2 copy-done
  230.7 1.1 bitcast_dynamic-update-slice_fusion
  (98 shorter events, 2.3 us)
Async XLA Ops:
  1.1 19.6 %collective-permute-start = (f32[2,192,384]{2,1,0:T(8,128)S(1)}, f32[2,192,384]{2,1,0:T(8,128)S(1)}, u32[]{:S(2)}, u32[]{:S(2)}) collective-permute-start(f32[2,192,384]{2,1,0:T(8,128)S(1)} %pad_maximum_fusion), channel_id=1, source_target_pairs={{0,8},{8,16},{16,24},{24,0},{1,9},{9,17},{17,25},{25,1},{2,10},{10... | collective-permute-start | bytes 1769480 | tf_op jit(solution)/shard_map/ppermute | solution.py:301
  5.6 15.1 %collective-permute-start.1 = (f32[2,384]{1,0:T(2,128)S(1)}, f32[2,384]{1,0:T(2,128)S(1)}, u32[]{:S(2)}, u32[]{:S(2)}) collective-permute-start(f32[2,384]{1,0:T(2,128)S(1)} %pad_maximum_fusion.4), channel_id=1, source_target_pairs={{0,8},{8,16},{16,24},{24,0},{1,9},{9,17},{17,25},{25,1},{2,10},{10... | collective-permute-start | bytes 9224 | tf_op jit(solution)/shard_map/ppermute | solution.py:301
  7.2 13.5 %collective-permute-start.2 = (f32[2,384]{1,0:T(2,128)S(1)}, f32[2,384]{1,0:T(2,128)S(1)}, u32[]{:S(2)}, u32[]{:S(2)}) collective-permute-start(f32[2,384]{1,0:T(2,128)S(1)} %pad_maximum_fusion.4), channel_id=1, source_target_pairs={{0,16},{8,24},{16,0},{24,8},{1,17},{9,25},{17,1},{25,9},{2,18},{10... | collective-permute-start | bytes 9224 | tf_op jit(solution)/shard_map/ppermute | solution.py:301
  8.3 12.4 %collective-permute-start.3 = (f32[2,384]{1,0:T(2,128)S(1)}, f32[2,384]{1,0:T(2,128)S(1)}, u32[]{:S(2)}, u32[]{:S(2)}) collective-permute-start(f32[2,384]{1,0:T(2,128)S(1)} %pad_maximum_fusion.4), channel_id=1, source_target_pairs={{0,24},{8,0},{16,8},{24,16},{1,25},{9,1},{17,9},{25,17},{2,26},{10... | collective-permute-start | bytes 9224 | tf_op jit(solution)/shard_map/ppermute | solution.py:301
  20.7 19.5 %copy-start.1 = (f32[2,192,384]{2,1,0:T(8,128)}, f32[2,192,384]{2,1,0:T(8,128)S(1)}, u32[]{:S(2)}) copy-start(f32[2,192,384]{2,1,0:T(8,128)S(1)} %collective-permute-done.refs_0_) | copy-start | bytes 1769476
  20.7 17.4 %collective-permute-start.4 = (f32[2,192,384]{2,1,0:T(8,128)S(1)}, f32[2,192,384]{2,1,0:T(8,128)S(1)}, u32[]{:S(2)}, u32[]{:S(2)}) collective-permute-start(f32[2,192,384]{2,1,0:T(8,128)S(1)} %collective-permute-done.refs_0_), channel_id=1, source_target_pairs={{0,1},{1,0},{2,3},{3,2},{4,5},{5,4},{6,7},{7,6},{8,9},{9,8},{10,11... | collective-permute-start | bytes 1769480 | tf_op jit(solution)/shard_map/ppermute | solution.py:292
  22.3 15.9 %collective-permute-start.5 = (f32[2,192,384]{2,1,0:T(8,128)S(1)}, f32[2,192,384]{2,1,0:T(8,128)S(1)}, u32[]{:S(2)}, u32[]{:S(2)}) collective-permute-start(f32[2,192,384]{2,1,0:T(8,128)S(1)} %collective-permute-done.refs_0_), channel_id=1, source_target_pairs={{0,4},{1,5},{2,6},{3,7},{4,0},{5,1},{6,2},{7,3},{8,12},{9,13},{10,... | collective-permute-start | bytes 1769480 | tf_op jit(solution)/shard_map/ppermute | solution.py:292
  23.8 15.3 %collective-permute-start.6 = (f32[2,192,384]{2,1,0:T(8,128)S(1)}, f32[2,192,384]{2,1,0:T(8,128)}, u32[]{:S(2)}, u32[]{:S(2)}) collective-permute-start(f32[2,192,384]{2,1,0:T(8,128)S(1)} %collective-permute-done.refs_0_), channel_id=1, source_target_pairs={{0,8},{8,16},{16,24},{24,0},{1,9},{9,17},{17,25},{25,1},{2,10},{10... | collective-permute-start | bytes 1769480 | tf_op jit(solution)/shard_map/ppermute | solution.py:301
  26.3 31.0 %copy-start.7 = (f32[4]{0:T(128)S(1)}, f32[4]{0:T(128)}, u32[]{:S(2)}) copy-start(f32[4]{0:T(128)} %param.15) | copy-start | bytes 52
  38.1 20.6 %copy-start.2 = (f32[2,192,384]{2,1,0:T(8,128)}, f32[2,192,384]{2,1,0:T(8,128)S(1)}, u32[]{:S(2)}) copy-start(f32[2,192,384]{2,1,0:T(8,128)S(1)} %collective-permute-done.4.refs_1_) | copy-start | bytes 1769476
  38.2 20.6 %copy-start.3 = (f32[2,192,384]{2,1,0:T(8,128)}, f32[2,192,384]{2,1,0:T(8,128)S(1)}, u32[]{:S(2)}) copy-start(f32[2,192,384]{2,1,0:T(8,128)S(1)} %collective-permute-done.5.refs_2_) | copy-start | bytes 1769476
  39.1 12.9 %collective-permute-start.7 = (f32[2,192,384]{2,1,0:T(8,128)}, f32[2,192,384]{2,1,0:T(8,128)}, u32[]{:S(2)}, u32[]{:S(2)}) collective-permute-start(f32[2,192,384]{2,1,0:T(8,128)} %collective-permute-done.6.refs_0_), channel_id=1, source_target_pairs={{0,1},{1,0},{2,3},{3,2},{4,5},{5,4},{6,7},{7,6},{8,9},{9,8},{10,11... | collective-permute-start | bytes 1769480 | tf_op jit(solution)/shard_map/ppermute | solution.py:292
  39.6 12.6 %collective-permute-start.8 = (f32[2,192,384]{2,1,0:T(8,128)}, f32[2,192,384]{2,1,0:T(8,128)}, u32[]{:S(2)}, u32[]{:S(2)}) collective-permute-start(f32[2,192,384]{2,1,0:T(8,128)} %collective-permute-done.6.refs_0_), channel_id=1, source_target_pairs={{0,4},{1,5},{2,6},{3,7},{4,0},{5,1},{6,2},{7,3},{8,12},{9,13},{10,... | collective-permute-start | bytes 1769480 | tf_op jit(solution)/shard_map/ppermute | solution.py:292
  40.1 14.1 %collective-permute-start.9 = (f32[2,192,384]{2,1,0:T(8,128)}, f32[2,192,384]{2,1,0:T(8,128)}, u32[]{:S(2)}, u32[]{:S(2)}) collective-permute-start(f32[2,192,384]{2,1,0:T(8,128)} %collective-permute-done.6.refs_0_), channel_id=1, source_target_pairs={{0,8},{8,16},{16,24},{24,0},{1,9},{9,17},{17,25},{25,1},{2,10},{10... | collective-permute-start | bytes 1769480 | tf_op jit(solution)/shard_map/ppermute | solution.py:301
  40.2 17.1 %collective-permute-start.15 = (f32[2,192,384]{2,1,0:T(8,128)S(1)}, f32[2,192,384]{2,1,0:T(8,128)S(1)}, u32[]{:S(2)}, u32[]{:S(2)}) collective-permute-start(f32[2,192,384]{2,1,0:T(8,128)S(1)} %collective-permute-done.refs_0_), channel_id=1, source_target_pairs={{0,2},{1,3},{2,0},{3,1},{4,6},{5,7},{6,4},{7,5},{8,10},{9,11},{10,... | collective-permute-start | bytes 1769480 | tf_op jit(solution)/shard_map/ppermute | solution.py:292
  40.2 17.9 %collective-permute-start.16 = (f32[2,192,384]{2,1,0:T(8,128)S(1)}, f32[2,192,384]{2,1,0:T(8,128)S(1)}, u32[]{:S(2)}, u32[]{:S(2)}) collective-permute-start(f32[2,192,384]{2,1,0:T(8,128)S(1)} %collective-permute-done.4.refs_1_), channel_id=1, source_target_pairs={{0,2},{1,3},{2,0},{3,1},{4,6},{5,7},{6,4},{7,5},{8,10},{9,11},{10,... | collective-permute-start | bytes 1769480 | tf_op jit(solution)/shard_map/ppermute | solution.py:292
  51.9 6.2 %collective-permute-start.17 = (f32[2,192,384]{2,1,0:T(8,128)S(1)}, f32[2,192,384]{2,1,0:T(8,128)S(1)}, u32[]{:S(2)}, u32[]{:S(2)}) collective-permute-start(f32[2,192,384]{2,1,0:T(8,128)S(1)} %collective-permute-done.5.refs_2_), channel_id=1, source_target_pairs={{0,2},{1,3},{2,0},{3,1},{4,6},{5,7},{6,4},{7,5},{8,10},{9,11},{10,... | collective-permute-start | bytes 1769480 | tf_op jit(solution)/shard_map/ppermute | solution.py:292
  54.3 19.1 %collective-permute-start.13 = (f32[2,192,384]{2,1,0:T(8,128)}, f32[2,192,384]{2,1,0:T(8,128)}, u32[]{:S(2)}, u32[]{:S(2)}) collective-permute-start(f32[2,192,384]{2,1,0:T(8,128)} %collective-permute-done.9.refs_6_), channel_id=1, source_target_pairs={{0,1},{1,0},{2,3},{3,2},{4,5},{5,4},{6,7},{7,6},{8,9},{9,8},{10,11... | collective-permute-start | bytes 1769480 | tf_op jit(solution)/shard_map/ppermute | solution.py:292
  55.7 17.6 %collective-permute-start.14 = (f32[2,192,384]{2,1,0:T(8,128)}, f32[2,192,384]{2,1,0:T(8,128)}, u32[]{:S(2)}, u32[]{:S(2)}) collective-permute-start(f32[2,192,384]{2,1,0:T(8,128)} %collective-permute-done.9.refs_6_), channel_id=1, source_target_pairs={{0,4},{1,5},{2,6},{3,7},{4,0},{5,1},{6,2},{7,3},{8,12},{9,13},{10,... | collective-permute-start | bytes 1769480 | tf_op jit(solution)/shard_map/ppermute | solution.py:292
  57.3 1.4 copy-start.4
  57.3 16.7 %collective-permute-start.10 = (f32[2,192,384]{2,1,0:T(8,128)}, f32[2,192,384]{2,1,0:T(8,128)S(1)}, u32[]{:S(2)}, u32[]{:S(2)}) collective-permute-start(f32[2,192,384]{2,1,0:T(8,128)} %collective-permute-done.6.refs_0_), channel_id=1, source_target_pairs={{0,2},{1,3},{2,0},{3,1},{4,6},{5,7},{6,4},{7,5},{8,10},{9,11},{10,... | collective-permute-start | bytes 1769480 | tf_op jit(solution)/shard_map/ppermute | solution.py:292
  58.1 0.8 copy-start.5
  58.1 1.0 copy-start.6
  58.1 16.8 %collective-permute-start.11 = (f32[2,192,384]{2,1,0:T(8,128)}, f32[2,192,384]{2,1,0:T(8,128)}, u32[]{:S(2)}, u32[]{:S(2)}) collective-permute-start(f32[2,192,384]{2,1,0:T(8,128)} %collective-permute-done.7.refs_1_), channel_id=1, source_target_pairs={{0,2},{1,3},{2,0},{3,1},{4,6},{5,7},{6,4},{7,5},{8,10},{9,11},{10,... | collective-permute-start | bytes 1769480 | tf_op jit(solution)/shard_map/ppermute | solution.py:292
  58.6 16.4 %collective-permute-start.12 = (f32[2,192,384]{2,1,0:T(8,128)}, f32[2,192,384]{2,1,0:T(8,128)}, u32[]{:S(2)}, u32[]{:S(2)}) collective-permute-start(f32[2,192,384]{2,1,0:T(8,128)} %collective-permute-done.8.refs_2_), channel_id=1, source_target_pairs={{0,2},{1,3},{2,0},{3,1},{4,6},{5,7},{6,4},{7,5},{8,10},{9,11},{10,... | collective-permute-start | bytes 1769480 | tf_op jit(solution)/shard_map/ppermute | solution.py:292
  73.4 2.3 collective-permute-start.18
  73.8 2.7 %collective-permute-start.19 = (f32[2,192,384]{2,1,0:T(8,128)}, f32[2,192,384]{2,1,0:T(8,128)S(1)}, u32[]{:S(2)}, u32[]{:S(2)}) collective-permute-start(f32[2,192,384]{2,1,0:T(8,128)} %collective-permute-done.13.refs_7_), channel_id=1, source_target_pairs={{0,2},{1,3},{2,0},{3,1},{4,6},{5,7},{6,4},{7,5},{8,10},{9,11},{10,... | collective-permute-start | bytes 1769480 | tf_op jit(solution)/shard_map/ppermute | solution.py:292
  73.9 3.4 %copy-start.8 = (f32[2,192,384]{2,1,0:T(8,128)}, f32[2,192,384]{2,1,0:T(8,128)S(1)}, u32[]{:S(2)}) copy-start(f32[2,192,384]{2,1,0:T(8,128)S(1)} %collective-permute-done.10.refs_3_) | copy-start | bytes 1769476
  73.9 3.4 %collective-permute-start.20 = (f32[2,192,384]{2,1,0:T(8,128)}, f32[2,192,384]{2,1,0:T(8,128)S(1)}, u32[]{:S(2)}, u32[]{:S(2)}) collective-permute-start(f32[2,192,384]{2,1,0:T(8,128)} %collective-permute-done.14.refs_8_), channel_id=1, source_target_pairs={{0,2},{1,3},{2,0},{3,1},{4,6},{5,7},{6,4},{7,5},{8,10},{9,11},{10,... | collective-permute-start | bytes 1769480 | tf_op jit(solution)/shard_map/ppermute | solution.py:292
  75.6 1.7 copy-start.9
  76.5 0.9 copy-start.10
  77.3 0.8 copy-start.11
  89.1 17.3 %collective-permute-start.21 = (f32[2,96,384]{2,1,0:T(8,128)}, f32[2,96,384]{2,1,0:T(8,128)S(1)}, u32[]{:S(2)}, u32[]{:S(2)}) collective-permute-start(f32[2,96,384]{2,1,0:T(8,128)} %get-tuple-element.90), channel_id=1, source_target_pairs={{0,4},{1,5},{2,6},{3,7},{4,0},{5,1},{6,2},{7,3},{8,12},{9,13},{10,... | collective-permute-start | bytes 884744 | tf_op jit(solution)/shard_map/ppermute | solution.py:292
  89.7 16.7 %collective-permute-start.22 = (f32[2,96,384]{2,1,0:T(8,128)}, f32[2,96,384]{2,1,0:T(8,128)S(1)}, u32[]{:S(2)}, u32[]{:S(2)}) collective-permute-start(f32[2,96,384]{2,1,0:T(8,128)} %get-tuple-element.91), channel_id=1, source_target_pairs={{0,1},{1,0},{2,3},{3,2},{4,5},{5,4},{6,7},{7,6},{8,9},{9,8},{10,11... | collective-permute-start | bytes 884744 | tf_op jit(solution)/shard_map/ppermute | solution.py:292
  90.3 16.2 %collective-permute-start.23 = (f32[2,96,384]{2,1,0:T(8,128)}, f32[2,96,384]{2,1,0:T(8,128)S(1)}, u32[]{:S(2)}, u32[]{:S(2)}) collective-permute-start(f32[2,96,384]{2,1,0:T(8,128)} %get-tuple-element.92), channel_id=1, source_target_pairs={{0,5},{1,4},{2,7},{3,6},{4,1},{5,0},{6,3},{7,2},{8,13},{9,12},{10,... | collective-permute-start | bytes 884744 | tf_op jit(solution)/shard_map/ppermute | solution.py:292
  92.7 17.3 %copy-start.19 = (f32[2,96,384]{2,1,0:T(8,128)S(1)}, f32[2,96,384]{2,1,0:T(8,128)}, u32[]{:S(2)}) copy-start(f32[2,96,384]{2,1,0:T(8,128)} %get-tuple-element.105) | copy-start | bytes 884740
  106.4 26.7 %copy-start.20 = (f32[2,96,384]{2,1,0:T(8,128)}, f32[2,96,384]{2,1,0:T(8,128)S(1)}, u32[]{:S(2)}) copy-start(f32[2,96,384]{2,1,0:T(8,128)S(1)} %collective-permute-done.21) | copy-start | bytes 884740
  106.4 26.7 %copy-start.21 = (f32[2,96,384]{2,1,0:T(8,128)}, f32[2,96,384]{2,1,0:T(8,128)S(1)}, u32[]{:S(2)}) copy-start(f32[2,96,384]{2,1,0:T(8,128)S(1)} %collective-permute-done.22) | copy-start | bytes 884740
  106.5 3.6 %copy-start.22 = (f32[2,96,384]{2,1,0:T(8,128)}, f32[2,96,384]{2,1,0:T(8,128)S(1)}, u32[]{:S(2)}) copy-start(f32[2,96,384]{2,1,0:T(8,128)S(1)} %collective-permute-done.23) | copy-start | bytes 884740
  106.5 12.5 %collective-permute-start.24 = (f32[3,96,384]{2,1,0:T(8,128)}, f32[3,96,384]{2,1,0:T(8,128)S(1)}, u32[]{:S(2)}, u32[]{:S(2)}) collective-permute-start(f32[3,96,384]{2,1,0:T(8,128)} %get-tuple-element.99), channel_id=1, source_target_pairs={{0,4},{1,5},{2,6},{3,7},{4,0},{5,1},{6,2},{7,3},{8,12},{9,13},{10,... | collective-permute-start | bytes 1327112 | tf_op jit(solution)/shard_map/ppermute | solution.py:292
  107.0 13.8 %collective-permute-start.25 = (f32[3,96,384]{2,1,0:T(8,128)}, f32[3,96,384]{2,1,0:T(8,128)S(1)}, u32[]{:S(2)}, u32[]{:S(2)}) collective-permute-start(f32[3,96,384]{2,1,0:T(8,128)} %get-tuple-element.100), channel_id=1, source_target_pairs={{0,1},{1,0},{2,3},{3,2},{4,5},{5,4},{6,7},{7,6},{8,9},{9,8},{10,11... | collective-permute-start | bytes 1327112 | tf_op jit(solution)/shard_map/ppermute | solution.py:292
  107.6 21.4 %collective-permute-start.26 = (f32[3,96,384]{2,1,0:T(8,128)}, f32[3,96,384]{2,1,0:T(8,128)S(1)}, u32[]{:S(2)}, u32[]{:S(2)}) collective-permute-start(f32[3,96,384]{2,1,0:T(8,128)} %get-tuple-element.101), channel_id=1, source_target_pairs={{0,5},{1,4},{2,7},{3,6},{4,1},{5,0},{6,3},{7,2},{8,13},{9,12},{10,... | collective-permute-start | bytes 1327112 | tf_op jit(solution)/shard_map/ppermute | solution.py:292
  110.0 19.5 %collective-permute-start.27 = (f32[1,192,384]{2,1,0:T(8,128)S(1)}, f32[1,192,384]{2,1,0:T(8,128)}, u32[]{:S(2)}, u32[]{:S(2)}) collective-permute-start(f32[1,192,384]{2,1,0:T(8,128)S(1)} %bitcast.28), channel_id=1, source_target_pairs={{0,2},{1,3},{2,0},{3,1},{4,6},{5,7},{6,4},{7,5},{8,10},{9,11},{10,... | collective-permute-start | bytes 884744 | tf_op jit(solution)/shard_map/ppermute | solution.py:292
  110.0 19.5 %collective-permute-start.29 = (f32[1,192,384]{2,1,0:T(8,128)S(1)}, f32[1,192,384]{2,1,0:T(8,128)}, u32[]{:S(2)}, u32[]{:S(2)}) collective-permute-start(f32[1,192,384]{2,1,0:T(8,128)S(1)} %bitcast.29), channel_id=1, source_target_pairs={{0,2},{1,3},{2,0},{3,1},{4,6},{5,7},{6,4},{7,5},{8,10},{9,11},{10,... | collective-permute-start | bytes 884744 | tf_op jit(solution)/shard_map/ppermute | solution.py:292
  118.9 14.2 %copy-start.12 = (f32[3,96,384]{2,1,0:T(8,128)}, f32[3,96,384]{2,1,0:T(8,128)S(1)}, u32[]{:S(2)}) copy-start(f32[3,96,384]{2,1,0:T(8,128)S(1)} %collective-permute-done.24.refs_5_) | copy-start | bytes 1327108
  119.0 11.1 %collective-permute-start.31 = (f32[1,192,384]{2,1,0:T(8,128)S(1)}, f32[1,192,384]{2,1,0:T(8,128)S(1)}, u32[]{:S(2)}, u32[]{:S(2)}) collective-permute-start(f32[1,192,384]{2,1,0:T(8,128)S(1)} %bitcast.32), channel_id=1, source_target_pairs={{0,2},{1,3},{2,0},{3,1},{4,6},{5,7},{6,4},{7,5},{8,10},{9,11},{10,... | collective-permute-start | bytes 884744 | tf_op jit(solution)/shard_map/ppermute | solution.py:292
  120.9 12.3 %copy-start.13 = (f32[3,96,384]{2,1,0:T(8,128)}, f32[3,96,384]{2,1,0:T(8,128)S(1)}, u32[]{:S(2)}) copy-start(f32[3,96,384]{2,1,0:T(8,128)S(1)} %collective-permute-done.25.refs_7_) | copy-start | bytes 1327108
  129.0 4.2 %copy-start.14 = (f32[3,96,384]{2,1,0:T(8,128)}, f32[3,96,384]{2,1,0:T(8,128)S(1)}, u32[]{:S(2)}) copy-start(f32[3,96,384]{2,1,0:T(8,128)S(1)} %collective-permute-done.26.refs_9_) | copy-start | bytes 1327108
  129.0 3.4 %collective-permute-start.28 = (f32[3,96,384]{2,1,0:T(8,128)}, f32[3,96,384]{2,1,0:T(8,128)S(1)}, u32[]{:S(2)}, u32[]{:S(2)}) collective-permute-start(f32[3,96,384]{2,1,0:T(8,128)} %get-tuple-element.106.refs_3_), channel_id=1, source_target_pairs={{0,2},{1,3},{2,0},{3,1},{4,6},{5,7},{6,4},{7,5},{8,10},{9,11},{10,... | collective-permute-start | bytes 1327112 | tf_op jit(solution)/shard_map/ppermute | solution.py:292
  129.0 3.4 %collective-permute-start.30 = (f32[3,96,384]{2,1,0:T(8,128)S(1)}, f32[3,96,384]{2,1,0:T(8,128)S(1)}, u32[]{:S(2)}, u32[]{:S(2)}) collective-permute-start(f32[3,96,384]{2,1,0:T(8,128)S(1)} %collective-permute-done.24.refs_5_), channel_id=1, source_target_pairs={{0,2},{1,3},{2,0},{3,1},{4,6},{5,7},{6,4},{7,5},{8,10},{9,11},{10,... | collective-permute-start | bytes 1327112 | tf_op jit(solution)/shard_map/ppermute | solution.py:292
  129.5 3.0 %collective-permute-start.32 = (f32[3,96,384]{2,1,0:T(8,128)S(1)}, f32[3,96,384]{2,1,0:T(8,128)S(1)}, u32[]{:S(2)}, u32[]{:S(2)}) collective-permute-start(f32[3,96,384]{2,1,0:T(8,128)S(1)} %collective-permute-done.25.refs_7_), channel_id=1, source_target_pairs={{0,2},{1,3},{2,0},{3,1},{4,6},{5,7},{6,4},{7,5},{8,10},{9,11},{10,... | collective-permute-start | bytes 1327112 | tf_op jit(solution)/shard_map/ppermute | solution.py:292
  129.5 3.6 %collective-permute-start.34 = (f32[3,96,384]{2,1,0:T(8,128)S(1)}, f32[3,96,384]{2,1,0:T(8,128)S(1)}, u32[]{:S(2)}, u32[]{:S(2)}) collective-permute-start(f32[3,96,384]{2,1,0:T(8,128)S(1)} %collective-permute-done.26.refs_9_), channel_id=1, source_target_pairs={{0,2},{1,3},{2,0},{3,1},{4,6},{5,7},{6,4},{7,5},{8,10},{9,11},{10,... | collective-permute-start | bytes 1327112 | tf_op jit(solution)/shard_map/ppermute | solution.py:292
  130.0 3.1 %copy-start.23 = (f32[1,192,384]{2,1,0:T(8,128)}, f32[1,192,384]{2,1,0:T(8,128)S(1)}, u32[]{:S(2)}) copy-start(f32[1,192,384]{2,1,0:T(8,128)S(1)} %collective-permute-done.31.refs_14_) | copy-start | bytes 884740
  130.0 2.4 %collective-permute-start.33 = (f32[1,192,384]{2,1,0:T(8,128)}, f32[1,192,384]{2,1,0:T(8,128)S(1)}, u32[]{:S(2)}, u32[]{:S(2)}) collective-permute-start(f32[1,192,384]{2,1,0:T(8,128)} %bitcast.35), channel_id=1, source_target_pairs={{0,2},{1,3},{2,0},{3,1},{4,6},{5,7},{6,4},{7,5},{8,10},{9,11},{10,... | collective-permute-start | bytes 884744 | tf_op jit(solution)/shard_map/ppermute | solution.py:292
  132.5 0.7 copy-start.24
  132.5 0.9 copy-start.15
  132.5 1.0 copy-start.16
  132.5 1.2 copy-start.17
  133.1 0.8 copy-start.18
  165.9 37.3 %collective-permute-start.35 = (f32[384,768]{1,0:T(8,128)}, f32[384,768]{1,0:T(8,128)S(1)}, u32[]{:S(2)}, u32[]{:S(2)}) collective-permute-start(f32[384,768]{1,0:T(8,128)} %get-tuple-element.115), channel_id=1, source_target_pairs={{0,1},{1,0},{2,5},{3,4},{4,3},{5,2},{6,7},{7,6},{8,9},{9,8},{10,13... | collective-permute-start | bytes 3538952 | tf_op jit(solution)/shard_map/ppermute | solution.py:292
  166.5 37.1 %collective-permute-start.36 = (f32[384,768]{1,0:T(8,128)}, f32[384,768]{1,0:T(8,128)S(1)}, u32[]{:S(2)}, u32[]{:S(2)}) collective-permute-start(f32[384,768]{1,0:T(8,128)} %get-tuple-element.116), channel_id=1, source_target_pairs={{0,0},{1,1},{2,4},{3,5},{4,2},{5,3},{6,6},{7,7},{8,8},{9,9},{10,12... | collective-permute-start | bytes 3538952 | tf_op jit(solution)/shard_map/ppermute | solution.py:292
  200.5 26.7 %collective-permute-start.37 = (f32[384,768]{1,0:T(8,128)}, f32[384,768]{1,0:T(8,128)}, u32[]{:S(2)}, u32[]{:S(2)}) collective-permute-start(f32[384,768]{1,0:T(8,128)} %get-tuple-element.117), channel_id=1, source_target_pairs={{0,2},{1,3},{2,6},{3,7},{4,0},{5,1},{6,4},{7,5},{8,10},{9,11},{10,... | collective-permute-start | bytes 3538952 | tf_op jit(solution)/shard_map/ppermute | solution.py:292
  202.0 28.4 %collective-permute-start.38 = (f32[384,768]{1,0:T(8,128)}, f32[384,768]{1,0:T(8,128)S(1)}, u32[]{:S(2)}, u32[]{:S(2)}) collective-permute-start(f32[384,768]{1,0:T(8,128)} %get-tuple-element.118), channel_id=1, source_target_pairs={{0,3},{1,2},{2,7},{3,6},{4,1},{5,0},{6,5},{7,4},{8,11},{9,10},{10,... | collective-permute-start | bytes 3538952 | tf_op jit(solution)/shard_map/ppermute | solution.py:292
  228.5 2.2 copy-start
